TPU v7x, 32 devices: a whole 2x2x4 slice. The times are simulated.
32 devices in a mesh: gx: 2 (over x), az: 4 (over y, core), ta: 4 (over z).
Axes of the slice: x: 2, y: 2, z: 4, core: 2. Of those that a mesh axis runs over, the one named last changes fastest.
Arguments:
- velocity: float32 [32, 32, 1024], P('gx', 'az', 'ta'), may hold values from -6 to 6
- pressure: float32 [32, 32, 1024], P('gx', 'az', 'ta'), may hold values from -6 to 6
- offsets: int32 [8], replicated, may hold values from 1 to 16, as said below
Outputs:
- correlation: float32 [32, 8, 1056], P(('gx', 'az', 'ta'))
Inputs may be any that keep to these rules, and one draw needn't show every extreme that they name: `offsets`: the 8 separations are distinct and the largest equals 16.
All inputs are finite; a program needn't handle non-finite values.
Results may differ from a plain program's by a relative error of at most 0.00007.
Values sent between devices are 32-bit elements; how exact they have to be, the bound alone decides.
No kernel may reach another device: no remote copies, remote signals or barrier semaphores. Data moves between devices by JAX's collectives and lax.ppermute only.
A program may use at most 64 MiB of HBM per device.

v0:
```python
import math

import jax
import jax.numpy as jnp
from jax import lax
from jax.sharding import PartitionSpec as P

AZIM = 32
NBR = 8
MAXLAG = 16
LAGS = 33


def from_behind(value, axis, steps):
    count = lax.axis_size(axis)
    leading, last = (max(0, -steps), min(count, count - steps))
    return lax.ppermute(value, axis, [(source, source + steps) for source in range(leading, last)])


def padded_2(block, sides, width):
    for axis, dim in sides:
        count = lax.axis_size(axis)
        forward = [(i, i + 1) for i in range(count - 1)]
        backward = [(target, source) for source, target in forward]
        low = lax.ppermute(
            lax.slice_in_dim(block, block.shape[dim] - width, None, axis=dim), axis, forward
        )
        high = lax.ppermute(lax.slice_in_dim(block, 0, width, axis=dim), axis, backward)
        block = jnp.concatenate([low, block, high], axis=dim)
    return block


def correlate(vel_block, vel_first, pres_block, offsets):
    sta_dev = vel_block.shape[0]
    vel_count = vel_block.shape[1]
    pres_count = pres_block.shape[1]
    window = pres_block.shape[2]
    lags_total = 2 * MAXLAG + 1
    group = 8
    blocks = sta_dev // group
    vel_rows = jnp.arange(vel_count, dtype=jnp.int32) + vel_first
    pres_rows = jnp.arange(pres_count, dtype=jnp.int32)
    spread = (pres_rows[None, :] - vel_rows[:, None]) % AZIM
    pairing = (spread[:, :, None] == jnp.arange(AZIM, dtype=jnp.int32)[None, None, :]).astype(
        jnp.float32
    )
    padded_vel = jnp.pad(vel_block, ((0, 0), (0, 0), (2 * MAXLAG, 2 * MAXLAG)))

    def one_block(block_id):
        first = block_id * group
        series = lax.dynamic_slice_in_dim(padded_vel, first, group, 0)
        stacked = jnp.stack(
            [
                series[:, :, 2 * MAXLAG - shift_lag : 2 * MAXLAG - shift_lag + window]
                for shift_lag in range(lags_total)
            ],
            axis=2,
        )
        stations = first + jnp.arange(group, dtype=jnp.int32)
        indices = (stations[:, None] + offsets[None, :]).reshape(-1)
        partners = jnp.take(pres_block, indices, axis=0).reshape(
            group, offsets.shape[0], pres_count, window
        )
        product = jnp.einsum("spjt,skqt->spjkq", stacked, partners, precision=lax.Precision.HIGHEST)
        return jnp.einsum("spjkq,pqd->skjd", product, pairing, precision=lax.Precision.HIGHEST)

    results = lax.map(one_block, jnp.arange(blocks, dtype=jnp.int32))
    return results.reshape(sta_dev, offsets.shape[0], lags_total, AZIM)


def shards(velocity, pressure, offsets):
    sta_dev, az_dev, time_dev = velocity.shape
    factor = 1.0 / math.sqrt(time_dev * lax.axis_size("ta") * AZIM)
    own_first = lax.axis_index("az") * az_dev
    ahead_rows = from_behind(pressure, "gx", -1)
    extended = jnp.concatenate([pressure, ahead_rows], axis=0)
    padded = padded_2(extended, (("ta", 2),), MAXLAG)
    totals = correlate(
        velocity, own_first, lax.all_gather(padded, "az", axis=1, tiled=True), offsets
    )
    partial_value = (totals * factor).reshape(sta_dev, NBR, LAGS * AZIM)
    result = lax.psum_scatter(partial_value, ("az", "ta"), scatter_dimension=0, tiled=True)
    return result


def solution(mesh):
    return jax.shard_map(
        shards,
        mesh=mesh,
        in_specs=(P("gx", "az", "ta"), P("gx", "az", "ta"), P()),
        out_specs=P(("gx", "az", "ta"), None, None),
        check_vma=False,
    )
```

profile of v0, /device:TPU:0, one launch (start us, length us, event | category | flops | bytes accessed | tf_op | source)
XLA Modules:
  0.0 200.5 jit_solution(12163193746003348553)
XLA Ops:
  6.5 1.3 collective-permute-start
  7.8 0.9 constant_dynamic-update-slice_fusion.1
  8.7 5.7 %collective-permute-done = f32[16,8,256]{2,1,0:T(8,128)S(1)} collective-permute-done((f32[16,8,256]{2,1,0:T(8,128)}, f32[16,8,256]{2,1,0:T(8,128)S(1)}, u32[]{:S(2)}, u32[]{:S(2)}) %collective-permute-start) | collective-permute-done | bytes 131104 | tf_op jit(solution)/shard_map/ppermute | solution.py:17
  14.6 4.3 %collective-permute-start.1 = (f32[32,8,16]{2,1,0:T(8,128)S(1)}, f32[32,8,16]{2,1,0:T(8,128)S(1)}, u32[]{:S(2)}, u32[]{:S(2)}) collective-permute-start(f32[32,8,16]{2,1,0:T(8,128)S(1)} %get-tuple-element.107), channel_id=1, source_target_pairs={{0,1},{1,2},{2,3},{4,5},{5,6},{6,7},{8,9},{9,10},{10,11},{12,13},{... | collective-permute-start | bytes 49160 | tf_op jit(solution)/shard_map/ppermute | solution.py:25
  18.9 1.3 collective-permute-start.2
  20.2 1.2 collective-permute-done.1
  21.4 4.4 %collective-permute-done.2 = f32[32,8,16]{2,1,0:T(8,128)S(1)} collective-permute-done((f32[32,8,16]{2,1,0:T(8,128)S(1)}, f32[32,8,16]{2,1,0:T(8,128)S(1)}, u32[]{:S(2)}, u32[]{:S(2)}) %collective-permute-start.2) | collective-permute-done | bytes 16416 | tf_op jit(solution)/shard_map/ppermute | solution.py:28
  25.8 0.9 pad_maximum_fusion
  26.8 1.0 pad.4
  27.9 17.9 %all-gather.2.cloned.1.call-done = f32[32,32,288]{2,1,0:T(8,128)} async-done(((f32[32,8,288]{2,1,0:T(8,128)}), f32[32,32,288]{2,1,0:T(8,128)}) %all-gather.2.cloned.1.call-update) | async-done | bytes 1179664 | tf_op jit(solution)/shard_map/all_gather | solution.py:79
  45.9 85.9 %while.11 = (s32[]{:T(128)}, f32[2,8,8,33,32]{3,4,2,1,0:T(8,128)}, s32[2]{0:T(128)S(1)}, f32[16,8,320]{2,1,0:T(8,128)S(1)}, s32[8]{0:T(128)}, /*index=5*/f32[32,...) while((s32[]{:T(128)}, f32[2,8,8,33,32]{3,4,2,1,0:T(8,128)}, ...), condition=%wide.region_1.2_spmd.clone, body=%wide.region_0.1_spmd.clone.sunk | while | flops 2076788480 | bytes 29491824 | solution.py:67
  45.9 0.7 dynamic_slice.10
  47.2 0.6 constant_dynamic-slice_fusion.2
  47.8 0.1 copy.100
  47.9 0.1 copy.101
  48.1 0.1 copy.103
  48.3 0.1 copy.104
  48.6 0.1 copy.90
  48.9 0.1 copy.93
  49.0 0.1 copy.94
  49.2 0.1 copy.96
  49.4 0.1 copy.97
  49.6 0.1 copy.99
  49.8 0.5 dynamic-slice_bitcast_fusion.33
  50.4 0.1 copy.76
  50.5 0.1 copy.77
  50.7 0.1 copy.79
  50.8 0.1 copy.80
  51.1 0.1 copy.82
  51.2 0.1 copy.83
  51.4 0.1 copy.85
  51.5 0.1 copy.86
  51.8 0.1 copy.89
  52.0 12.0 %stack.139 = f32[8,8,33,288]{3,2,1,0:T(8,128)} concatenate(f32[8,8,1,288]{3,2,1,0:T(1,128)S(1)} %copy.75, f32[8,8,1,288]{3,2,1,0:T(1,128)S(1)} %copy.76, f32[8,8,1,288]{3,2,1,0:T(1,128)S(1)} %copy.77, f32[8,8,1,288]{3,2,1,0:T(1,128)S(1)} %copy.78, f32[8,8,1,288]{3,2,1,0:T(1,128)S(1)} %copy.79, f32[8,8,1,288]{3,2,1,0:T(1,128)S(1)} %copy.80, f32[8,8,1,288]{3,2,1,0:T(1,128)S(1)} %copy.81, ...), dimensions={2} | concatenate | bytes 4866048 | tf_op jit(solution)/shard_map/while/body/eval_jaxpr/stack | solution.py:52
  64.1 2.2 %gather_fusion = f32[64,32,288]{2,1,0:T(8,128)S(1)} fusion(f32[32,32,288]{2,1,0:T(8,128)} %get-tuple-element.309, s32[1024]{0:T(1024)S(1)} %pad_clamp_fusion.2), kind=kCustom, calls=%fused_computation.clone.clone.1 | custom fusion | bytes 4718848 | tf_op jit(solution)/shard_map/while/body/eval_jaxpr/jit(_take)/gather | solution.py:61
  66.3 16.2 %fusion.32 = f32[8,8,33,8,32]{2,4,1,3,0:T(8,128)S(1)} fusion(f32[8,8,33,288]{3,2,1,0:T(8,128)} %stack.139, f32[8,8,32,288]{3,2,1,0:T(8,128)S(1)} %bitcast.112, pred[8,8]{1,0:T(8,128)(4,1)S(1)} %compare_and_fusion.2), kind=kOutput, calls=%fused_computation.2.clone.1 | convolution fusion | flops 1869152256 | bytes 6955072 | tf_op jit(solution)/shard_map/while/body/eval_jaxpr/spjt,skqt->spjkq/dot_general | solution.py:64
  82.6 6.2 %fusion.33 = f32[2,8,8,33,32]{3,4,2,1,0:T(8,128)} fusion(f32[2,8,8,33,32]{3,4,2,1,0:T(8,128)} %get-tuple-element.262, s32[]{:T(128)} %get-tuple-element.261, f32[8,8,33,8,32]{2,4,1,3,0:T(8,128)S(1)} %fusion.32, s32[8,32]{1,0:T(8,128)S(1)} %get-tuple-element.310), kind=kOutput, calls=%fused_computation.9.clone.1 | convolution fusion | flops 207634432 | bytes 3212800 | tf_op jit(solution)/shard_map/while/body/eval_jaxpr/spjkq,pqd->skjd/dot_general | solution.py:65
  88.8 0.7 dynamic_slice.10
  90.2 0.6 constant_dynamic-slice_fusion.2
  92.7 0.5 dynamic-slice_bitcast_fusion.33
  94.9 12.0 %stack.139 = f32[8,8,33,288]{3,2,1,0:T(8,128)} concatenate(f32[8,8,1,288]{3,2,1,0:T(1,128)S(1)} %copy.75, f32[8,8,1,288]{3,2,1,0:T(1,128)S(1)} %copy.76, f32[8,8,1,288]{3,2,1,0:T(1,128)S(1)} %copy.77, f32[8,8,1,288]{3,2,1,0:T(1,128)S(1)} %copy.78, f32[8,8,1,288]{3,2,1,0:T(1,128)S(1)} %copy.79, f32[8,8,1,288]{3,2,1,0:T(1,128)S(1)} %copy.80, f32[8,8,1,288]{3,2,1,0:T(1,128)S(1)} %copy.81, ...), dimensions={2} | concatenate | bytes 4866048 | tf_op jit(solution)/shard_map/while/body/eval_jaxpr/stack | solution.py:52
  107.0 2.2 %gather_fusion = f32[64,32,288]{2,1,0:T(8,128)S(1)} fusion(f32[32,32,288]{2,1,0:T(8,128)} %get-tuple-element.309, s32[1024]{0:T(1024)S(1)} %pad_clamp_fusion.2), kind=kCustom, calls=%fused_computation.clone.clone.1 | custom fusion | bytes 4718848 | tf_op jit(solution)/shard_map/while/body/eval_jaxpr/jit(_take)/gather | solution.py:61
  109.3 16.2 %fusion.32 = f32[8,8,33,8,32]{2,4,1,3,0:T(8,128)S(1)} fusion(f32[8,8,33,288]{3,2,1,0:T(8,128)} %stack.139, f32[8,8,32,288]{3,2,1,0:T(8,128)S(1)} %bitcast.112, pred[8,8]{1,0:T(8,128)(4,1)S(1)} %compare_and_fusion.2), kind=kOutput, calls=%fused_computation.2.clone.1 | convolution fusion | flops 1869152256 | bytes 6955072 | tf_op jit(solution)/shard_map/while/body/eval_jaxpr/spjt,skqt->spjkq/dot_general | solution.py:64
  125.5 6.3 %fusion.33 = f32[2,8,8,33,32]{3,4,2,1,0:T(8,128)} fusion(f32[2,8,8,33,32]{3,4,2,1,0:T(8,128)} %get-tuple-element.262, s32[]{:T(128)} %get-tuple-element.261, f32[8,8,33,8,32]{2,4,1,3,0:T(8,128)S(1)} %fusion.32, s32[8,32]{1,0:T(8,128)S(1)} %get-tuple-element.310), kind=kOutput, calls=%fused_computation.9.clone.1 | convolution fusion | flops 207634432 | bytes 3212800 | tf_op jit(solution)/shard_map/while/body/eval_jaxpr/spjkq,pqd->skjd/dot_general | solution.py:65
  131.8 3.2 %broadcast_multiply_fusion = f32[2,8,8,33,32]{3,4,2,1,0:T(8,128)} fusion(f32[2,8,8,33,32]{3,4,2,1,0:T(8,128)} %get-tuple-element.42), kind=kLoop, calls=%fused_computation.55 | loop fusion | flops 135168 | bytes 1081344 | tf_op jit(solution)/shard_map/mul | solution.py:81
  135.0 2.3 %copy.38 = f32[2,8,8,33,32]{4,3,2,1,0:T(8,128)S(1)} copy(f32[2,8,8,33,32]{3,4,2,1,0:T(8,128)} %broadcast_multiply_fusion) | data formatting | bytes 1081344 | tf_op jit(solution)/shard_map/mul | solution.py:81
  137.3 1.3 mul.22
  138.7 55.0 %reduce-scatter.4.cloned.1.call-done = f32[1,8,1056]{2,1,0:T(8,128)} async-done(((f32[16,8,1056]{2,1,0:T(8,128)}), f32[1,8,1056]{2,1,0:T(8,128)}) %reduce-scatter.4.cloned.1.call-update) | async-done | bytes 33808
  (73 shorter events, 5.5 us)
Async XLA Ops:
  6.5 39.3 %all-gather.2.cloned.1.call-start = ((), (), s32[]{:S(2)}) async-start(), calls=%async_computation.1 | async-start | bytes 1966080 | tf_op jit(solution)/shard_map/all_gather | solution.py:79
  6.5 7.9 %collective-permute-start = (f32[16,8,256]{2,1,0:T(8,128)}, f32[16,8,256]{2,1,0:T(8,128)S(1)}, u32[]{:S(2)}, u32[]{:S(2)}) collective-permute-start(f32[16,8,256]{2,1,0:T(8,128)} %param.6), channel_id=1, source_target_pairs={{16,0},{17,1},{18,2},{19,3},{20,4},{21,5},{22,6},{23,7},{24,8},{25... | collective-permute-start | bytes 393224 | tf_op jit(solution)/shard_map/ppermute | solution.py:17
  14.6 6.8 %collective-permute-start.1 = (f32[32,8,16]{2,1,0:T(8,128)S(1)}, f32[32,8,16]{2,1,0:T(8,128)S(1)}, u32[]{:S(2)}, u32[]{:S(2)}) collective-permute-start(f32[32,8,16]{2,1,0:T(8,128)S(1)} %get-tuple-element.107), channel_id=1, source_target_pairs={{0,1},{1,2},{2,3},{4,5},{5,6},{6,7},{8,9},{9,10},{10,11},{12,13},{... | collective-permute-start | bytes 49160 | tf_op jit(solution)/shard_map/ppermute | solution.py:25
  18.9 6.9 %collective-permute-start.2 = (f32[32,8,16]{2,1,0:T(8,128)S(1)}, f32[32,8,16]{2,1,0:T(8,128)S(1)}, u32[]{:S(2)}, u32[]{:S(2)}) collective-permute-start(f32[32,8,16]{2,1,0:T(8,128)S(1)} %get-tuple-element.108), channel_id=1, source_target_pairs={{1,0},{2,1},{3,2},{5,4},{6,5},{7,6},{9,8},{10,9},{11,10},{13,12},{... | collective-permute-start | bytes 49160 | tf_op jit(solution)/shard_map/ppermute | solution.py:28
  26.8 166.9 %reduce-scatter.4.cloned.1.call-start = ((), (), s32[]{:S(2)}) async-start(), calls=%async_computation.2 | async-start | bytes 626688
  51.9 12.0 %copy-start = (s32[8]{0:T(128)S(1)}, s32[8]{0:T(128)}, u32[]{:S(2)}) copy-start(s32[8]{0:T(128)} %get-tuple-element.308) | copy-start | bytes 100 | tf_op jit(solution)/shard_map/while
  94.9 12.0 %copy-start = (s32[8]{0:T(128)S(1)}, s32[8]{0:T(128)}, u32[]{:S(2)}) copy-start(s32[8]{0:T(128)} %get-tuple-element.308) | copy-start | bytes 100 | tf_op jit(solution)/shard_map/while
Sparse Core Ops, SparseCore 0:
  26.9 18.9 all-gather.1
  138.8 54.7 reduce-scatter.3
where the time goes:
time: 201 us; the launch traced here: 200 us
  waiting for transfers between devices  84.2 us (42%)
  matrix products  45 us (22%)
  local copies, waits for them, and re-layouts  44.3 us (22%)
  between operations  13.5 us (7%)
  starting transfers between devices  6.93 us (3%)
  other arithmetic  4.56 us (2%)
    unnamed x3, waiting for transfers between devices  55 us
    dot_general x2, matrix products, one_block(): jnp.einsum('spjt,skqt->spjkq', stacked, partners, precision=lax.Precision...  32.5 us
    another operation x70, local copies, waits for them, and re-layouts, one_block(): jnp.stack([series[:, :, 2 * MAXLAG - shift_lag:2 * MAXLAG - shift_lag + w...  31.7 us
    all_gather x1, waiting for transfers between devices, shards(): lax.all_gather(padded, 'az', axis=1, tiled=True)  17.9 us
    dot_general x2, matrix products, one_block(): jnp.einsum('spjkq,pqd->skjd', product, pairing, precision=lax.Precision.H...  12.5 us
    ppermute x1, waiting for transfers between devices, from_behind(): lax.ppermute(value, axis, [(source, source + steps) for source in range(l...  5.74 us
    ppermute x1, waiting for transfers between devices, padded_2(): lax.ppermute(lax.slice_in_dim(block, 0, width, axis=dim), axis, backward)  4.36 us
    ppermute x1, starting transfers between devices, padded_2(): lax.ppermute(lax.slice_in_dim(block, block.shape[dim] - width, None, axis...  4.32 us
  transfers between devices with their start and end apart: 5, of which 5 were waited for; matrix products, arithmetic and copies ran while one was open for 1% of the time, Pallas kernels for 0%

commit v1 on v0

v1 whole, which is shorter than its diff:
```python
import functools
import math

import jax
import jax.numpy as jnp
from jax import lax
from jax.experimental import pallas as pl
from jax.experimental.pallas import tpu as pltpu
from jax.sharding import PartitionSpec as P

MAXLAG = 16
LAGS = 2 * MAXLAG + 1
MAIN = 2 * MAXLAG
LANES = 128
BF16 = jnp.bfloat16
F32 = jnp.float32


def split(x):
    high = x.astype(BF16)
    return high, (x - high.astype(F32)).astype(BF16)


def in_core_order(core, mine, other):
    first = jnp.where(core == 0, mine, other)
    second = jnp.where(core == 0, other, mine)
    return jnp.concatenate([first, second], axis=0)


def lag_kernel(info, v_own, v_sib, v_far, v_far_sib, h_own, h_sib, h_far, h_far_sib, out):
    step = pl.program_id(0)
    core, row_y = info[0], info[1]
    own, far = info[3] + step, info[4] + step
    rows, times = v_own.shape[1:]
    width = times + LANES
    far_v = far + v_far.shape[0] - h_far.shape[0]
    near = (v_own, v_sib, h_own, h_sib, own, own, row_y)
    away = (v_far, v_far_sib, h_far, h_far_sib, far_v, far, 1 - row_y)
    for v_a, v_b, h_a, h_b, at_v, at_h, place in (near, away):
        mine = jnp.concatenate([v_a[at_v], h_a[at_h]], axis=1)
        other = jnp.concatenate([v_b[at_v], h_b[at_h]], axis=1)
        series = in_core_order(core, mine, other)
        for b in range(2 * rows):
            line = jnp.broadcast_to(series[b : b + 1, :], (8, width))
            for half in range(MAIN // 16):
                parts = [
                    pltpu.roll(line, (8 * g - MAXLAG) % width, 1, stride=1, stride_axis=0)[:, :times]
                    for g in (2 * half, 2 * half + 1)
                ]
                high, low = split(jnp.concatenate(parts, axis=0))
                at = b * MAIN + 16 * half
                out[0, 0, place, at : at + 16, :] = high
                out[0, 1, place, at : at + 16, :] = low
        last = pltpu.roll(series, MAXLAG, 1)[:, :times]
        high, low = split(last)
        at = 2 * rows * MAIN
        out[0, 0, place, at : at + 2 * rows, :] = high
        out[0, 1, place, at : at + 2 * rows, :] = low


def turn(x, by, azim):
    lane = lax.broadcasted_iota(jnp.int32, x.shape, 1) % azim
    left = pltpu.roll(x, LANES - by, 1)
    right = pltpu.roll(x, azim - by, 1)
    return jnp.where(lane < azim - by, left, right)


def product_kernel(info, offsets, lags, o_own, u_own, near, upper, third,
                   o_sib, u_sib, near_sib, upper_sib, third_sib, *rest):
    outs, (high_p, low_p, prod) = rest[:-3], rest[-3:]
    step = pl.program_id(0)
    core, row_y, place, last_gx = info[0], info[1], info[2], info[5]
    half = third.shape[0]
    rows, times = o_own.shape[1:]
    azim = 4 * rows
    count = offsets.shape[0]

    @pl.when(step == 0)
    def _():
        keep_up = jnp.where(last_gx == 1, 0.0, 1.0).astype(F32)
        keep_mid = jnp.where((last_gx == 1) & (row_y == 1), 0.0, 1.0).astype(F32)

        def one(w, carry):
            def block(mine, other, keep=None):
                x = in_core_order(core, mine, other)
                return x if keep is None else x * keep

            def pick(a, b):
                return jnp.where(row_y == 0, a, b)

            shift = row_y * half
            found = {
                (0, 0): block(o_own[shift + w], o_sib[shift + w]),
                (0, 1): block(pick(o_own[half + w], u_own[w]), pick(o_sib[half + w], u_sib[w]), keep_mid),
                (0, 2): block(u_own[shift + w], u_sib[shift + w], keep_up),
                (1, 0): block(pick(third[w], near[w]), pick(third_sib[w], near_sib[w])),
                (1, 1): block(pick(near[w], upper[w]), pick(near_sib[w], upper_sib[w]), keep_mid),
                (1, 2): block(pick(upper[w], third[w]), pick(upper_sib[w], third_sib[w]), keep_up),
            }
            for (away, slot), x in found.items():
                high, low = split(x)
                at = jnp.where(row_y == away, 0, 1)
                high_p[slot * half + w, at] = high
                low_p[slot * half + w, at] = low
            return carry

        lax.fori_loop(0, half, one, 0)

    station = place ^ step
    first = (half // 2) * core + station
    right = []
    for turned in (0, 1):
        tiles = {0: [], 1: []}
        for k in range(count):
            w = first + offsets[k]
            for which, source in ((0, high_p), (1, low_p)):
                tiles[which] += [source[w, turned], source[w, 1 - turned]]
        high = jnp.concatenate(tiles[0], axis=0)
        low = jnp.concatenate(tiles[1], axis=0)
        right += [high, low, high]
    right = jnp.concatenate(right, axis=1)
    left = []
    for y in (0, 1):
        left += [lags[0, 0, y], lags[0, 0, y], lags[0, 1, y]]
    left = jnp.concatenate(left, axis=1)
    prod[...] = lax.dot_general(left, right, (((1,), (1,)), ((), ())), preferred_element_type=F32)

    pieces = []
    for c in range(0, count * azim, LANES):
        level = [prod[b * MAIN : (b + 1) * MAIN, c : c + LANES] for b in range(2 * rows)]
        by = 1
        while len(level) > 1:
            level = [level[i] + turn(level[i + 1], by, azim) for i in range(0, len(level), 2)]
            by *= 2
        extra = prod[2 * rows * MAIN : 2 * rows * (MAIN + 1), c : c + LANES]
        row = lax.broadcasted_iota(jnp.int32, extra.shape, 0)
        by = 1
        while by < 2 * rows:
            extra = jnp.where((row & by) != 0, turn(extra, by, azim), extra)
            by *= 2
        tail = jnp.broadcast_to(jnp.sum(extra, axis=0, keepdims=True), (8, LANES))
        pieces.append(jnp.concatenate([level[0], tail], axis=0))
    result = jnp.concatenate(pieces, axis=1)
    for i, out in enumerate(outs):
        @pl.when(step == i)
        def _(out=out):
            out[...] = result


def close_kernel(factor, count, azim, *refs):
    out = refs[-1]
    total = refs[0][...]
    for ref in refs[1:-1]:
        total = total + ref[...]
    total = total * factor
    groups = LANES // azim
    lane = lax.broadcasted_iota(jnp.int32, (count, LANES), 1) // azim
    sub = lax.broadcasted_iota(jnp.int32, (count, LANES), 0)
    for tile in range(-(-LAGS // groups)):
        acc = jnp.zeros((count, LANES), F32)
        for j in range(groups):
            tau = tile * groups + j
            if tau >= LAGS:
                continue
            x = jnp.zeros((count, LANES), F32)
            for part in range(count // groups):
                line = total[tau : tau + 1, part * LANES : (part + 1) * LANES]
                x = jnp.where(sub // groups == part, jnp.broadcast_to(line, (count, LANES)), x)
            moved = x
            for s in range(groups):
                by = ((j - s) * azim) % LANES
                shifted = pltpu.roll(x, by, 1) if by else x
                moved = jnp.where(sub % groups == s, shifted, moved)
            acc = jnp.where(lane == j, moved, acc)
        width = min(LANES, (LAGS - tile * groups) * azim)
        out[0, :, tile * LANES : tile * LANES + width] = acc[:, :width]


def whole(shape):
    return pl.BlockSpec(shape, lambda *_: (0,) * len(shape))


def lag_rows(info, *arrays):
    own = arrays[0]
    stations = info_stations(own)
    rows, times = own.shape[1:]
    height = 2 * rows * (MAIN + 1)
    shape = (stations, 2, 2, height, times)
    return pl.pallas_call(
        lag_kernel,
        grid_spec=pltpu.PrefetchScalarGridSpec(
            num_scalar_prefetch=1,
            grid=(stations,),
            in_specs=[whole(x.shape) for x in arrays],
            out_specs=pl.BlockSpec((1,) + shape[1:], lambda i, info: (i, 0, 0, 0, 0)),
        ),
        out_shape=jax.ShapeDtypeStruct(shape, BF16),
        compiler_params=pltpu.CompilerParams(vmem_limit_bytes=24 << 20),
        cost_estimate=pl.CostEstimate(flops=20_000_000, bytes_accessed=6 << 20, transcendentals=0),
    )(info, *arrays)


def info_stations(own):
    return own.shape[0] // 4


def products(info, offsets, lags, pieces):
    stations = lags.shape[0]
    half = pieces[4].shape[0]
    rows, times = pieces[0].shape[1:]
    columns = offsets.shape[0] * 4 * rows
    out = jax.ShapeDtypeStruct((MAIN + 8, columns), F32)
    window = (3 * half, 2, 2 * rows, times)
    return pl.pallas_call(
        product_kernel,
        grid_spec=pltpu.PrefetchScalarGridSpec(
            num_scalar_prefetch=2,
            grid=(stations,),
            in_specs=[
                pl.BlockSpec((1,) + lags.shape[1:], lambda i, info, off: (info[2] ^ i, 0, 0, 0, 0))
            ]
            + [whole(x.shape) for x in pieces],
            out_specs=[whole(out.shape)] * stations,
            scratch_shapes=[
                pltpu.VMEM(window, BF16),
                pltpu.VMEM(window, BF16),
                pltpu.VMEM((lags.shape[3], columns), F32),
            ],
        ),
        out_shape=[out] * stations,
        compiler_params=pltpu.CompilerParams(vmem_limit_bytes=32 << 20),
        cost_estimate=pl.CostEstimate(
            flops=2 * 3 * stations * 2 * lags.shape[3] * times * columns,
            bytes_accessed=8 << 20, transcendentals=0,
        ),
    )(info, offsets, lags, *pieces)


def close(parts, factor, count, azim):
    return pl.pallas_call(
        functools.partial(close_kernel, factor, count, azim),
        out_shape=jax.ShapeDtypeStruct((1, count, LAGS * azim), F32),
        cost_estimate=pl.CostEstimate(flops=1_000_000, bytes_accessed=1 << 18, transcendentals=0),
    )(*parts)


def shards(velocity, pressure, offsets):
    sta, rows, times = velocity.shape
    gx_n, az_n, ta_n = (lax.axis_size(name) for name in ("gx", "az", "ta"))
    gx, az, ta = (lax.axis_index(name) for name in ("gx", "az", "ta"))
    assert az_n == 4 and sta == az_n * ta_n
    half, mine = sta // 2, sta // az_n
    core, row_y = az % 2, az // 2
    azim = rows * az_n
    factor = 1.0 / math.sqrt(times * ta_n * azim)

    sibling = [(i, i ^ 1) for i in range(az_n)]
    across = [(i, i ^ 2) for i in range(az_n)]
    gx_az = [(g, a) for g in range(gx_n) for a in range(az_n)]
    flat = lambda g, a: (g % gx_n) * az_n + a
    upstream = [(g, (g - 1) % gx_n) for g in range(gx_n)]
    diagonal = [(flat(g, a), flat(g - 1, a ^ 2)) for g, a in gx_az]
    mixed = [(flat(g, a), flat(g, a ^ 2) if a >= 2 else flat(g - 1, a ^ 2)) for g, a in gx_az]
    pair = lambda i: i if not 0 <= i < ta_n else i
    even_odd = [(i, i ^ 1 if (i ^ 1) < ta_n else i) for i in range(ta_n)]
    odd_even = [(i, min(max(((i + 1) ^ 1) - 1, 0), ta_n - 1)) for i in range(ta_n)]

    to_sibling = lambda x: lax.ppermute(x, "az", sibling)

    info = jnp.stack([
        core, row_y, ta, mine * az, mine * core, (gx == gx_n - 1).astype(jnp.int32),
    ]).astype(jnp.int32)

    left_edge, right_edge = velocity[:, :, :LANES], velocity[:, :, times - LANES :]
    even = ta % 2 == 0
    got_a = lax.ppermute(jnp.where(even, right_edge, left_edge), "ta", even_odd)
    got_b = lax.ppermute(jnp.where(even, left_edge, right_edge), "ta", odd_even)

    v_for = lax.dynamic_slice_in_dim(velocity, half * (1 - row_y), half, 0)
    far = lax.ppermute(jnp.concatenate([pressure[half:], v_for], axis=0), "az", across)
    up = lax.ppermute(pressure, "gx", upstream)
    upper = lax.ppermute(pressure[:half], ("gx", "az"), diagonal)
    third = lax.ppermute(jnp.where(row_y == 1, pressure[:half], pressure[half:]), ("gx", "az"), mixed)

    before = jnp.where(even, got_b, got_a) * (ta > 0).astype(F32)
    after = jnp.where(even, got_a, got_b) * (ta < ta_n - 1).astype(F32)
    lane = lax.broadcasted_iota(jnp.int32, before.shape, 2)
    halo = jnp.where(lane < LANES // 2, after, before)
    halo_for = lax.dynamic_slice_in_dim(halo, half * (1 - row_y), half, 0)
    halo_far = lax.ppermute(halo_for, "az", across)

    v_sib, p_sib = to_sibling(velocity), to_sibling(pressure)
    far_sib, halo_sib, halo_far_sib = to_sibling(far), to_sibling(halo), to_sibling(halo_far)
    lags = lag_rows(info, velocity, v_sib, far, far_sib, halo, halo_sib, halo_far, halo_far_sib)

    up_sib, upper_sib, third_sib = to_sibling(up), to_sibling(upper), to_sibling(third)
    outs = products(
        info, offsets, lags,
        [pressure, up, far, upper, third, p_sib, up_sib, far_sib, upper_sib, third_sib],
    )
    parts = [outs[0]]
    for k in range(1, ta_n):
        parts.append(lax.ppermute(outs[k], "ta", [(i, i ^ k) for i in range(ta_n)]))
    return close(parts, factor, offsets.shape[0], azim)


def solution(mesh):
    return jax.shard_map(
        shards,
        mesh=mesh,
        in_specs=(P("gx", "az", "ta"), P("gx", "az", "ta"), P()),
        out_specs=P(("gx", "az", "ta"), None, None),
        check_vma=False,
    )
```

time: 201 us -> 40.9 us (0.20)
  waiting for transfers between devices: 84.2 us -> 8.33 us
  matrix products: 45 us -> 0 us
  local copies, waits for them, and re-layouts: 44.3 us -> 3.08 us
  between operations: 13.5 us -> 0.14 us
  starting transfers between devices: 6.93 us -> 18.2 us
  Pallas kernels: 0 us -> 8.94 us
  other arithmetic: 4.56 us -> 1.83 us
    unnamed x3 -> x0, waiting for transfers between devices: 55 us -> none
    dot_general x4 -> x0, matrix products: 45 us -> none  [the longest x2 32.5 us: one_block(): jnp.einsum('spjt,skqt->spjkq', stacked, partners, precision=lax.Precision...]
    another operation x70 -> x1, local copies, waits for them, and re-layouts: 31.7 us -> 0.08 us  [shards(): jnp.stack([core, row_y, ta, mine * az, mine * core, (gx == gx_n - 1).asty...]
    all_gather x1 -> x0, waiting for transfers between devices: 17.9 us -> none  [shards(): lax.all_gather(padded, 'az', axis=1, tiled=True)]
    ppermute x3 -> x18, starting transfers between devices: 6.89 us -> 18.2 us  [the longest x3 6.75 us: shards(): parts.append(lax.ppermute(outs[k], 'ta', [(i, i ^ k) for i in range(ta_n)]))]
    pallas_call x0 -> x3, Pallas kernels: none -> 8.94 us  [the longest x1 4.77 us: products(): pl.pallas_call(product_kernel, grid_spec=pltpu.PrefetchScalarGridSpec(num...]
    gather x2 -> x0, local copies, waits for them, and re-layouts: 4.32 us -> none  [one_block(): jnp.take(pres_block, indices, axis=0)]
    mul x2 -> x0, local copies, waits for them, and re-layouts: 3.64 us -> none  [shards(): partial_value = (totals * factor).reshape(sta_dev, NBR, LAGS * AZIM)]
  transfers between devices with their start and end apart: 5 -> 18, of which waited for: 5 -> 4; matrix products, arithmetic and copies ran while one was open for 1% -> 5% of each run, Pallas kernels for 0% -> 6%
where the time goes in v1:
time: 40.9 us; the launch traced here: 40.6 us
  starting transfers between devices  18.2 us (44%)
  Pallas kernels  8.94 us (22%)
  waiting for transfers between devices  8.33 us (20%)
  local copies, waits for them, and re-layouts  3.08 us (8%)
  other arithmetic  1.83 us (4%)
    ppermute x3, starting transfers between devices, shards(): parts.append(lax.ppermute(outs[k], 'ta', [(i, i ^ k) for i in range(ta_n)]))  6.75 us
    pallas_call x1, Pallas kernels, products(): pl.pallas_call(product_kernel, grid_spec=pltpu.PrefetchScalarGridSpec(num...  4.77 us
    ppermute x3, waiting for transfers between devices, shards(): parts.append(lax.ppermute(outs[k], 'ta', [(i, i ^ k) for i in range(ta_n)]))  3.73 us
    ppermute x1, starting transfers between devices, shards(): got_a = lax.ppermute(jnp.where(even, right_edge, left_edge), 'ta', even_odd)  3.09 us
    pallas_call x1, Pallas kernels, lag_rows(): pl.pallas_call(lag_kernel, grid_spec=pltpu.PrefetchScalarGridSpec(num_sca...  2.54 us
    ppermute x1, starting transfers between devices, shards(): lax.ppermute(jnp.where(row_y == 1, pressure[:half], pressure[half:]), ('g...  2.45 us
    ppermute x1, waiting for transfers between devices, shards(): upper = lax.ppermute(pressure[:half], ('gx', 'az'), diagonal)  2.22 us
    unnamed x14, local copies, waits for them, and re-layouts  2.14 us
  transfers between devices with their start and end apart: 18, of which 4 were waited for; matrix products, arithmetic and copies ran while one was open for 5% of the time, Pallas kernels for 6%

profile of v1, /device:TPU:0, one launch (start us, length us, event | category | flops | bytes accessed | tf_op | source)
XLA Modules:
  0.0 40.6 jit_solution(1529635501894698181)
XLA Ops:
  0.0 0.9 %slice_select_fusion.1 = (f32[16,8,128]{2,1,0:T(8,128)S(1)}, f32[16,8,128]{2,1,0:T(8,128)S(1)}) fusion(f32[16,8,256]{2,1,0:T(8,128)} %v_own.1, pred[]{:T(512)S(6)} %eq.13), kind=kLoop, calls=%fused_computation.3 | loop fusion | flops 32768 | bytes 262145 | tf_op jit(solution)/shard_map/jit(_where)/select_n | solution.py:276
  0.9 3.1 %collective-permute-start.3 = (f32[16,8,128]{2,1,0:T(8,128)S(1)}, f32[16,8,128]{2,1,0:T(8,128)S(1)}, u32[]{:S(2)}, u32[]{:S(2)}) collective-permute-start(f32[16,8,128]{2,1,0:T(8,128)S(1)} %get-tuple-element.16), channel_id=1, source_target_pairs={{0,1},{1,0},{2,3},{3,2},{4,5},{5,4},{6,7},{7,6},{8,9},{9,8},{10,11... | collective-permute-start | bytes 196616 | tf_op jit(solution)/shard_map/ppermute | solution.py:276
  4.0 0.7 %collective-permute-start.4 = (f32[16,8,128]{2,1,0:T(8,128)S(1)}, f32[16,8,128]{2,1,0:T(8,128)S(1)}, u32[]{:S(2)}, u32[]{:S(2)}) collective-permute-start(f32[16,8,128]{2,1,0:T(8,128)S(1)} %get-tuple-element.17), channel_id=1, source_target_pairs={{0,0},{1,2},{2,1},{3,3},{4,4},{5,6},{6,5},{7,7},{8,8},{9,10},{10,9... | collective-permute-start | bytes 196616 | tf_op jit(solution)/shard_map/ppermute | solution.py:277
  4.7 1.6 %collective-permute-start.8 = (f32[16,8,256]{2,1,0:T(8,128)}, f32[16,8,256]{2,1,0:T(8,128)S(1)}, u32[]{:S(2)}, u32[]{:S(2)}) collective-permute-start(f32[16,8,256]{2,1,0:T(8,128)} %o_own.1), channel_id=1, source_target_pairs={{0,16},{16,0},{1,17},{17,1},{2,18},{18,2},{3,19},{19,3},{4,20},{20... | collective-permute-start | bytes 393224 | tf_op jit(solution)/shard_map/ppermute | solution.py:281
  6.2 0.9 %broadcast_select_fusion = (f32[8,8,256]{2,1,0:T(8,128)S(1)}, f32[8,8,256]{2,1,0:T(8,128)S(1)}, f32[8,8,256]{2,1,0:T(8,128)S(1)}) fusion(pred[]{:T(512)S(6)} %eq.14, f32[16,8,256]{2,1,0:T(8,128)} %o_own.1), kind=kLoop, calls=%fused_computation.4 | loop fusion | flops 16384 | bytes 327681 | tf_op jit(solution)/shard_map/jit(_where)/select_n | solution.py:283
  7.1 0.8 %constant_dynamic-slice_fusion.1 = f32[8,8,256]{2,1,0:T(8,128)S(1)} fusion(f32[16,8,256]{2,1,0:T(8,128)} %v_own.1, s32[]{:T(128)S(6)} %select_n.53), kind=kLoop, calls=%fused_computation.7 | loop fusion | bytes 131076 | tf_op jit(solution)/shard_map/dynamic_slice | solution.py:279
  8.0 1.6 %collective-permute-start.1 = (f32[16,8,256]{2,1,0:T(8,128)S(1)}, f32[16,8,256]{2,1,0:T(8,128)S(1)}, u32[]{:S(2)}, u32[]{:S(2)}) collective-permute-start(f32[16,8,256]{2,1,0:T(8,128)S(1)} %pad_maximum_fusion), channel_id=1, source_target_pairs={{0,8},{4,12},{8,0},{12,4},{1,9},{5,13},{9,1},{13,5},{2,10},{6,14},... | collective-permute-start | bytes 393224 | tf_op jit(solution)/shard_map/ppermute | solution.py:280
  9.6 0.5 %collective-permute-start.9 = (f32[8,8,256]{2,1,0:T(8,128)S(1)}, f32[8,8,256]{2,1,0:T(8,128)S(1)}, u32[]{:S(2)}, u32[]{:S(2)}) collective-permute-start(f32[8,8,256]{2,1,0:T(8,128)S(1)} %get-tuple-element.14), channel_id=1, source_target_pairs={{0,24},{4,28},{8,16},{12,20},{16,8},{20,12},{24,0},{28,4},{1,25},{... | collective-permute-start | bytes 196616 | tf_op jit(solution)/shard_map/ppermute | solution.py:282
  10.1 0.0 collective-permute-done.3
  10.1 2.4 %collective-permute-start.10 = (f32[8,8,256]{2,1,0:T(8,128)S(1)}, f32[8,8,256]{2,1,0:T(8,128)S(1)}, u32[]{:S(2)}, u32[]{:S(2)}) collective-permute-start(f32[8,8,256]{2,1,0:T(8,128)S(1)} %get-tuple-element.13), channel_id=1, source_target_pairs={{0,24},{4,28},{8,0},{12,4},{16,8},{20,12},{24,16},{28,20},{1,25},{... | collective-permute-start | bytes 196616 | tf_op jit(solution)/shard_map/ppermute | solution.py:283
  12.5 0.0 collective-permute-done.4
  12.6 0.1 collective-permute-start.6
  12.6 2.2 %collective-permute-done.9.upper = f32[8,8,256]{2,1,0:T(8,128)S(1)} collective-permute-done((f32[8,8,256]{2,1,0:T(8,128)S(1)}, f32[8,8,256]{2,1,0:T(8,128)S(1)}, u32[]{:S(2)}, u32[]{:S(2)}) %collective-permute-start.9) | collective-permute-done | bytes 65568 | tf_op jit(solution)/shard_map/ppermute | solution.py:282
  14.9 0.0 collective-permute-start
  14.9 1.7 %collective-permute-done.6.h_far = f32[8,8,128]{2,1,0:T(8,128)S(1)} collective-permute-done((f32[8,8,128]{2,1,0:T(8,128)S(1)}, f32[8,8,128]{2,1,0:T(8,128)S(1)}, u32[]{:S(2)}, u32[]{:S(2)}) %collective-permute-start.6) | collective-permute-done | bytes 32800 | tf_op jit(solution)/shard_map/ppermute | solution.py:290
  16.5 0.0 collective-permute-start.7
  16.5 0.0 collective-permute-done.1.v_far.near
  16.5 0.5 %collective-permute-start.2 = (f32[16,8,256]{2,1,0:T(8,128)S(1)}, f32[16,8,256]{2,1,0:T(8,128)S(1)}, u32[]{:S(2)}, u32[]{:S(2)}) collective-permute-start(f32[16,8,256]{2,1,0:T(8,128)S(1)} %collective-permute-done.1.v_far.near), channel_id=1, source_target_pairs={{0,4},{4,0},{8,12},{12,8},{1,5},{5,1},{9,13},{13,9},{2,6},{6,2},{1... | collective-permute-start | bytes 393224 | tf_op jit(solution)/shard_map/ppermute | solution.py:268
  17.0 0.0 collective-permute-done.10.third
  17.1 0.1 collective-permute-start.5
  17.1 0.6 %collective-permute-done.7.h_far_sib = f32[8,8,128]{2,1,0:T(8,128)S(1)} collective-permute-done((f32[8,8,128]{2,1,0:T(8,128)S(1)}, f32[8,8,128]{2,1,0:T(8,128)S(1)}, u32[]{:S(2)}, u32[]{:S(2)}) %collective-permute-start.7) | collective-permute-done | bytes 32800 | tf_op jit(solution)/shard_map/ppermute | solution.py:268
  17.7 0.2 collective-permute-start.11
  17.9 0.0 collective-permute-done.8.u_own
  17.9 0.3 collective-permute-start.12
  18.3 0.1 collective-permute-done.5.h_sib
  18.3 0.2 collective-permute-start.13
  18.5 0.0 collective-permute-done.v_sib
  18.5 0.3 collective-permute-start.14
  18.8 0.1 stack.31.info
  18.9 0.0 collective-permute-done.2.v_far_sib.near_sib
  18.9 0.9 %copy-done = f32[16,8,256]{2,1,0:T(8,128)S(1)} copy-done((f32[16,8,256]{2,1,0:T(8,128)S(1)}, f32[16,8,256]{2,1,0:T(8,128)}, u32[]{:S(2)}) %copy-start) | copy-done | bytes 131096
  19.8 2.5 %shard_map.37.lags = bf16[4,2,2,528,256]{4,3,2,1,0:T(8,128)(2,1)S(1)} custom-call(s32[6]{0:T(128)S(1)} %stack.31.info, f32[16,8,256]{2,1,0:T(8,128)S(1)} %copy-done, f32[16,8,256]{2,1,0:T(8,128)S(1)} %collective-permute-done.v_sib, f32[16,8,256]{2,1,0:T(8,128)S(1)} %collective-permute-done.1.v_far.near, ...), custom_call_target="tpu_custom_call" | custom-call | flops 20000000 | bytes 6291456 | tf_op jit(solution)/shard_map/pallas_call | solution.py:189
  22.4 0.0 collective-permute-done.13.upper_sib
  22.4 0.0 collective-permute-done.14.third_sib
  22.4 0.0 collective-permute-done.11.o_sib
  22.4 0.0 collective-permute-done.12.u_sib
  22.4 0.0 copy-done.1
  22.4 4.8 %shard_map.38 = (f32[40,256]{1,0:T(8,128)S(1)}, f32[40,256]{1,0:T(8,128)S(1)}, f32[40,256]{1,0:T(8,128)S(1)}, f32[40,256]{1,0:T(8,128)S(1)}) custom-call(s32[6]{0:T(128)S(1)} %stack.31.info, s32[8]{0:T(128)S(1)} %copy-done.3, bf16[4,2,2,528,256]{4,3,2,1,0:T(8,128)(2,1)S(1)} %shard_map.37.lags, f32[16,8,256]{2,1,0:T(8,128)S(1)} %copy-done.1, ...), custom_call_target="tpu_custom_call" | custom-call | flops 1660944384 | bytes 8388608 | tf_op jit(solution)/shard_map/pallas_call | solution.py:214
  27.2 0.6 %copy-done.2 = f32[40,256]{1,0:T(8,128)} copy-done((f32[40,256]{1,0:T(8,128)}, f32[40,256]{1,0:T(8,128)S(1)}, u32[]{:S(2)}) %copy-start.2) | copy-done | bytes 40984
  27.8 4.4 %collective-permute-start.15 = (f32[40,256]{1,0:T(8,128)S(1)}, f32[40,256]{1,0:T(8,128)S(1)}, u32[]{:S(2)}, u32[]{:S(2)}) collective-permute-start(f32[40,256]{1,0:T(8,128)S(1)} %get-tuple-element.10), channel_id=1, source_target_pairs={{0,1},{1,0},{2,3},{3,2},{4,5},{5,4},{6,7},{7,6},{8,9},{9,8},{10,11... | collective-permute-start | bytes 122888 | tf_op jit(solution)/shard_map/ppermute | solution.py:303
  32.2 0.0 collective-permute-start.16
  32.2 2.4 %collective-permute-start.17 = (f32[40,256]{1,0:T(8,128)S(1)}, f32[40,256]{1,0:T(8,128)S(1)}, u32[]{:S(2)}, u32[]{:S(2)}) collective-permute-start(f32[40,256]{1,0:T(8,128)S(1)} %get-tuple-element.12), channel_id=1, source_target_pairs={{0,3},{1,2},{2,1},{3,0},{4,7},{5,6},{6,5},{7,4},{8,11},{9,10},{10,... | collective-permute-start | bytes 122888 | tf_op jit(solution)/shard_map/ppermute | solution.py:303
  34.6 0.0 collective-permute-done.15.refs_1_
  34.6 3.7 %collective-permute-done.16.refs_2_ = f32[40,256]{1,0:T(8,128)S(1)} collective-permute-done((f32[40,256]{1,0:T(8,128)S(1)}, f32[40,256]{1,0:T(8,128)S(1)}, u32[]{:S(2)}, u32[]{:S(2)}) %collective-permute-start.16) | collective-permute-done | bytes 40992 | tf_op jit(solution)/shard_map/ppermute | solution.py:303
  38.3 0.0 collective-permute-done.17.refs_3_
  38.3 0.6 %copy-done.5 = f32[40,256]{1,0:T(8,128)} copy-done((f32[40,256]{1,0:T(8,128)}, f32[40,256]{1,0:T(8,128)S(1)}, u32[]{:S(2)}) %copy-start.5) | copy-done | bytes 40984
  38.9 0.0 copy-done.6
  38.9 1.6 %shard_map.39 = f32[1,8,1056]{2,1,0:T(8,128)} custom-call(f32[40,256]{1,0:T(8,128)} %copy-done.2, f32[40,256]{1,0:T(8,128)} %copy-done.4, f32[40,256]{1,0:T(8,128)} %copy-done.5, f32[40,256]{1,0:T(8,128)} %copy-done.6), custom_call_target="tpu_custom_call" | custom-call | flops 1000000 | bytes 262144 | tf_op jit(solution)/shard_map/pallas_call | solution.py:240
  (13 shorter events, 0.1 us)
Async XLA Ops:
  0.0 22.4 %copy-start.1 = (f32[16,8,256]{2,1,0:T(8,128)S(1)}, f32[16,8,256]{2,1,0:T(8,128)}, u32[]{:S(2)}) copy-start(f32[16,8,256]{2,1,0:T(8,128)} %o_own.1) | copy-start | bytes 393220
  0.0 22.4 %copy-start.3 = (s32[8]{0:T(128)S(1)}, s32[8]{0:T(128)}, u32[]{:S(2)}) copy-start(s32[8]{0:T(128)} %offsets.1) | copy-start | bytes 100
  0.9 9.1 %collective-permute-start.3 = (f32[16,8,128]{2,1,0:T(8,128)S(1)}, f32[16,8,128]{2,1,0:T(8,128)S(1)}, u32[]{:S(2)}, u32[]{:S(2)}) collective-permute-start(f32[16,8,128]{2,1,0:T(8,128)S(1)} %get-tuple-element.16), channel_id=1, source_target_pairs={{0,1},{1,0},{2,3},{3,2},{4,5},{5,4},{6,7},{7,6},{8,9},{9,8},{10,11... | collective-permute-start | bytes 196616 | tf_op jit(solution)/shard_map/ppermute | solution.py:276
  4.0 8.5 %collective-permute-start.4 = (f32[16,8,128]{2,1,0:T(8,128)S(1)}, f32[16,8,128]{2,1,0:T(8,128)S(1)}, u32[]{:S(2)}, u32[]{:S(2)}) collective-permute-start(f32[16,8,128]{2,1,0:T(8,128)S(1)} %get-tuple-element.17), channel_id=1, source_target_pairs={{0,0},{1,2},{2,1},{3,3},{4,4},{5,6},{6,5},{7,7},{8,8},{9,10},{10,9... | collective-permute-start | bytes 196616 | tf_op jit(solution)/shard_map/ppermute | solution.py:277
  4.7 13.2 %collective-permute-start.8 = (f32[16,8,256]{2,1,0:T(8,128)}, f32[16,8,256]{2,1,0:T(8,128)S(1)}, u32[]{:S(2)}, u32[]{:S(2)}) collective-permute-start(f32[16,8,256]{2,1,0:T(8,128)} %o_own.1), channel_id=1, source_target_pairs={{0,16},{16,0},{1,17},{17,1},{2,18},{18,2},{3,19},{19,3},{4,20},{20... | collective-permute-start | bytes 393224 | tf_op jit(solution)/shard_map/ppermute | solution.py:281
  8.0 8.5 %collective-permute-start.1 = (f32[16,8,256]{2,1,0:T(8,128)S(1)}, f32[16,8,256]{2,1,0:T(8,128)S(1)}, u32[]{:S(2)}, u32[]{:S(2)}) collective-permute-start(f32[16,8,256]{2,1,0:T(8,128)S(1)} %pad_maximum_fusion), channel_id=1, source_target_pairs={{0,8},{4,12},{8,0},{12,4},{1,9},{5,13},{9,1},{13,5},{2,10},{6,14},... | collective-permute-start | bytes 393224 | tf_op jit(solution)/shard_map/ppermute | solution.py:280
  9.6 5.3 %collective-permute-start.9 = (f32[8,8,256]{2,1,0:T(8,128)S(1)}, f32[8,8,256]{2,1,0:T(8,128)S(1)}, u32[]{:S(2)}, u32[]{:S(2)}) collective-permute-start(f32[8,8,256]{2,1,0:T(8,128)S(1)} %get-tuple-element.14), channel_id=1, source_target_pairs={{0,24},{4,28},{8,16},{12,20},{16,8},{20,12},{24,0},{28,4},{1,25},{... | collective-permute-start | bytes 196616 | tf_op jit(solution)/shard_map/ppermute | solution.py:282
  10.1 7.0 %collective-permute-start.10 = (f32[8,8,256]{2,1,0:T(8,128)S(1)}, f32[8,8,256]{2,1,0:T(8,128)S(1)}, u32[]{:S(2)}, u32[]{:S(2)}) collective-permute-start(f32[8,8,256]{2,1,0:T(8,128)S(1)} %get-tuple-element.13), channel_id=1, source_target_pairs={{0,24},{4,28},{8,0},{12,4},{16,8},{20,12},{24,16},{28,20},{1,25},{... | collective-permute-start | bytes 196616 | tf_op jit(solution)/shard_map/ppermute | solution.py:283
  12.6 4.0 %collective-permute-start.6 = (f32[8,8,128]{2,1,0:T(8,128)S(1)}, f32[8,8,128]{2,1,0:T(8,128)S(1)}, u32[]{:S(2)}, u32[]{:S(2)}) collective-permute-start(f32[8,8,128]{2,1,0:T(8,128)S(1)} %constant_dynamic-slice_fusion), channel_id=1, source_target_pairs={{0,8},{4,12},{8,0},{12,4},{1,9},{5,13},{9,1},{13,5},{2,10},{6,14},... | collective-permute-start | bytes 98312 | tf_op jit(solution)/shard_map/ppermute | solution.py:290
  14.9 3.6 %collective-permute-start = (f32[16,8,256]{2,1,0:T(8,128)}, f32[16,8,256]{2,1,0:T(8,128)S(1)}, u32[]{:S(2)}, u32[]{:S(2)}) collective-permute-start(f32[16,8,256]{2,1,0:T(8,128)} %v_own.1), channel_id=1, source_target_pairs={{0,4},{4,0},{8,12},{12,8},{1,5},{5,1},{9,13},{13,9},{2,6},{6,2},{1... | collective-permute-start | bytes 393224 | tf_op jit(solution)/shard_map/ppermute | solution.py:268
  16.5 1.2 %collective-permute-start.7 = (f32[8,8,128]{2,1,0:T(8,128)S(1)}, f32[8,8,128]{2,1,0:T(8,128)S(1)}, u32[]{:S(2)}, u32[]{:S(2)}) collective-permute-start(f32[8,8,128]{2,1,0:T(8,128)S(1)} %collective-permute-done.6.h_far), channel_id=1, source_target_pairs={{0,4},{4,0},{8,12},{12,8},{1,5},{5,1},{9,13},{13,9},{2,6},{6,2},{1... | collective-permute-start | bytes 98312 | tf_op jit(solution)/shard_map/ppermute | solution.py:268
  16.5 2.4 %collective-permute-start.2 = (f32[16,8,256]{2,1,0:T(8,128)S(1)}, f32[16,8,256]{2,1,0:T(8,128)S(1)}, u32[]{:S(2)}, u32[]{:S(2)}) collective-permute-start(f32[16,8,256]{2,1,0:T(8,128)S(1)} %collective-permute-done.1.v_far.near), channel_id=1, source_target_pairs={{0,4},{4,0},{8,12},{12,8},{1,5},{5,1},{9,13},{13,9},{2,6},{6,2},{1... | collective-permute-start | bytes 393224 | tf_op jit(solution)/shard_map/ppermute | solution.py:268
  17.1 1.3 %collective-permute-start.5 = (f32[16,8,128]{2,1,0:T(8,128)S(1)}, f32[16,8,128]{2,1,0:T(8,128)S(1)}, u32[]{:S(2)}, u32[]{:S(2)}) collective-permute-start(f32[16,8,128]{2,1,0:T(8,128)S(1)} %multiply_select_fusion.h_own), channel_id=1, source_target_pairs={{0,4},{4,0},{8,12},{12,8},{1,5},{5,1},{9,13},{13,9},{2,6},{6,2},{1... | collective-permute-start | bytes 196616 | tf_op jit(solution)/shard_map/ppermute | solution.py:268
  17.7 4.6 %collective-permute-start.11 = (f32[16,8,256]{2,1,0:T(8,128)}, f32[16,8,256]{2,1,0:T(8,128)S(1)}, u32[]{:S(2)}, u32[]{:S(2)}) collective-permute-start(f32[16,8,256]{2,1,0:T(8,128)} %o_own.1), channel_id=1, source_target_pairs={{0,4},{4,0},{8,12},{12,8},{1,5},{5,1},{9,13},{13,9},{2,6},{6,2},{1... | collective-permute-start | bytes 393224 | tf_op jit(solution)/shard_map/ppermute | solution.py:268
  17.9 4.5 %collective-permute-start.12 = (f32[16,8,256]{2,1,0:T(8,128)S(1)}, f32[16,8,256]{2,1,0:T(8,128)S(1)}, u32[]{:S(2)}, u32[]{:S(2)}) collective-permute-start(f32[16,8,256]{2,1,0:T(8,128)S(1)} %collective-permute-done.8.u_own), channel_id=1, source_target_pairs={{0,4},{4,0},{8,12},{12,8},{1,5},{5,1},{9,13},{13,9},{2,6},{6,2},{1... | collective-permute-start | bytes 393224 | tf_op jit(solution)/shard_map/ppermute | solution.py:268
  18.3 4.1 %collective-permute-start.13 = (f32[8,8,256]{2,1,0:T(8,128)S(1)}, f32[8,8,256]{2,1,0:T(8,128)S(1)}, u32[]{:S(2)}, u32[]{:S(2)}) collective-permute-start(f32[8,8,256]{2,1,0:T(8,128)S(1)} %collective-permute-done.9.upper), channel_id=1, source_target_pairs={{0,4},{4,0},{8,12},{12,8},{1,5},{5,1},{9,13},{13,9},{2,6},{6,2},{1... | collective-permute-start | bytes 196616 | tf_op jit(solution)/shard_map/ppermute | solution.py:268
  18.5 3.9 %collective-permute-start.14 = (f32[8,8,256]{2,1,0:T(8,128)S(1)}, f32[8,8,256]{2,1,0:T(8,128)S(1)}, u32[]{:S(2)}, u32[]{:S(2)}) collective-permute-start(f32[8,8,256]{2,1,0:T(8,128)S(1)} %collective-permute-done.10.third), channel_id=1, source_target_pairs={{0,4},{4,0},{8,12},{12,8},{1,5},{5,1},{9,13},{13,9},{2,6},{6,2},{1... | collective-permute-start | bytes 196616 | tf_op jit(solution)/shard_map/ppermute | solution.py:268
  18.9 0.9 %copy-start = (f32[16,8,256]{2,1,0:T(8,128)S(1)}, f32[16,8,256]{2,1,0:T(8,128)}, u32[]{:S(2)}) copy-start(f32[16,8,256]{2,1,0:T(8,128)} %v_own.1) | copy-start | bytes 393220
  27.2 0.6 %copy-start.2 = (f32[40,256]{1,0:T(8,128)}, f32[40,256]{1,0:T(8,128)S(1)}, u32[]{:S(2)}) copy-start(f32[40,256]{1,0:T(8,128)S(1)} %get-tuple-element.9.refs_0_) | copy-start | bytes 122884
  27.8 6.8 %collective-permute-start.15 = (f32[40,256]{1,0:T(8,128)S(1)}, f32[40,256]{1,0:T(8,128)S(1)}, u32[]{:S(2)}, u32[]{:S(2)}) collective-permute-start(f32[40,256]{1,0:T(8,128)S(1)} %get-tuple-element.10), channel_id=1, source_target_pairs={{0,1},{1,0},{2,3},{3,2},{4,5},{5,4},{6,7},{7,6},{8,9},{9,8},{10,11... | collective-permute-start | bytes 122888 | tf_op jit(solution)/shard_map/ppermute | solution.py:303
  32.2 6.1 %collective-permute-start.16 = (f32[40,256]{1,0:T(8,128)S(1)}, f32[40,256]{1,0:T(8,128)S(1)}, u32[]{:S(2)}, u32[]{:S(2)}) collective-permute-start(f32[40,256]{1,0:T(8,128)S(1)} %get-tuple-element.11), channel_id=1, source_target_pairs={{0,2},{1,3},{2,0},{3,1},{4,6},{5,7},{6,4},{7,5},{8,10},{9,11},{10,... | collective-permute-start | bytes 122888 | tf_op jit(solution)/shard_map/ppermute | solution.py:303
  32.2 6.1 %collective-permute-start.17 = (f32[40,256]{1,0:T(8,128)S(1)}, f32[40,256]{1,0:T(8,128)S(1)}, u32[]{:S(2)}, u32[]{:S(2)}) collective-permute-start(f32[40,256]{1,0:T(8,128)S(1)} %get-tuple-element.12), channel_id=1, source_target_pairs={{0,3},{1,2},{2,1},{3,0},{4,7},{5,6},{6,5},{7,4},{8,11},{9,10},{10,... | collective-permute-start | bytes 122888 | tf_op jit(solution)/shard_map/ppermute | solution.py:303
  34.6 3.7 %copy-start.4 = (f32[40,256]{1,0:T(8,128)}, f32[40,256]{1,0:T(8,128)S(1)}, u32[]{:S(2)}) copy-start(f32[40,256]{1,0:T(8,128)S(1)} %collective-permute-done.15.refs_1_) | copy-start | bytes 122884
  38.3 0.6 %copy-start.5 = (f32[40,256]{1,0:T(8,128)}, f32[40,256]{1,0:T(8,128)S(1)}, u32[]{:S(2)}) copy-start(f32[40,256]{1,0:T(8,128)S(1)} %collective-permute-done.16.refs_2_) | copy-start | bytes 122884
  38.3 0.6 %copy-start.6 = (f32[40,256]{1,0:T(8,128)}, f32[40,256]{1,0:T(8,128)S(1)}, u32[]{:S(2)}) copy-start(f32[40,256]{1,0:T(8,128)S(1)} %collective-permute-done.17.refs_3_) | copy-start | bytes 122884

commit v2 on v0

v2 whole, which is shorter than its diff:
```python
import functools
import math

import jax
import jax.numpy as jnp
from jax import lax
from jax.experimental import pallas as pl
from jax.experimental.pallas import tpu as pltpu
from jax.sharding import PartitionSpec as P

MAXLAG = 16
LAGS = 2 * MAXLAG + 1
MAIN = 2 * MAXLAG
LANES = 128
BF16 = jnp.bfloat16
F32 = jnp.float32


def split(x):
    high = x.astype(BF16)
    return high, (x - high.astype(F32)).astype(BF16)


def in_core_order(core, mine, other):
    first = jnp.where(core == 0, mine, other)
    second = jnp.where(core == 0, other, mine)
    return jnp.concatenate([first, second], axis=0)


def fetch_kernel(info, velocity, out, part):
    half = part.shape[0]
    for i in range(half):
        part[i] = velocity[(1 - info[1]) * half + i]
    out[...] = velocity[...]


def lag_kernel(flip, info, v_own, v_sib, v_far, v_far_sib, h_near, h_away, out):
    core, row_y = info[0], info[1]
    rows, times = v_own.shape[1:]
    width = times + LANES
    for i in range(out.shape[0]):
        station = info[2] ^ (flip + 2 * i)
        near = (v_own, v_sib, h_near, info[3] + station, row_y)
        away = (v_far, v_far_sib, h_away, info[4] + station, 1 - row_y)
        for v_a, v_b, h, at_v, place in (near, away):
            series = in_core_order(core, v_a[at_v], v_b[at_v])
            series = jnp.concatenate([series, h[info[4] + station]], axis=1)
            for b in range(2 * rows):
                line = jnp.broadcast_to(series[b : b + 1, :], (8, width))
                for half in range(MAIN // 16):
                    parts = [
                        pltpu.roll(line, (8 * g - MAXLAG) % width, 1, stride=1, stride_axis=0)[:, :times]
                        for g in (2 * half, 2 * half + 1)
                    ]
                    high, low = split(jnp.concatenate(parts, axis=0))
                    at = b * MAIN + 16 * half
                    out[i, 0, place, at : at + 16, :] = high
                    out[i, 1, place, at : at + 16, :] = low
            high, low = split(pltpu.roll(series, MAXLAG, 1)[:, :times])
            at = 2 * rows * MAIN
            out[i, 0, place, at : at + 2 * rows, :] = high
            out[i, 1, place, at : at + 2 * rows, :] = low


def turn(x, by, azim):
    lane = lax.broadcasted_iota(jnp.int32, x.shape, 1) % azim
    left = pltpu.roll(x, LANES - by, 1)
    right = pltpu.roll(x, azim - by, 1)
    return jnp.where(lane < azim - by, left, right)


def window_kernel(info, o_own, u_own, o_far, u_far, o_sib, u_sib, o_far_sib, u_far_sib, high_p, low_p):
    core, row_y, last_gx = info[0], info[1], info[5]
    half = o_own.shape[0] // 2
    keep_up = jnp.where(last_gx == 1, 0.0, 1.0).astype(F32)
    keep_mid = jnp.where((last_gx == 1) & (row_y == 1), 0.0, 1.0).astype(F32)
    near = (o_own, u_own, o_sib, u_sib, row_y)
    away = (o_far, u_far, o_far_sib, u_far_sib, 1 - row_y)

    def one(w, carry):
        shift = row_y * half + w
        for o_a, u_a, o_b, u_b, at in (near, away):
            low_slot = in_core_order(core, o_a[shift], o_b[shift])
            middle = in_core_order(
                core,
                jnp.where(row_y == 0, o_a[half + w], u_a[w]),
                jnp.where(row_y == 0, o_b[half + w], u_b[w]),
            )
            high_slot = in_core_order(core, u_a[shift], u_b[shift])
            for slot, x in enumerate((low_slot, middle * keep_mid, high_slot * keep_up)):
                high, low = split(x)
                high_p[slot * half + w, at] = high
                low_p[slot * half + w, at] = low
        return carry

    lax.fori_loop(0, half, one, 0)


def product_kernel(flip, info, offsets, lags, high_p, low_p, out, prod):
    core, place = info[0], info[2]
    half = high_p.shape[0] // 3
    rows, azim = high_p.shape[2] // 2, 2 * high_p.shape[2]
    count = offsets.shape[0]
    for i in range(out.shape[0]):
        station = place ^ (flip + 2 * i)
        first = (half // 2) * core + station
        right = []
        for turned in (0, 1):
            tiles = {0: [], 1: []}
            for k in range(count):
                w = first + offsets[k]
                for which, source in ((0, high_p), (1, low_p)):
                    tiles[which] += [source[w, turned], source[w, 1 - turned]]
            high = jnp.concatenate(tiles[0], axis=0)
            low = jnp.concatenate(tiles[1], axis=0)
            right += [high, low, high]
        right = jnp.concatenate(right, axis=1)
        left = []
        for y in (0, 1):
            left += [lags[i, 0, y], lags[i, 0, y], lags[i, 1, y]]
        left = jnp.concatenate(left, axis=1)
        prod[i] = lax.dot_general(left, right, (((1,), (1,)), ((), ())), preferred_element_type=F32)
        out[i] = diagonals(prod.at[i], rows, azim, count)


def diagonals(prod, rows, azim, count):
    pieces = []
    for c in range(0, count * azim, LANES):
        level = [prod[b * MAIN : (b + 1) * MAIN, c : c + LANES] for b in range(2 * rows)]
        by = 1
        while len(level) > 1:
            level = [level[i] + turn(level[i + 1], by, azim) for i in range(0, len(level), 2)]
            by *= 2
        extra = prod[2 * rows * MAIN : 2 * rows * (MAIN + 1), c : c + LANES]
        row = lax.broadcasted_iota(jnp.int32, extra.shape, 0)
        by = 1
        while by < 2 * rows:
            extra = jnp.where((row & by) != 0, turn(extra, by, azim), extra)
            by *= 2
        tail = jnp.broadcast_to(jnp.sum(extra, axis=0, keepdims=True), (8, LANES))
        pieces.append(jnp.concatenate([level[0], tail], axis=0))
    return jnp.concatenate(pieces, axis=1)


def close_kernel(factor, count, azim, *refs):
    mine, first, second, out = refs
    total = (mine[0] + first[0] + second[...]) * factor
    groups = LANES // azim
    lane = lax.broadcasted_iota(jnp.int32, (count, LANES), 1) // azim
    sub = lax.broadcasted_iota(jnp.int32, (count, LANES), 0)
    for tile in range(-(-LAGS // groups)):
        acc = jnp.zeros((count, LANES), F32)
        for j in range(groups):
            tau = tile * groups + j
            if tau >= LAGS:
                continue
            x = jnp.zeros((count, LANES), F32)
            for part in range(count // groups):
                line = total[tau : tau + 1, part * LANES : (part + 1) * LANES]
                x = jnp.where(sub // groups == part, jnp.broadcast_to(line, (count, LANES)), x)
            moved = x
            for s in range(groups):
                by = ((j - s) * azim) % LANES
                shifted = pltpu.roll(x, by, 1) if by else x
                moved = jnp.where(sub % groups == s, shifted, moved)
            acc = jnp.where(lane == j, moved, acc)
        width = min(LANES, (LAGS - tile * groups) * azim)
        out[0, :, tile * LANES : tile * LANES + width] = acc[:, :width]


VMEM = pl.BlockSpec(memory_space=pltpu.VMEM)
SMEM = pl.BlockSpec(memory_space=pltpu.SMEM)


def fetch(info, velocity):
    shape = velocity.shape
    return pl.pallas_call(
        fetch_kernel,
        in_specs=[SMEM, VMEM],
        out_specs=[VMEM, VMEM],
        out_shape=[
            jax.ShapeDtypeStruct(shape, F32),
            jax.ShapeDtypeStruct((shape[0] // 2,) + shape[1:], F32),
        ],
        compiler_params=pltpu.CompilerParams(vmem_limit_bytes=2 << 20),
        cost_estimate=pl.CostEstimate(flops=0, bytes_accessed=1 << 19, transcendentals=0),
    )(info, velocity)


def lag_rows(flip, info, stations, *arrays):
    rows, times = arrays[0].shape[1:]
    shape = (stations, 2, 2, 2 * rows * (MAIN + 1), times)
    return pl.pallas_call(
        functools.partial(lag_kernel, flip),
        in_specs=[SMEM] + [VMEM] * len(arrays),
        out_specs=VMEM,
        out_shape=jax.ShapeDtypeStruct(shape, BF16),
        compiler_params=pltpu.CompilerParams(vmem_limit_bytes=12 << 20),
        cost_estimate=pl.CostEstimate(flops=10_000_000, bytes_accessed=3 << 20, transcendentals=0),
    )(info, *arrays)


def window(info, pieces):
    stations, rows, times = pieces[0].shape
    shape = jax.ShapeDtypeStruct((stations // 2 * 3, 2, 2 * rows, times), BF16)
    return pl.pallas_call(
        window_kernel,
        in_specs=[SMEM] + [VMEM] * len(pieces),
        out_specs=[VMEM, VMEM],
        out_shape=[shape, shape],
        compiler_params=pltpu.CompilerParams(vmem_limit_bytes=8 << 20),
        cost_estimate=pl.CostEstimate(flops=2_000_000, bytes_accessed=2 << 20, transcendentals=0),
    )(info, *pieces)


def products(flip, info, offsets, lags, high_p, low_p):
    stations, _, _, height, times = lags.shape
    columns = offsets.shape[0] * 2 * high_p.shape[2]
    return pl.pallas_call(
        functools.partial(product_kernel, flip),
        in_specs=[SMEM, SMEM, VMEM, VMEM, VMEM],
        out_specs=VMEM,
        out_shape=jax.ShapeDtypeStruct((stations, MAIN + 8, columns), F32),
        scratch_shapes=[pltpu.VMEM((stations, height, columns), F32)],
        compiler_params=pltpu.CompilerParams(vmem_limit_bytes=24 << 20),
        cost_estimate=pl.CostEstimate(
            flops=2 * 3 * stations * 2 * height * times * columns,
            bytes_accessed=4 << 20, transcendentals=0,
        ),
    )(info, offsets, lags, high_p, low_p)


def close(parts, factor, count, azim):
    return pl.pallas_call(
        functools.partial(close_kernel, factor, count, azim),
        in_specs=[VMEM] * len(parts),
        out_specs=VMEM,
        out_shape=jax.ShapeDtypeStruct((1, count, LAGS * azim), F32),
        compiler_params=pltpu.CompilerParams(vmem_limit_bytes=4 << 20),
        cost_estimate=pl.CostEstimate(flops=1_000_000, bytes_accessed=1 << 18, transcendentals=0),
    )(*parts)


def shards(velocity, pressure, offsets):
    sta, rows, times = velocity.shape
    gx_n, az_n, ta_n = (lax.axis_size(name) for name in ("gx", "az", "ta"))
    gx, az, ta = (lax.axis_index(name) for name in ("gx", "az", "ta"))
    assert az_n == 4 and ta_n == 4 and sta == az_n * ta_n
    half, mine = sta // 2, sta // az_n
    core, row_y = az % 2, az // 2
    azim = rows * az_n
    factor = 1.0 / math.sqrt(times * ta_n * azim)

    sibling = [(i, i ^ 1) for i in range(az_n)]
    across = [(i, i ^ 2) for i in range(az_n)]
    gx_az = [(g, a) for g in range(gx_n) for a in range(az_n)]
    flat = lambda g, a: (g % gx_n) * az_n + a
    upstream = [(g, (g - 1) % gx_n) for g in range(gx_n)]
    diagonal = [(flat(g, a), flat(g - 1, a ^ 2)) for g, a in gx_az]
    pairs = (
        [i ^ 1 if (i ^ 1) < ta_n else i for i in range(ta_n)],
        [min(max(((i + 1) ^ 1) - 1, 0), ta_n - 1) for i in range(ta_n)],
    )
    az_ta = [(a, t) for a in range(az_n) for t in range(ta_n)]
    in_time = [(a * ta_n + t, a * ta_n + pairs[a % 2][t]) for a, t in az_ta]
    in_time_across = [(a * ta_n + t, (a ^ 2) * ta_n + pairs[a % 2][t]) for a, t in az_ta]

    to_sibling = lambda x: lax.ppermute(x, "az", sibling)

    info = jnp.stack([
        core, row_y, ta, mine * az, mine * core, (gx == gx_n - 1).astype(jnp.int32),
    ]).astype(jnp.int32)

    diag = lax.ppermute(pressure, ("gx", "az"), diagonal)
    far = lax.ppermute(pressure, "az", across)
    vel, v_for = fetch(info, velocity)
    v_sib = to_sibling(velocity)
    v_far = lax.ppermute(v_for, "az", across)
    later, v_far = lax.optimization_barrier((pressure, v_far))
    up = lax.ppermute(later, "gx", upstream)

    even = ta % 2 == 0
    use_right = even == (core == 0)

    def edge(x):
        return jnp.where(use_right, x[:, :, times - LANES :], x[:, :, :LANES])

    edge_own, edge_sib = edge(vel), edge(v_sib)
    first_core = jnp.where(core == 0, edge_own, edge_sib)
    second_core = jnp.where(core == 0, edge_sib, edge_own)
    edges = jnp.concatenate([first_core, second_core], axis=1)
    ends = [lax.dynamic_slice_in_dim(edges, half * at, half, 0) for at in (row_y, 1 - row_y)]
    h_near = lax.ppermute(ends[0], ("az", "ta"), in_time)
    h_away = lax.ppermute(ends[1], ("az", "ta"), in_time_across)

    def halo(mine, other):
        got_a = jnp.where(core == 0, mine, other)
        got_b = jnp.where(core == 0, other, mine)
        before = jnp.where(even, got_b, got_a) * (ta > 0).astype(F32)
        after = jnp.where(even, got_a, got_b) * (ta < ta_n - 1).astype(F32)
        lane = lax.broadcasted_iota(jnp.int32, before.shape, before.ndim - 1)
        return jnp.where(lane < LANES // 2, after, before)

    v_far_sib = to_sibling(v_far)
    series = (vel, v_sib, v_far, v_far_sib, halo(h_near, to_sibling(h_near)), halo(h_away, to_sibling(h_away)))
    lags_give = lag_rows(1, info, ta_n // 2, *series)
    p_sib, up_sib, diag_sib, far_sib = (to_sibling(x) for x in (pressure, up, diag, far))
    lags_keep = lag_rows(0, info, ta_n // 2, *series)
    high_p, low_p = window(info, [pressure, up, far, diag, p_sib, up_sib, far_sib, diag_sib])

    give = products(1, info, offsets, lags_give, high_p, low_p)
    first = lax.ppermute(give, "ta", [(i, i ^ 1) for i in range(ta_n)])
    keep = products(0, info, offsets, lags_keep, high_p, low_p)
    second = lax.ppermute(keep[1] + first[1], "ta", [(i, i ^ 2) for i in range(ta_n)])
    return close([keep, first, second], factor, offsets.shape[0], azim)


def solution(mesh):
    return jax.shard_map(
        shards,
        mesh=mesh,
        in_specs=(P("gx", "az", "ta"), P("gx", "az", "ta"), P()),
        out_specs=P(("gx", "az", "ta"), None, None),
        check_vma=False,
    )
```

time: 201 us -> 35 us (0.17)
  waiting for transfers between devices: 84.2 us -> 8.64 us
  matrix products: 45 us -> 0 us
  local copies, waits for them, and re-layouts: 44.3 us -> 1 us
  between operations: 13.5 us -> 0.15 us
  Pallas kernels: 0 us -> 9.28 us
  starting transfers between devices: 6.93 us -> 15.6 us
  other arithmetic: 4.56 us -> 0.08 us
    unnamed x3 -> x0, waiting for transfers between devices: 55 us -> none
    dot_general x4 -> x0, matrix products: 45 us -> none  [the longest x2 32.5 us: one_block(): jnp.einsum('spjt,skqt->spjkq', stacked, partners, precision=lax.Precision...]
    another operation x70 -> x1, local copies, waits for them, and re-layouts: 31.7 us -> 0.08 us  [shards(): jnp.stack([core, row_y, ta, mine * az, mine * core, (gx == gx_n - 1).asty...]
    all_gather x1 -> x0, waiting for transfers between devices: 17.9 us -> none  [shards(): lax.all_gather(padded, 'az', axis=1, tiled=True)]
    pallas_call x0 -> x7, Pallas kernels: none -> 9.28 us  [the longest x2 4.29 us: products(): pl.pallas_call(functools.partial(product_kernel, flip), in_specs=[SMEM, S...]
    ppermute x3 -> x16, starting transfers between devices: 6.89 us -> 15.6 us  [the longest x1 3 us: shards(): first = lax.ppermute(give, 'ta', [(i, i ^ 1) for i in range(ta_n)])]
    gather x2 -> x0, local copies, waits for them, and re-layouts: 4.32 us -> none  [one_block(): jnp.take(pres_block, indices, axis=0)]
    mul x2 -> x0, local copies, waits for them, and re-layouts: 3.64 us -> none  [shards(): partial_value = (totals * factor).reshape(sta_dev, NBR, LAGS * AZIM)]
  transfers between devices with their start and end apart: 5 -> 16, of which waited for: 5 -> 6; matrix products, arithmetic and copies ran while one was open for 1% -> 0% of each run, Pallas kernels for 0% -> 16%
where the time goes in v2:
time: 35 us; the launch traced here: 34.8 us
  starting transfers between devices  15.6 us (45%)
  Pallas kernels  9.28 us (27%)
  waiting for transfers between devices  8.64 us (25%)
  local copies, waits for them, and re-layouts  1 us (3%)
    pallas_call x2, Pallas kernels, products(): pl.pallas_call(functools.partial(product_kernel, flip), in_specs=[SMEM, S...  4.29 us
    ppermute x1, waiting for transfers between devices, shards(): lax.ppermute(keep[1] + first[1], 'ta', [(i, i ^ 2) for i in range(ta_n)])  3.51 us
    ppermute x1, starting transfers between devices, shards(): first = lax.ppermute(give, 'ta', [(i, i ^ 1) for i in range(ta_n)])  3 us
    pallas_call x2, Pallas kernels, lag_rows(): pl.pallas_call(functools.partial(lag_kernel, flip), in_specs=[SMEM] + [VM...  2.9 us
    ppermute x1, starting transfers between devices, shards(): diag = lax.ppermute(pressure, ('gx', 'az'), diagonal)  2.88 us
    ppermute x1, starting transfers between devices, shards(): v_far = lax.ppermute(v_for, 'az', across)  2.58 us
    ppermute x1, waiting for transfers between devices, shards(): diag = lax.ppermute(pressure, ('gx', 'az'), diagonal)  2.47 us
    ppermute x1, starting transfers between devices, shards(): h_near = lax.ppermute(ends[0], ('az', 'ta'), in_time)  1.98 us
  transfers between devices with their start and end apart: 16, of which 6 were waited for; matrix products, arithmetic and copies ran while one was open for 0% of the time, Pallas kernels for 16%

profile of v2, /device:TPU:0, one launch (start us, length us, event | category | flops | bytes accessed | tf_op | source)
XLA Modules:
  0.0 34.8 jit_solution(3915948314462534201)
XLA Ops:
  0.0 0.5 %collective-permute-start = (f32[16,8,256]{2,1,0:T(8,128)}, f32[16,8,256]{2,1,0:T(8,128)S(1)}, u32[]{:S(2)}, u32[]{:S(2)}) collective-permute-start(f32[16,8,256]{2,1,0:T(8,128)} %velocity.1), channel_id=1, source_target_pairs={{0,4},{4,0},{8,12},{12,8},{1,5},{5,1},{9,13},{13,9},{2,6},{6,2},{1... | collective-permute-start | bytes 393224 | tf_op jit(solution)/shard_map/ppermute | solution.py:268
  0.5 0.1 stack.31.info
  0.5 0.0 copy-start
  0.5 0.9 %copy-done = f32[16,8,256]{2,1,0:T(8,128)S(1)} copy-done((f32[16,8,256]{2,1,0:T(8,128)S(1)}, f32[16,8,256]{2,1,0:T(8,128)}, u32[]{:S(2)}) %copy-start) | copy-done | bytes 131096
  1.4 0.0 copy-start.1
  1.4 0.6 %shard_map.37 = (f32[16,8,256]{2,1,0:T(8,128)S(1)}, f32[8,8,256]{2,1,0:T(8,128)S(1)}) custom-call(s32[6]{0:T(128)S(1)} %stack.31.info, f32[16,8,256]{2,1,0:T(8,128)S(1)} %copy-done), custom_call_target="tpu_custom_call" | custom-call | bytes 524288 | tf_op jit(solution)/shard_map/pallas_call | solution.py:177
  2.0 2.6 %collective-permute-start.1 = (f32[8,8,256]{2,1,0:T(8,128)S(1)}, f32[8,8,256]{2,1,0:T(8,128)S(1)}, u32[]{:S(2)}, u32[]{:S(2)}) collective-permute-start(f32[8,8,256]{2,1,0:T(8,128)S(1)} %get-tuple-element.12), channel_id=1, source_target_pairs={{0,8},{4,12},{8,0},{12,4},{1,9},{5,13},{9,1},{13,5},{2,10},{6,14},... | collective-permute-start | bytes 196616 | tf_op jit(solution)/shard_map/ppermute | solution.py:278
  4.6 0.0 collective-permute-done.v_sib
  4.6 0.0 copy-start.2
  4.7 1.6 %collective-permute-start.5 = (f32[8,16,128]{2,1,0:T(8,128)S(1)}, f32[8,16,128]{2,1,0:T(8,128)S(1)}, u32[]{:S(2)}, u32[]{:S(2)}) collective-permute-start(f32[8,16,128]{2,1,0:T(8,128)S(1)} %get-tuple-element.19), channel_id=1, source_target_pairs={{0,9},{1,8},{2,11},{3,10},{4,12},{5,14},{6,13},{7,15},{8,1},{9,0},... | collective-permute-start | bytes 196616 | tf_op jit(solution)/shard_map/ppermute | solution.py:294
  6.2 2.0 %collective-permute-start.3 = (f32[8,16,128]{2,1,0:T(8,128)S(1)}, f32[8,16,128]{2,1,0:T(8,128)S(1)}, u32[]{:S(2)}, u32[]{:S(2)}) collective-permute-start(f32[8,16,128]{2,1,0:T(8,128)S(1)} %get-tuple-element.20), channel_id=1, source_target_pairs={{0,1},{1,0},{2,3},{3,2},{4,4},{5,6},{6,5},{7,7},{8,9},{9,8},{10,11... | collective-permute-start | bytes 196616 | tf_op jit(solution)/shard_map/ppermute | solution.py:293
  8.2 2.9 %collective-permute-start.9 = (f32[16,8,256]{2,1,0:T(8,128)}, f32[16,8,256]{2,1,0:T(8,128)S(1)}, u32[]{:S(2)}, u32[]{:S(2)}) collective-permute-start(f32[16,8,256]{2,1,0:T(8,128)} %o_own.1), channel_id=1, source_target_pairs={{0,24},{4,28},{8,16},{12,20},{16,8},{20,12},{24,0},{28,4},{1,25},{... | collective-permute-start | bytes 393224 | tf_op jit(solution)/shard_map/ppermute | solution.py:274
  11.1 0.5 %collective-permute-start.8 = (f32[16,8,256]{2,1,0:T(8,128)}, f32[16,8,256]{2,1,0:T(8,128)S(1)}, u32[]{:S(2)}, u32[]{:S(2)}) collective-permute-start(f32[16,8,256]{2,1,0:T(8,128)} %o_own.1), channel_id=1, source_target_pairs={{0,8},{4,12},{8,0},{12,4},{1,9},{5,13},{9,1},{13,5},{2,10},{6,14},... | collective-permute-start | bytes 393224 | tf_op jit(solution)/shard_map/ppermute | solution.py:275
  11.6 0.0 collective-permute-done.1.v_far
  11.6 0.2 collective-permute-start.7
  11.8 0.0 collective-permute-done.5
  11.8 0.0 collective-permute-start.6
  11.8 0.6 %collective-permute-done.3 = f32[8,16,128]{2,1,0:T(8,128)S(1)} collective-permute-done((f32[8,16,128]{2,1,0:T(8,128)S(1)}, f32[8,16,128]{2,1,0:T(8,128)S(1)}, u32[]{:S(2)}, u32[]{:S(2)}) %collective-permute-start.3) | collective-permute-done | bytes 65568 | tf_op jit(solution)/shard_map/ppermute | solution.py:293
  12.4 0.0 collective-permute-start.4
  12.4 2.5 %collective-permute-done.9.u_far = f32[16,8,256]{2,1,0:T(8,128)S(1)} collective-permute-done((f32[16,8,256]{2,1,0:T(8,128)}, f32[16,8,256]{2,1,0:T(8,128)S(1)}, u32[]{:S(2)}, u32[]{:S(2)}) %collective-permute-start.9) | collective-permute-done | bytes 131104 | tf_op jit(solution)/shard_map/ppermute | solution.py:274
  14.9 0.0 collective-permute-start.10
  14.9 1.4 %collective-permute-done.8.o_far = f32[16,8,256]{2,1,0:T(8,128)S(1)} collective-permute-done((f32[16,8,256]{2,1,0:T(8,128)}, f32[16,8,256]{2,1,0:T(8,128)S(1)}, u32[]{:S(2)}, u32[]{:S(2)}) %collective-permute-start.8) | collective-permute-done | bytes 131104 | tf_op jit(solution)/shard_map/ppermute | solution.py:275
  16.3 0.0 collective-permute-start.2
  16.3 0.5 %collective-permute-done.7.u_own = f32[16,8,256]{2,1,0:T(8,128)S(1)} collective-permute-done((f32[16,8,256]{2,1,0:T(8,128)}, f32[16,8,256]{2,1,0:T(8,128)S(1)}, u32[]{:S(2)}, u32[]{:S(2)}) %collective-permute-start.7) | collective-permute-done | bytes 131104 | tf_op jit(solution)/shard_map/ppermute | solution.py:280
  16.8 0.0 collective-permute-start.13
  16.8 0.0 collective-permute-done.6
  16.8 0.5 %collective-permute-start.12 = (f32[16,8,256]{2,1,0:T(8,128)S(1)}, f32[16,8,256]{2,1,0:T(8,128)S(1)}, u32[]{:S(2)}, u32[]{:S(2)}) collective-permute-start(f32[16,8,256]{2,1,0:T(8,128)S(1)} %collective-permute-done.8.o_far), channel_id=1, source_target_pairs={{0,4},{4,0},{8,12},{12,8},{1,5},{5,1},{9,13},{13,9},{2,6},{6,2},{1... | collective-permute-start | bytes 393224 | tf_op jit(solution)/shard_map/ppermute | solution.py:268
  17.3 0.0 collective-permute-done.4
  17.3 0.1 collective-permute-start.11
  17.4 0.1 collective-permute-done.2.v_far_sib
  17.5 1.4 %shard_map.41.lags = bf16[2,2,2,528,256]{4,3,2,1,0:T(8,128)(2,1)S(1)} custom-call(s32[6]{0:T(128)S(1)} %stack.31.info, f32[16,8,256]{2,1,0:T(8,128)S(1)} %get-tuple-element.11.v_own, f32[16,8,256]{2,1,0:T(8,128)S(1)} %collective-permute-done.v_sib, f32[8,8,256]{2,1,0:T(8,128)S(1)} %collective-permute-done.1.v_far, ...), custom_call_target="tpu_custom_call" | custom-call | flops 10000000 | bytes 3145728 | tf_op jit(solution)/shard_map/pallas_call | solution.py:193
  19.0 0.0 collective-permute-done.10.o_sib
  19.0 0.0 collective-permute-done.13.u_far_sib
  19.0 0.0 collective-permute-done.12.o_far_sib
  19.0 0.0 collective-permute-done.11.u_sib
  19.0 0.0 copy-done.1
  19.0 0.7 %shard_map.39 = (bf16[24,2,16,256]{3,2,1,0:T(8,128)(2,1)S(1)}, bf16[24,2,16,256]{3,2,1,0:T(8,128)(2,1)S(1)}) custom-call(s32[6]{0:T(128)S(1)} %stack.31.info, f32[16,8,256]{2,1,0:T(8,128)S(1)} %copy-done.1, f32[16,8,256]{2,1,0:T(8,128)S(1)} %collective-permute-done.7.u_own, f32[16,8,256]{2,1,0:T(8,128)S(1)} %collective-permute-done.8.o_far, ...), custom_call_target="tpu_custom_call" | custom-call | flops 2000000 | bytes 2097152 | tf_op jit(solution)/shard_map/pallas_call | solution.py:206
  19.8 0.0 copy-done.2
  19.8 2.1 %shard_map.42 = f32[2,40,256]{2,1,0:T(8,128)S(1)} custom-call(s32[6]{0:T(128)S(1)} %stack.31.info, s32[8]{0:T(128)S(1)} %copy-done.2, bf16[2,2,2,528,256]{4,3,2,1,0:T(8,128)(2,1)S(1)} %shard_map.41.lags, bf16[24,2,16,256]{3,2,1,0:T(8,128)(2,1)S(1)} %get-tuple-element.15.high_p, bf16[24,2,16,256]{3,2,1,0:T(8,128)(2,1)S(1)} %get-tuple-element.16.low_p), custom_call_target="tpu_custom_call" | custom-call | flops 830472192 | bytes 4194304 | tf_op jit(solution)/shard_map/pallas_call | solution.py:219
  22.0 3.0 %collective-permute-start.14 = (f32[2,40,256]{2,1,0:T(8,128)S(1)}, f32[2,40,256]{2,1,0:T(8,128)S(1)}, u32[]{:S(2)}, u32[]{:S(2)}) collective-permute-start(f32[2,40,256]{2,1,0:T(8,128)S(1)} %shard_map.42), channel_id=1, source_target_pairs={{0,1},{1,0},{2,3},{3,2},{4,5},{5,4},{6,7},{7,6},{8,9},{9,8},{10,11... | collective-permute-start | bytes 245768 | tf_op jit(solution)/shard_map/ppermute | solution.py:312
  25.0 1.4 %shard_map.38.lags = bf16[2,2,2,528,256]{4,3,2,1,0:T(8,128)(2,1)S(1)} custom-call(s32[6]{0:T(128)S(1)} %stack.31.info, f32[16,8,256]{2,1,0:T(8,128)S(1)} %get-tuple-element.11.v_own, f32[16,8,256]{2,1,0:T(8,128)S(1)} %collective-permute-done.v_sib, f32[8,8,256]{2,1,0:T(8,128)S(1)} %collective-permute-done.1.v_far, ...), custom_call_target="tpu_custom_call" | custom-call | flops 10000000 | bytes 3145728 | tf_op jit(solution)/shard_map/pallas_call | solution.py:193
  26.4 2.1 %shard_map.40.refs_0_ = f32[2,40,256]{2,1,0:T(8,128)S(1)} custom-call(s32[6]{0:T(128)S(1)} %stack.31.info, s32[8]{0:T(128)S(1)} %copy-done.2, bf16[2,2,2,528,256]{4,3,2,1,0:T(8,128)(2,1)S(1)} %shard_map.38.lags, bf16[24,2,16,256]{3,2,1,0:T(8,128)(2,1)S(1)} %get-tuple-element.15.high_p, bf16[24,2,16,256]{3,2,1,0:T(8,128)(2,1)S(1)} %get-tuple-element.16.low_p), custom_call_target="tpu_custom_call" | custom-call | flops 830472192 | bytes 4194304 | tf_op jit(solution)/shard_map/pallas_call | solution.py:219
  28.6 0.0 collective-permute-done.14.refs_1_
  28.6 1.9 %collective-permute-start.15 = (f32[40,256]{1,0:T(8,128)S(1)}, f32[40,256]{1,0:T(8,128)S(1)}, u32[]{:S(2)}, u32[]{:S(2)}) collective-permute-start(f32[40,256]{1,0:T(8,128)S(1)} %fusion.2), channel_id=1, source_target_pairs={{0,2},{1,3},{2,0},{3,1},{4,6},{5,7},{6,4},{7,5},{8,10},{9,11},{10,... | collective-permute-start | bytes 122888 | tf_op jit(solution)/shard_map/ppermute | solution.py:314
  30.5 3.5 %collective-permute-done.15.refs_2_ = f32[40,256]{1,0:T(8,128)S(1)} collective-permute-done((f32[40,256]{1,0:T(8,128)S(1)}, f32[40,256]{1,0:T(8,128)S(1)}, u32[]{:S(2)}, u32[]{:S(2)}) %collective-permute-start.15) | collective-permute-done | bytes 40992 | tf_op jit(solution)/shard_map/ppermute | solution.py:314
  34.0 0.8 %shard_map.43 = f32[1,8,1056]{2,1,0:T(8,128)} custom-call(f32[2,40,256]{2,1,0:T(8,128)S(1)} %shard_map.40.refs_0_, f32[2,40,256]{2,1,0:T(8,128)S(1)} %collective-permute-done.14.refs_1_, f32[40,256]{1,0:T(8,128)S(1)} %collective-permute-done.15.refs_2_), custom_call_target="tpu_custom_call" | custom-call | flops 1000000 | bytes 262144 | tf_op jit(solution)/shard_map/pallas_call | solution.py:234
  (5 shorter events, 0.1 us)
Async XLA Ops:
  0.0 4.6 %collective-permute-start = (f32[16,8,256]{2,1,0:T(8,128)}, f32[16,8,256]{2,1,0:T(8,128)S(1)}, u32[]{:S(2)}, u32[]{:S(2)}) collective-permute-start(f32[16,8,256]{2,1,0:T(8,128)} %velocity.1), channel_id=1, source_target_pairs={{0,4},{4,0},{8,12},{12,8},{1,5},{5,1},{9,13},{13,9},{2,6},{6,2},{1... | collective-permute-start | bytes 393224 | tf_op jit(solution)/shard_map/ppermute | solution.py:268
  0.5 0.9 %copy-start = (f32[16,8,256]{2,1,0:T(8,128)S(1)}, f32[16,8,256]{2,1,0:T(8,128)}, u32[]{:S(2)}) copy-start(f32[16,8,256]{2,1,0:T(8,128)} %velocity.1) | copy-start | bytes 393220
  1.4 17.6 %copy-start.1 = (f32[16,8,256]{2,1,0:T(8,128)S(1)}, f32[16,8,256]{2,1,0:T(8,128)}, u32[]{:S(2)}) copy-start(f32[16,8,256]{2,1,0:T(8,128)} %o_own.1) | copy-start | bytes 393220
  2.0 9.6 %collective-permute-start.1 = (f32[8,8,256]{2,1,0:T(8,128)S(1)}, f32[8,8,256]{2,1,0:T(8,128)S(1)}, u32[]{:S(2)}, u32[]{:S(2)}) collective-permute-start(f32[8,8,256]{2,1,0:T(8,128)S(1)} %get-tuple-element.12), channel_id=1, source_target_pairs={{0,8},{4,12},{8,0},{12,4},{1,9},{5,13},{9,1},{13,5},{2,10},{6,14},... | collective-permute-start | bytes 196616 | tf_op jit(solution)/shard_map/ppermute | solution.py:278
  4.6 15.2 %copy-start.2 = (s32[8]{0:T(128)S(1)}, s32[8]{0:T(128)}, u32[]{:S(2)}) copy-start(s32[8]{0:T(128)} %offsets.3) | copy-start | bytes 100
  4.7 7.1 %collective-permute-start.5 = (f32[8,16,128]{2,1,0:T(8,128)S(1)}, f32[8,16,128]{2,1,0:T(8,128)S(1)}, u32[]{:S(2)}, u32[]{:S(2)}) collective-permute-start(f32[8,16,128]{2,1,0:T(8,128)S(1)} %get-tuple-element.19), channel_id=1, source_target_pairs={{0,9},{1,8},{2,11},{3,10},{4,12},{5,14},{6,13},{7,15},{8,1},{9,0},... | collective-permute-start | bytes 196616 | tf_op jit(solution)/shard_map/ppermute | solution.py:294
  6.2 6.1 %collective-permute-start.3 = (f32[8,16,128]{2,1,0:T(8,128)S(1)}, f32[8,16,128]{2,1,0:T(8,128)S(1)}, u32[]{:S(2)}, u32[]{:S(2)}) collective-permute-start(f32[8,16,128]{2,1,0:T(8,128)S(1)} %get-tuple-element.20), channel_id=1, source_target_pairs={{0,1},{1,0},{2,3},{3,2},{4,4},{5,6},{6,5},{7,7},{8,9},{9,8},{10,11... | collective-permute-start | bytes 196616 | tf_op jit(solution)/shard_map/ppermute | solution.py:293
  8.2 6.6 %collective-permute-start.9 = (f32[16,8,256]{2,1,0:T(8,128)}, f32[16,8,256]{2,1,0:T(8,128)S(1)}, u32[]{:S(2)}, u32[]{:S(2)}) collective-permute-start(f32[16,8,256]{2,1,0:T(8,128)} %o_own.1), channel_id=1, source_target_pairs={{0,24},{4,28},{8,16},{12,20},{16,8},{20,12},{24,0},{28,4},{1,25},{... | collective-permute-start | bytes 393224 | tf_op jit(solution)/shard_map/ppermute | solution.py:274
  11.1 5.2 %collective-permute-start.8 = (f32[16,8,256]{2,1,0:T(8,128)}, f32[16,8,256]{2,1,0:T(8,128)S(1)}, u32[]{:S(2)}, u32[]{:S(2)}) collective-permute-start(f32[16,8,256]{2,1,0:T(8,128)} %o_own.1), channel_id=1, source_target_pairs={{0,8},{4,12},{8,0},{12,4},{1,9},{5,13},{9,1},{13,5},{2,10},{6,14},... | collective-permute-start | bytes 393224 | tf_op jit(solution)/shard_map/ppermute | solution.py:275
  11.6 5.2 %collective-permute-start.7 = (f32[16,8,256]{2,1,0:T(8,128)}, f32[16,8,256]{2,1,0:T(8,128)S(1)}, u32[]{:S(2)}, u32[]{:S(2)}) collective-permute-start(f32[16,8,256]{2,1,0:T(8,128)} %o_own.1), channel_id=1, source_target_pairs={{0,16},{16,0},{1,17},{17,1},{2,18},{18,2},{3,19},{19,3},{4,20},{20... | collective-permute-start | bytes 393224 | tf_op jit(solution)/shard_map/ppermute | solution.py:280
  11.8 5.0 %collective-permute-start.6 = (f32[8,16,128]{2,1,0:T(8,128)S(1)}, f32[8,16,128]{2,1,0:T(8,128)S(1)}, u32[]{:S(2)}, u32[]{:S(2)}) collective-permute-start(f32[8,16,128]{2,1,0:T(8,128)S(1)} %collective-permute-done.5), channel_id=1, source_target_pairs={{0,4},{4,0},{8,12},{12,8},{1,5},{5,1},{9,13},{13,9},{2,6},{6,2},{1... | collective-permute-start | bytes 196616 | tf_op jit(solution)/shard_map/ppermute | solution.py:268
  12.4 4.9 %collective-permute-start.4 = (f32[8,16,128]{2,1,0:T(8,128)S(1)}, f32[8,16,128]{2,1,0:T(8,128)S(1)}, u32[]{:S(2)}, u32[]{:S(2)}) collective-permute-start(f32[8,16,128]{2,1,0:T(8,128)S(1)} %collective-permute-done.3), channel_id=1, source_target_pairs={{0,4},{4,0},{8,12},{12,8},{1,5},{5,1},{9,13},{13,9},{2,6},{6,2},{1... | collective-permute-start | bytes 196616 | tf_op jit(solution)/shard_map/ppermute | solution.py:268
  14.9 4.1 %collective-permute-start.10 = (f32[16,8,256]{2,1,0:T(8,128)}, f32[16,8,256]{2,1,0:T(8,128)S(1)}, u32[]{:S(2)}, u32[]{:S(2)}) collective-permute-start(f32[16,8,256]{2,1,0:T(8,128)} %o_own.1), channel_id=1, source_target_pairs={{0,4},{4,0},{8,12},{12,8},{1,5},{5,1},{9,13},{13,9},{2,6},{6,2},{1... | collective-permute-start | bytes 393224 | tf_op jit(solution)/shard_map/ppermute | solution.py:268
  16.3 1.3 %collective-permute-start.2 = (f32[8,8,256]{2,1,0:T(8,128)S(1)}, f32[8,8,256]{2,1,0:T(8,128)S(1)}, u32[]{:S(2)}, u32[]{:S(2)}) collective-permute-start(f32[8,8,256]{2,1,0:T(8,128)S(1)} %collective-permute-done.1.v_far), channel_id=1, source_target_pairs={{0,4},{4,0},{8,12},{12,8},{1,5},{5,1},{9,13},{13,9},{2,6},{6,2},{1... | collective-permute-start | bytes 196616 | tf_op jit(solution)/shard_map/ppermute | solution.py:268
  16.8 2.2 %collective-permute-start.13 = (f32[16,8,256]{2,1,0:T(8,128)S(1)}, f32[16,8,256]{2,1,0:T(8,128)S(1)}, u32[]{:S(2)}, u32[]{:S(2)}) collective-permute-start(f32[16,8,256]{2,1,0:T(8,128)S(1)} %collective-permute-done.9.u_far), channel_id=1, source_target_pairs={{0,4},{4,0},{8,12},{12,8},{1,5},{5,1},{9,13},{13,9},{2,6},{6,2},{1... | collective-permute-start | bytes 393224 | tf_op jit(solution)/shard_map/ppermute | solution.py:268
  16.8 2.2 %collective-permute-start.12 = (f32[16,8,256]{2,1,0:T(8,128)S(1)}, f32[16,8,256]{2,1,0:T(8,128)S(1)}, u32[]{:S(2)}, u32[]{:S(2)}) collective-permute-start(f32[16,8,256]{2,1,0:T(8,128)S(1)} %collective-permute-done.8.o_far), channel_id=1, source_target_pairs={{0,4},{4,0},{8,12},{12,8},{1,5},{5,1},{9,13},{13,9},{2,6},{6,2},{1... | collective-permute-start | bytes 393224 | tf_op jit(solution)/shard_map/ppermute | solution.py:268
  17.3 1.7 %collective-permute-start.11 = (f32[16,8,256]{2,1,0:T(8,128)S(1)}, f32[16,8,256]{2,1,0:T(8,128)S(1)}, u32[]{:S(2)}, u32[]{:S(2)}) collective-permute-start(f32[16,8,256]{2,1,0:T(8,128)S(1)} %collective-permute-done.7.u_own), channel_id=1, source_target_pairs={{0,4},{4,0},{8,12},{12,8},{1,5},{5,1},{9,13},{13,9},{2,6},{6,2},{1... | collective-permute-start | bytes 393224 | tf_op jit(solution)/shard_map/ppermute | solution.py:268
  22.0 6.6 %collective-permute-start.14 = (f32[2,40,256]{2,1,0:T(8,128)S(1)}, f32[2,40,256]{2,1,0:T(8,128)S(1)}, u32[]{:S(2)}, u32[]{:S(2)}) collective-permute-start(f32[2,40,256]{2,1,0:T(8,128)S(1)} %shard_map.42), channel_id=1, source_target_pairs={{0,1},{1,0},{2,3},{3,2},{4,5},{5,4},{6,7},{7,6},{8,9},{9,8},{10,11... | collective-permute-start | bytes 245768 | tf_op jit(solution)/shard_map/ppermute | solution.py:312
  28.6 5.4 %collective-permute-start.15 = (f32[40,256]{1,0:T(8,128)S(1)}, f32[40,256]{1,0:T(8,128)S(1)}, u32[]{:S(2)}, u32[]{:S(2)}) collective-permute-start(f32[40,256]{1,0:T(8,128)S(1)} %fusion.2), channel_id=1, source_target_pairs={{0,2},{1,3},{2,0},{3,1},{4,6},{5,7},{6,4},{7,5},{8,10},{9,11},{10,... | collective-permute-start | bytes 122888 | tf_op jit(solution)/shard_map/ppermute | solution.py:314

commit v3 on v2

--- a/solution.py
+++ b/solution.py
@@ -16,6 +16,11 @@
 F32 = jnp.float32
 
 
+def position():
+    az, ta = lax.axis_index("az"), lax.axis_index("ta")
+    return az, lax.rem(az, 2), lax.div(az, 2), ta
+
+
 def split(x):
     high = x.astype(BF16)
     return high, (x - high.astype(F32)).astype(BF16)
@@ -27,24 +32,54 @@
     return jnp.concatenate([first, second], axis=0)
 
 
-def fetch_kernel(info, velocity, out, part):
+def fetch_kernel(velocity, v_sib, out, part, ends_near, ends_away):
     half = part.shape[0]
+    _, core, row_y, ta = position()
+    right = lax.rem(ta + core, 2) == 0
+    times = velocity.shape[2]
     for i in range(half):
-        part[i] = velocity[(1 - info[1]) * half + i]
+        part[i] = velocity[(1 - row_y) * half + i]
     out[...] = velocity[...]
-
-
-def lag_kernel(flip, info, v_own, v_sib, v_far, v_far_sib, h_near, h_away, out):
-    core, row_y = info[0], info[1]
+    lane = lax.broadcasted_iota(jnp.int32, ends_near.shape, 1) // MAXLAG
+    for ends, first in ((ends_near, row_y * half), (ends_away, (1 - row_y) * half)):
+        acc = jnp.zeros(ends.shape, F32)
+        for j in range(half):
+            def tile(lo):
+                return in_core_order(core, velocity[first + j, :, lo : lo + LANES], v_sib[first + j, :, lo : lo + LANES])
+
+            edge = jnp.where(right, pltpu.roll(tile(times - LANES), MAXLAG, 1), tile(0))
+            edge = pltpu.roll(edge, MAXLAG * j, 1) if j else edge
+            acc = jnp.where(lane == j, edge, acc)
+        ends[...] = acc
+
+
+def halo_tile(station, mine, other):
+    _, core, _, ta = position()
+    swap = lax.rem(ta + core, 2) == 0
+    last = lax.axis_size("ta") - 1
+    before = jnp.where(swap, other, mine) * jnp.where(ta == 0, 0.0, 1.0).astype(F32)
+    after = jnp.where(swap, mine, other) * jnp.where(ta == last, 0.0, 1.0).astype(F32)
+    start = lax.rem(LANES - MAXLAG * station, LANES)
+    after = pltpu.roll(after, start, 1)
+    before = pltpu.roll(before, lax.rem(start + LANES - MAXLAG, LANES), 1)
+    lane = lax.broadcasted_iota(jnp.int32, after.shape, 1)
+    return jnp.where(lane < LANES // 2, after, before)
+
+
+def lag_kernel(flip, v_own, v_sib, v_far, v_far_sib, halos, halos_sib, out):
+    az, core, row_y, place = position()
     rows, times = v_own.shape[1:]
+    mine = v_own.shape[0] // lax.axis_size("az")
     width = times + LANES
     for i in range(out.shape[0]):
-        station = info[2] ^ (flip + 2 * i)
-        near = (v_own, v_sib, h_near, info[3] + station, row_y)
-        away = (v_far, v_far_sib, h_away, info[4] + station, 1 - row_y)
-        for v_a, v_b, h, at_v, place in (near, away):
+        station = place ^ (flip + 2 * i)
+        in_chip = mine * core + station
+        near = (v_own, v_sib, mine * az + station, row_y)
+        away = (v_far, v_far_sib, in_chip, 1 - row_y)
+        for which, (v_a, v_b, at_v, at) in enumerate((near, away)):
             series = in_core_order(core, v_a[at_v], v_b[at_v])
-            series = jnp.concatenate([series, h[info[4] + station]], axis=1)
+            edges = halo_tile(in_chip, halos[which], halos_sib[which])
+            series = jnp.concatenate([series, edges], axis=1)
             for b in range(2 * rows):
                 line = jnp.broadcast_to(series[b : b + 1, :], (8, width))
                 for half in range(MAIN // 16):
@@ -53,13 +88,13 @@
                         for g in (2 * half, 2 * half + 1)
                     ]
                     high, low = split(jnp.concatenate(parts, axis=0))
-                    at = b * MAIN + 16 * half
-                    out[i, 0, place, at : at + 16, :] = high
-                    out[i, 1, place, at : at + 16, :] = low
+                    row = b * MAIN + 16 * half
+                    out[i, 0, at, row : row + 16, :] = high
+                    out[i, 1, at, row : row + 16, :] = low
             high, low = split(pltpu.roll(series, MAXLAG, 1)[:, :times])
-            at = 2 * rows * MAIN
-            out[i, 0, place, at : at + 2 * rows, :] = high
-            out[i, 1, place, at : at + 2 * rows, :] = low
+            row = 2 * rows * MAIN
+            out[i, 0, at, row : row + 2 * rows, :] = high
+            out[i, 1, at, row : row + 2 * rows, :] = low
 
 
 def turn(x, by, azim):
@@ -69,11 +104,12 @@
     return jnp.where(lane < azim - by, left, right)
 
 
-def window_kernel(info, o_own, u_own, o_far, u_far, o_sib, u_sib, o_far_sib, u_far_sib, high_p, low_p):
-    core, row_y, last_gx = info[0], info[1], info[5]
+def window_kernel(o_own, u_own, o_far, u_far, o_sib, u_sib, o_far_sib, u_far_sib, high_p, low_p):
+    _, core, row_y, _ = position()
+    last_gx = lax.axis_index("gx") == lax.axis_size("gx") - 1
     half = o_own.shape[0] // 2
-    keep_up = jnp.where(last_gx == 1, 0.0, 1.0).astype(F32)
-    keep_mid = jnp.where((last_gx == 1) & (row_y == 1), 0.0, 1.0).astype(F32)
+    keep_up = jnp.where(last_gx, 0.0, 1.0).astype(F32)
+    keep_mid = jnp.where(last_gx & (row_y == 1), 0.0, 1.0).astype(F32)
     near = (o_own, u_own, o_sib, u_sib, row_y)
     away = (o_far, u_far, o_far_sib, u_far_sib, 1 - row_y)
 
@@ -96,11 +132,11 @@
     lax.fori_loop(0, half, one, 0)
 
 
-def product_kernel(flip, info, offsets, lags, high_p, low_p, out, prod):
-    core, place = info[0], info[2]
+def product_kernel(flip, offsets, lags, high_p, low_p, out, prod):
+    _, core, _, place = position()
     half = high_p.shape[0] // 3
     rows, azim = high_p.shape[2] // 2, 2 * high_p.shape[2]
-    count = offsets.shape[0]
+    count = offsets.shape[1]
     for i in range(out.shape[0]):
         station = place ^ (flip + 2 * i)
         first = (half // 2) * core + station
@@ -108,7 +144,7 @@
         for turned in (0, 1):
             tiles = {0: [], 1: []}
             for k in range(count):
-                w = first + offsets[k]
+                w = first + offsets[0, k]
                 for which, source in ((0, high_p), (1, low_p)):
                     tiles[which] += [source[w, turned], source[w, 1 - turned]]
             high = jnp.concatenate(tiles[0], axis=0)
@@ -169,56 +205,56 @@
 
 
 VMEM = pl.BlockSpec(memory_space=pltpu.VMEM)
-SMEM = pl.BlockSpec(memory_space=pltpu.SMEM)
-
-
-def fetch(info, velocity):
-    shape = velocity.shape
+
+
+def fetch(velocity, v_sib):
+    stations, rows, times = velocity.shape
+    shapes = [
+        (stations, rows, times), (stations // 2, rows, times),
+        (2 * rows, stations // 2 * MAXLAG), (2 * rows, stations // 2 * MAXLAG),
+    ]
     return pl.pallas_call(
         fetch_kernel,
-        in_specs=[SMEM, VMEM],
-        out_specs=[VMEM, VMEM],
-        out_shape=[
-            jax.ShapeDtypeStruct(shape, F32),
-            jax.ShapeDtypeStruct((shape[0] // 2,) + shape[1:], F32),
-        ],
+        in_specs=[VMEM, VMEM],
+        out_specs=[VMEM] * len(shapes),
+        out_shape=[jax.ShapeDtypeStruct(shape, F32) for shape in shapes],
         compiler_params=pltpu.CompilerParams(vmem_limit_bytes=2 << 20),
         cost_estimate=pl.CostEstimate(flops=0, bytes_accessed=1 << 19, transcendentals=0),
-    )(info, velocity)
-
-
-def lag_rows(flip, info, stations, *arrays):
+    )(velocity, v_sib)
+
+
+def lag_rows(flip, stations, *arrays):
     rows, times = arrays[0].shape[1:]
     shape = (stations, 2, 2, 2 * rows * (MAIN + 1), times)
     return pl.pallas_call(
         functools.partial(lag_kernel, flip),
-        in_specs=[SMEM] + [VMEM] * len(arrays),
+        in_specs=[VMEM] * len(arrays),
         out_specs=VMEM,
         out_shape=jax.ShapeDtypeStruct(shape, BF16),
         compiler_params=pltpu.CompilerParams(vmem_limit_bytes=12 << 20),
         cost_estimate=pl.CostEstimate(flops=10_000_000, bytes_accessed=3 << 20, transcendentals=0),
-    )(info, *arrays)
-
-
-def window(info, pieces):
+    )(*arrays)
+
+
+def window(pieces):
     stations, rows, times = pieces[0].shape
     shape = jax.ShapeDtypeStruct((stations // 2 * 3, 2, 2 * rows, times), BF16)
     return pl.pallas_call(
         window_kernel,
-        in_specs=[SMEM] + [VMEM] * len(pieces),
+        in_specs=[VMEM] * len(pieces),
         out_specs=[VMEM, VMEM],
         out_shape=[shape, shape],
         compiler_params=pltpu.CompilerParams(vmem_limit_bytes=8 << 20),
         cost_estimate=pl.CostEstimate(flops=2_000_000, bytes_accessed=2 << 20, transcendentals=0),
-    )(info, *pieces)
-
-
-def products(flip, info, offsets, lags, high_p, low_p):
+    )(*pieces)
+
+
+def products(flip, offsets, lags, high_p, low_p):
     stations, _, _, height, times = lags.shape
-    columns = offsets.shape[0] * 2 * high_p.shape[2]
+    columns = offsets.shape[1] * 2 * high_p.shape[2]
     return pl.pallas_call(
         functools.partial(product_kernel, flip),
-        in_specs=[SMEM, SMEM, VMEM, VMEM, VMEM],
+        in_specs=[VMEM] * 4,
         out_specs=VMEM,
         out_shape=jax.ShapeDtypeStruct((stations, MAIN + 8, columns), F32),
         scratch_shapes=[pltpu.VMEM((stations, height, columns), F32)],
@@ -227,7 +263,7 @@
             flops=2 * 3 * stations * 2 * height * times * columns,
             bytes_accessed=4 << 20, transcendentals=0,
         ),
-    )(info, offsets, lags, high_p, low_p)
+    )(offsets, lags, high_p, low_p)
 
 
 def close(parts, factor, count, azim):
@@ -244,10 +280,7 @@
 def shards(velocity, pressure, offsets):
     sta, rows, times = velocity.shape
     gx_n, az_n, ta_n = (lax.axis_size(name) for name in ("gx", "az", "ta"))
-    gx, az, ta = (lax.axis_index(name) for name in ("gx", "az", "ta"))
     assert az_n == 4 and ta_n == 4 and sta == az_n * ta_n
-    half, mine = sta // 2, sta // az_n
-    core, row_y = az % 2, az // 2
     azim = rows * az_n
     factor = 1.0 / math.sqrt(times * ta_n * azim)
 
@@ -267,52 +300,28 @@
 
     to_sibling = lambda x: lax.ppermute(x, "az", sibling)
 
-    info = jnp.stack([
-        core, row_y, ta, mine * az, mine * core, (gx == gx_n - 1).astype(jnp.int32),
-    ]).astype(jnp.int32)
-
+    far = lax.ppermute(pressure, "az", across)
+    up = lax.ppermute(pressure, "gx", upstream)
     diag = lax.ppermute(pressure, ("gx", "az"), diagonal)
-    far = lax.ppermute(pressure, "az", across)
-    vel, v_for = fetch(info, velocity)
-    v_sib = to_sibling(velocity)
+    v_sib, p_sib = to_sibling(velocity), to_sibling(pressure)
+    vel, v_for, ends_near, ends_away = fetch(velocity, v_sib)
+    ends_near, ends_away, p_sib = lax.optimization_barrier((ends_near, ends_away, p_sib))
     v_far = lax.ppermute(v_for, "az", across)
-    later, v_far = lax.optimization_barrier((pressure, v_far))
-    up = lax.ppermute(later, "gx", upstream)
-
-    even = ta % 2 == 0
-    use_right = even == (core == 0)
-
-    def edge(x):
-        return jnp.where(use_right, x[:, :, times - LANES :], x[:, :, :LANES])
-
-    edge_own, edge_sib = edge(vel), edge(v_sib)
-    first_core = jnp.where(core == 0, edge_own, edge_sib)
-    second_core = jnp.where(core == 0, edge_sib, edge_own)
-    edges = jnp.concatenate([first_core, second_core], axis=1)
-    ends = [lax.dynamic_slice_in_dim(edges, half * at, half, 0) for at in (row_y, 1 - row_y)]
-    h_near = lax.ppermute(ends[0], ("az", "ta"), in_time)
-    h_away = lax.ppermute(ends[1], ("az", "ta"), in_time_across)
-
-    def halo(mine, other):
-        got_a = jnp.where(core == 0, mine, other)
-        got_b = jnp.where(core == 0, other, mine)
-        before = jnp.where(even, got_b, got_a) * (ta > 0).astype(F32)
-        after = jnp.where(even, got_a, got_b) * (ta < ta_n - 1).astype(F32)
-        lane = lax.broadcasted_iota(jnp.int32, before.shape, before.ndim - 1)
-        return jnp.where(lane < LANES // 2, after, before)
-
-    v_far_sib = to_sibling(v_far)
-    series = (vel, v_sib, v_far, v_far_sib, halo(h_near, to_sibling(h_near)), halo(h_away, to_sibling(h_away)))
-    lags_give = lag_rows(1, info, ta_n // 2, *series)
-    p_sib, up_sib, diag_sib, far_sib = (to_sibling(x) for x in (pressure, up, diag, far))
-    lags_keep = lag_rows(0, info, ta_n // 2, *series)
-    high_p, low_p = window(info, [pressure, up, far, diag, p_sib, up_sib, far_sib, diag_sib])
-
-    give = products(1, info, offsets, lags_give, high_p, low_p)
+    h_near = lax.ppermute(ends_near, ("az", "ta"), in_time)
+    h_away = lax.ppermute(ends_away, ("az", "ta"), in_time_across)
+
+    h_away, h_near, diag, up, far = lax.optimization_barrier((h_away, h_near, diag, up, far))
+    halos = jnp.stack([h_near, h_away])
+    halos_sib = to_sibling(halos)
+    up_sib, diag_sib, far_sib = (to_sibling(x) for x in (up, diag, far))
+    series = (vel, v_sib, v_far, to_sibling(v_far), halos, halos_sib)
+    high_p, low_p = window([pressure, up, far, diag, p_sib, up_sib, far_sib, diag_sib])
+    offsets = offsets.reshape(1, -1)
+    give = products(1, offsets, lag_rows(1, ta_n // 2, *series), high_p, low_p)
     first = lax.ppermute(give, "ta", [(i, i ^ 1) for i in range(ta_n)])
-    keep = products(0, info, offsets, lags_keep, high_p, low_p)
+    keep = products(0, offsets, lag_rows(0, ta_n // 2, *series), high_p, low_p)
     second = lax.ppermute(keep[1] + first[1], "ta", [(i, i ^ 2) for i in range(ta_n)])
-    return close([keep, first, second], factor, offsets.shape[0], azim)
+    return close([keep, first, second], factor, offsets.shape[1], azim)
 
 
 def solution(mesh):

time: 35 us -> 31.2 us (0.89)
  Pallas kernels: 9.28 us -> 6.82 us
  starting transfers between devices: 15.6 us -> 14.4 us
    ppermute x1, starting transfers between devices: 3 us -> 0.17 us  [shards(): first = lax.ppermute(give, 'ta', [(i, i ^ 1) for i in range(ta_n)])]
    ppermute x3, starting transfers between devices: 3.73 us -> 6.47 us  [the longest x1 2.94 us: shards(): up = lax.ppermute(pressure, 'gx', upstream)]
    ppermute x1, waiting for transfers between devices: 2.47 us -> 0.01 us  [shards(): diag = lax.ppermute(pressure, ('gx', 'az'), diagonal)]
    pallas_call x6, Pallas kernels: 8.49 us -> 6.03 us  [the longest x2 3.34 us: products(): pl.pallas_call(functools.partial(product_kernel, flip), in_specs=[VMEM] *...]
    ppermute x1, waiting for transfers between devices: 0.01 us -> 1.58 us  [shards(): first = lax.ppermute(give, 'ta', [(i, i ^ 1) for i in range(ta_n)])]
    ppermute x1, starting transfers between devices: 2.88 us -> 1.49 us  [shards(): diag = lax.ppermute(pressure, ('gx', 'az'), diagonal)]
    ppermute x8 -> x7, waiting for transfers between devices: 0.14 us -> 1.13 us  [shards(): to_sibling = lambda x: lax.ppermute(x, 'az', sibling)]
    ppermute x1, waiting for transfers between devices: 3.51 us -> 2.61 us  [shards(): lax.ppermute(keep[1] + first[1], 'ta', [(i, i ^ 2) for i in range(ta_n)])]
  transfers between devices with their start and end apart: 16 -> 15, of which waited for: 6 -> 5; matrix products, arithmetic and copies ran while one was open for 0% -> 0% of each run, Pallas kernels for 16% -> 13%
where the time goes in v3:
time: 31.2 us; the launch traced here: 31.1 us
  starting transfers between devices  14.4 us (46%)
  waiting for transfers between devices  8.83 us (28%)
  Pallas kernels  6.82 us (22%)
  local copies, waits for them, and re-layouts  0.91 us (3%)
    pallas_call x2, Pallas kernels, products(): pl.pallas_call(functools.partial(product_kernel, flip), in_specs=[VMEM] *...  3.34 us
    ppermute x1, starting transfers between devices, shards(): up = lax.ppermute(pressure, 'gx', upstream)  2.94 us
    ppermute x1, waiting for transfers between devices, shards(): lax.ppermute(keep[1] + first[1], 'ta', [(i, i ^ 2) for i in range(ta_n)])  2.61 us
    ppermute x1, starting transfers between devices, shards(): lax.ppermute(keep[1] + first[1], 'ta', [(i, i ^ 2) for i in range(ta_n)])  2.59 us
    pallas_call x2, Pallas kernels, lag_rows(): pl.pallas_call(functools.partial(lag_kernel, flip), in_specs=[VMEM] * len...  2.29 us
    ppermute x1, starting transfers between devices, shards(): v_far = lax.ppermute(v_for, 'az', across)  2.06 us
    ppermute x1, waiting for transfers between devices, shards(): far = lax.ppermute(pressure, 'az', across)  2.01 us
    ppermute x1, starting transfers between devices, shards(): h_near = lax.ppermute(ends_near, ('az', 'ta'), in_time)  2.01 us
  transfers between devices with their start and end apart: 15, of which 5 were waited for; matrix products, arithmetic and copies ran while one was open for 0% of the time, Pallas kernels for 13%

profile of v3, /device:TPU:0, one launch (start us, length us, event | category | flops | bytes accessed | tf_op | source)
XLA Modules:
  0.0 31.1 jit_solution(18261395645910500532)
XLA Ops:
  0.0 0.5 %collective-permute-start = (f32[16,8,256]{2,1,0:T(8,128)}, f32[16,8,256]{2,1,0:T(8,128)S(1)}, u32[]{:S(2)}, u32[]{:S(2)}) collective-permute-start(f32[16,8,256]{2,1,0:T(8,128)} %velocity.1), channel_id=1, source_target_pairs={{0,4},{4,0},{8,12},{12,8},{1,5},{5,1},{9,13},{13,9},{2,6},{6,2},{1... | collective-permute-start | bytes 393224 | tf_op jit(solution)/shard_map/ppermute | solution.py:301
  0.5 0.1 collective-permute-start.3
  0.5 2.9 %collective-permute-start.7 = (f32[16,8,256]{2,1,0:T(8,128)}, f32[16,8,256]{2,1,0:T(8,128)S(1)}, u32[]{:S(2)}, u32[]{:S(2)}) collective-permute-start(f32[16,8,256]{2,1,0:T(8,128)} %o_own.1), channel_id=1, source_target_pairs={{0,16},{16,0},{1,17},{17,1},{2,18},{18,2},{3,19},{19,3},{4,20},{20... | collective-permute-start | bytes 393224 | tf_op jit(solution)/shard_map/ppermute | solution.py:304
  3.5 1.5 %collective-permute-start.6 = (f32[16,8,256]{2,1,0:T(8,128)}, f32[16,8,256]{2,1,0:T(8,128)S(1)}, u32[]{:S(2)}, u32[]{:S(2)}) collective-permute-start(f32[16,8,256]{2,1,0:T(8,128)} %o_own.1), channel_id=1, source_target_pairs={{0,24},{4,28},{8,16},{12,20},{16,8},{20,12},{24,0},{28,4},{1,25},{... | collective-permute-start | bytes 393224 | tf_op jit(solution)/shard_map/ppermute | solution.py:305
  4.9 0.0 collective-permute-start.8
  5.0 0.0 collective-permute-done.v_sib
  5.0 0.0 copy-start
  5.0 0.9 %copy-done = f32[16,8,256]{2,1,0:T(8,128)S(1)} copy-done((f32[16,8,256]{2,1,0:T(8,128)S(1)}, f32[16,8,256]{2,1,0:T(8,128)}, u32[]{:S(2)}) %copy-start) | copy-done | bytes 131096
  5.9 0.0 copy-start.1
  5.9 0.0 copy-start.2
  5.9 0.2 shard_map.37
  6.1 2.1 %collective-permute-start.1 = (f32[8,8,256]{2,1,0:T(8,128)S(1)}, f32[8,8,256]{2,1,0:T(8,128)S(1)}, u32[]{:S(2)}, u32[]{:S(2)}) collective-permute-start(f32[8,8,256]{2,1,0:T(8,128)S(1)} %get-tuple-element.20), channel_id=1, source_target_pairs={{0,8},{4,12},{8,0},{12,4},{1,9},{5,13},{9,1},{13,5},{2,10},{6,14},... | collective-permute-start | bytes 196616 | tf_op jit(solution)/shard_map/ppermute | solution.py:309
  8.1 0.0 collective-permute-done.3.o_sib
  8.1 1.5 %collective-permute-start.4 = (f32[16,128]{1,0:T(8,128)S(1)}, f32[16,128]{1,0:T(8,128)S(1)}, u32[]{:S(2)}, u32[]{:S(2)}) collective-permute-start(f32[16,128]{1,0:T(8,128)S(1)} %get-tuple-element.23), channel_id=1, source_target_pairs={{0,9},{1,8},{2,11},{3,10},{4,12},{5,14},{6,13},{7,15},{8,1},{9,0},... | collective-permute-start | bytes 24584 | tf_op jit(solution)/shard_map/ppermute | solution.py:311
  9.6 0.0 collective-permute-done.7.u_own
  9.6 2.0 %collective-permute-start.5 = (f32[16,128]{1,0:T(8,128)S(1)}, f32[16,128]{1,0:T(8,128)S(1)}, u32[]{:S(2)}, u32[]{:S(2)}) collective-permute-start(f32[16,128]{1,0:T(8,128)S(1)} %get-tuple-element.24), channel_id=1, source_target_pairs={{0,1},{1,0},{2,3},{3,2},{4,4},{5,6},{6,5},{7,7},{8,9},{9,8},{10,11... | collective-permute-start | bytes 24584 | tf_op jit(solution)/shard_map/ppermute | solution.py:310
  11.7 0.0 collective-permute-done.6.u_far
  11.7 2.0 %collective-permute-done.8.o_far = f32[16,8,256]{2,1,0:T(8,128)S(1)} collective-permute-done((f32[16,8,256]{2,1,0:T(8,128)}, f32[16,8,256]{2,1,0:T(8,128)S(1)}, u32[]{:S(2)}, u32[]{:S(2)}) %collective-permute-start.8) | collective-permute-done | bytes 131104 | tf_op jit(solution)/shard_map/ppermute | solution.py:303
  13.7 0.0 collective-permute-done.4
  13.7 1.5 %collective-permute-done.5 = f32[16,128]{1,0:T(8,128)S(1)} collective-permute-done((f32[16,128]{1,0:T(8,128)S(1)}, f32[16,128]{1,0:T(8,128)S(1)}, u32[]{:S(2)}, u32[]{:S(2)}) %collective-permute-start.5) | collective-permute-done | bytes 8224 | tf_op jit(solution)/shard_map/ppermute | solution.py:310
  15.2 0.0 collective-permute-start.10
  15.2 0.5 %collective-permute-start.11 = (f32[16,8,256]{2,1,0:T(8,128)S(1)}, f32[16,8,256]{2,1,0:T(8,128)S(1)}, u32[]{:S(2)}, u32[]{:S(2)}) collective-permute-start(f32[16,8,256]{2,1,0:T(8,128)S(1)} %collective-permute-done.8.o_far), channel_id=1, source_target_pairs={{0,4},{4,0},{8,12},{12,8},{1,5},{5,1},{9,13},{13,9},{2,6},{6,2},{1... | collective-permute-start | bytes 393224 | tf_op jit(solution)/shard_map/ppermute | solution.py:301
  15.7 0.0 collective-permute-start.12
  15.7 0.0 collective-permute-done.1.v_far
  15.7 0.5 %collective-permute-start.2 = (f32[8,8,256]{2,1,0:T(8,128)S(1)}, f32[8,8,256]{2,1,0:T(8,128)S(1)}, u32[]{:S(2)}, u32[]{:S(2)}) collective-permute-start(f32[8,8,256]{2,1,0:T(8,128)S(1)} %collective-permute-done.1.v_far), channel_id=1, source_target_pairs={{0,4},{4,0},{8,12},{12,8},{1,5},{5,1},{9,13},{13,9},{2,6},{6,2},{1... | collective-permute-start | bytes 196616 | tf_op jit(solution)/shard_map/ppermute | solution.py:301
  16.2 0.1 collective-permute-start.9
  16.3 1.1 %collective-permute-done.9.halos_sib = f32[2,16,128]{2,1,0:T(8,128)S(1)} collective-permute-done((f32[2,16,128]{2,1,0:T(8,128)S(1)}, f32[2,16,128]{2,1,0:T(8,128)S(1)}, u32[]{:S(2)}, u32[]{:S(2)}) %collective-permute-start.9) | collective-permute-done | bytes 16416 | tf_op jit(solution)/shard_map/ppermute | solution.py:301
  17.4 0.0 collective-permute-done.2.v_far_sib
  17.4 1.1 %shard_map.41.lags = bf16[2,2,2,528,256]{4,3,2,1,0:T(8,128)(2,1)S(1)} custom-call(f32[16,8,256]{2,1,0:T(8,128)S(1)} %get-tuple-element.19.v_own, f32[16,8,256]{2,1,0:T(8,128)S(1)} %collective-permute-done.v_sib, f32[8,8,256]{2,1,0:T(8,128)S(1)} %collective-permute-done.1.v_far, f32[8,8,256]{2,1,0:T(8,128)S(1)} %collective-permute-done.2.v_far_sib, ...), custom_call_target="tpu_custom_call" | custom-call | flops 10000000 | bytes 3145728 | tf_op jit(solution)/shard_map/pallas_call | solution.py:229
  18.6 0.0 collective-permute-done.10.u_sib
  18.6 0.0 collective-permute-done.11.o_far_sib
  18.6 0.0 collective-permute-done.12.u_far_sib
  18.6 0.0 copy-done.1
  18.6 0.2 shard_map.39
  18.8 0.0 copy-done.2
  18.8 1.7 %shard_map.42 = f32[2,40,256]{2,1,0:T(8,128)S(1)} custom-call(s32[1,8]{1,0:T(1,128)S(1)} %bitcast.5, bf16[2,2,2,528,256]{4,3,2,1,0:T(8,128)(2,1)S(1)} %shard_map.41.lags, bf16[24,2,16,256]{3,2,1,0:T(8,128)(2,1)S(1)} %get-tuple-element.31.high_p, bf16[24,2,16,256]{3,2,1,0:T(8,128)(2,1)S(1)} %get-tuple-element.32.low_p), custom_call_target="tpu_custom_call" | custom-call | flops 830472192 | bytes 4194304 | tf_op jit(solution)/shard_map/pallas_call | solution.py:255
  20.5 0.2 collective-permute-start.13
  20.7 1.1 %shard_map.38.lags = bf16[2,2,2,528,256]{4,3,2,1,0:T(8,128)(2,1)S(1)} custom-call(f32[16,8,256]{2,1,0:T(8,128)S(1)} %get-tuple-element.19.v_own, f32[16,8,256]{2,1,0:T(8,128)S(1)} %collective-permute-done.v_sib, f32[8,8,256]{2,1,0:T(8,128)S(1)} %collective-permute-done.1.v_far, f32[8,8,256]{2,1,0:T(8,128)S(1)} %collective-permute-done.2.v_far_sib, ...), custom_call_target="tpu_custom_call" | custom-call | flops 10000000 | bytes 3145728 | tf_op jit(solution)/shard_map/pallas_call | solution.py:229
  21.8 1.7 %shard_map.40.refs_0_ = f32[2,40,256]{2,1,0:T(8,128)S(1)} custom-call(s32[1,8]{1,0:T(1,128)S(1)} %bitcast.6, bf16[2,2,2,528,256]{4,3,2,1,0:T(8,128)(2,1)S(1)} %shard_map.38.lags, bf16[24,2,16,256]{3,2,1,0:T(8,128)(2,1)S(1)} %get-tuple-element.31.high_p, bf16[24,2,16,256]{3,2,1,0:T(8,128)(2,1)S(1)} %get-tuple-element.32.low_p), custom_call_target="tpu_custom_call" | custom-call | flops 830472192 | bytes 4194304 | tf_op jit(solution)/shard_map/pallas_call | solution.py:255
  23.5 1.6 %collective-permute-done.13.refs_1_ = f32[2,40,256]{2,1,0:T(8,128)S(1)} collective-permute-done((f32[2,40,256]{2,1,0:T(8,128)S(1)}, f32[2,40,256]{2,1,0:T(8,128)S(1)}, u32[]{:S(2)}, u32[]{:S(2)}) %collective-permute-start.13) | collective-permute-done | bytes 81952 | tf_op jit(solution)/shard_map/ppermute | solution.py:321
  25.1 2.6 %collective-permute-start.14 = (f32[40,256]{1,0:T(8,128)S(1)}, f32[40,256]{1,0:T(8,128)S(1)}, u32[]{:S(2)}, u32[]{:S(2)}) collective-permute-start(f32[40,256]{1,0:T(8,128)S(1)} %fusion), channel_id=1, source_target_pairs={{0,2},{1,3},{2,0},{3,1},{4,6},{5,7},{6,4},{7,5},{8,10},{9,11},{10,... | collective-permute-start | bytes 122888 | tf_op jit(solution)/shard_map/ppermute | solution.py:323
  27.7 2.6 %collective-permute-done.14.refs_2_ = f32[40,256]{1,0:T(8,128)S(1)} collective-permute-done((f32[40,256]{1,0:T(8,128)S(1)}, f32[40,256]{1,0:T(8,128)S(1)}, u32[]{:S(2)}, u32[]{:S(2)}) %collective-permute-start.14) | collective-permute-done | bytes 40992 | tf_op jit(solution)/shard_map/ppermute | solution.py:323
  30.3 0.8 %shard_map.43 = f32[1,8,1056]{2,1,0:T(8,128)} custom-call(f32[2,40,256]{2,1,0:T(8,128)S(1)} %shard_map.40.refs_0_, f32[2,40,256]{2,1,0:T(8,128)S(1)} %collective-permute-done.13.refs_1_, f32[40,256]{1,0:T(8,128)S(1)} %collective-permute-done.14.refs_2_), custom_call_target="tpu_custom_call" | custom-call | flops 1000000 | bytes 262144 | tf_op jit(solution)/shard_map/pallas_call | solution.py:270
  (2 shorter events, 0.0 us)
Async XLA Ops:
  0.0 5.0 %collective-permute-start = (f32[16,8,256]{2,1,0:T(8,128)}, f32[16,8,256]{2,1,0:T(8,128)S(1)}, u32[]{:S(2)}, u32[]{:S(2)}) collective-permute-start(f32[16,8,256]{2,1,0:T(8,128)} %velocity.1), channel_id=1, source_target_pairs={{0,4},{4,0},{8,12},{12,8},{1,5},{5,1},{9,13},{13,9},{2,6},{6,2},{1... | collective-permute-start | bytes 393224 | tf_op jit(solution)/shard_map/ppermute | solution.py:301
  0.5 7.7 %collective-permute-start.3 = (f32[16,8,256]{2,1,0:T(8,128)}, f32[16,8,256]{2,1,0:T(8,128)S(1)}, u32[]{:S(2)}, u32[]{:S(2)}) collective-permute-start(f32[16,8,256]{2,1,0:T(8,128)} %o_own.1), channel_id=1, source_target_pairs={{0,4},{4,0},{8,12},{12,8},{1,5},{5,1},{9,13},{13,9},{2,6},{6,2},{1... | collective-permute-start | bytes 393224 | tf_op jit(solution)/shard_map/ppermute | solution.py:301
  0.5 9.1 %collective-permute-start.7 = (f32[16,8,256]{2,1,0:T(8,128)}, f32[16,8,256]{2,1,0:T(8,128)S(1)}, u32[]{:S(2)}, u32[]{:S(2)}) collective-permute-start(f32[16,8,256]{2,1,0:T(8,128)} %o_own.1), channel_id=1, source_target_pairs={{0,16},{16,0},{1,17},{17,1},{2,18},{18,2},{3,19},{19,3},{4,20},{20... | collective-permute-start | bytes 393224 | tf_op jit(solution)/shard_map/ppermute | solution.py:304
  3.5 8.2 %collective-permute-start.6 = (f32[16,8,256]{2,1,0:T(8,128)}, f32[16,8,256]{2,1,0:T(8,128)S(1)}, u32[]{:S(2)}, u32[]{:S(2)}) collective-permute-start(f32[16,8,256]{2,1,0:T(8,128)} %o_own.1), channel_id=1, source_target_pairs={{0,24},{4,28},{8,16},{12,20},{16,8},{20,12},{24,0},{28,4},{1,25},{... | collective-permute-start | bytes 393224 | tf_op jit(solution)/shard_map/ppermute | solution.py:305
  4.9 8.7 %collective-permute-start.8 = (f32[16,8,256]{2,1,0:T(8,128)}, f32[16,8,256]{2,1,0:T(8,128)S(1)}, u32[]{:S(2)}, u32[]{:S(2)}) collective-permute-start(f32[16,8,256]{2,1,0:T(8,128)} %o_own.1), channel_id=1, source_target_pairs={{0,8},{4,12},{8,0},{12,4},{1,9},{5,13},{9,1},{13,5},{2,10},{6,14},... | collective-permute-start | bytes 393224 | tf_op jit(solution)/shard_map/ppermute | solution.py:303
  5.0 0.9 %copy-start = (f32[16,8,256]{2,1,0:T(8,128)S(1)}, f32[16,8,256]{2,1,0:T(8,128)}, u32[]{:S(2)}) copy-start(f32[16,8,256]{2,1,0:T(8,128)} %velocity.1) | copy-start | bytes 393220
  5.9 12.7 %copy-start.1 = (f32[16,8,256]{2,1,0:T(8,128)S(1)}, f32[16,8,256]{2,1,0:T(8,128)}, u32[]{:S(2)}) copy-start(f32[16,8,256]{2,1,0:T(8,128)} %o_own.1) | copy-start | bytes 393220
  5.9 12.9 %copy-start.2 = (s32[8]{0:T(128)S(1)}, s32[8]{0:T(128)}, u32[]{:S(2)}) copy-start(s32[8]{0:T(128)} %param.5) | copy-start | bytes 100
  6.1 9.6 %collective-permute-start.1 = (f32[8,8,256]{2,1,0:T(8,128)S(1)}, f32[8,8,256]{2,1,0:T(8,128)S(1)}, u32[]{:S(2)}, u32[]{:S(2)}) collective-permute-start(f32[8,8,256]{2,1,0:T(8,128)S(1)} %get-tuple-element.20), channel_id=1, source_target_pairs={{0,8},{4,12},{8,0},{12,4},{1,9},{5,13},{9,1},{13,5},{2,10},{6,14},... | collective-permute-start | bytes 196616 | tf_op jit(solution)/shard_map/ppermute | solution.py:309
  8.1 5.6 %collective-permute-start.4 = (f32[16,128]{1,0:T(8,128)S(1)}, f32[16,128]{1,0:T(8,128)S(1)}, u32[]{:S(2)}, u32[]{:S(2)}) collective-permute-start(f32[16,128]{1,0:T(8,128)S(1)} %get-tuple-element.23), channel_id=1, source_target_pairs={{0,9},{1,8},{2,11},{3,10},{4,12},{5,14},{6,13},{7,15},{8,1},{9,0},... | collective-permute-start | bytes 24584 | tf_op jit(solution)/shard_map/ppermute | solution.py:311
  9.6 5.5 %collective-permute-start.5 = (f32[16,128]{1,0:T(8,128)S(1)}, f32[16,128]{1,0:T(8,128)S(1)}, u32[]{:S(2)}, u32[]{:S(2)}) collective-permute-start(f32[16,128]{1,0:T(8,128)S(1)} %get-tuple-element.24), channel_id=1, source_target_pairs={{0,1},{1,0},{2,3},{3,2},{4,4},{5,6},{6,5},{7,7},{8,9},{9,8},{10,11... | collective-permute-start | bytes 24584 | tf_op jit(solution)/shard_map/ppermute | solution.py:310
  15.2 3.4 %collective-permute-start.10 = (f32[16,8,256]{2,1,0:T(8,128)S(1)}, f32[16,8,256]{2,1,0:T(8,128)S(1)}, u32[]{:S(2)}, u32[]{:S(2)}) collective-permute-start(f32[16,8,256]{2,1,0:T(8,128)S(1)} %collective-permute-done.7.u_own), channel_id=1, source_target_pairs={{0,4},{4,0},{8,12},{12,8},{1,5},{5,1},{9,13},{13,9},{2,6},{6,2},{1... | collective-permute-start | bytes 393224 | tf_op jit(solution)/shard_map/ppermute | solution.py:301
  15.2 3.4 %collective-permute-start.11 = (f32[16,8,256]{2,1,0:T(8,128)S(1)}, f32[16,8,256]{2,1,0:T(8,128)S(1)}, u32[]{:S(2)}, u32[]{:S(2)}) collective-permute-start(f32[16,8,256]{2,1,0:T(8,128)S(1)} %collective-permute-done.8.o_far), channel_id=1, source_target_pairs={{0,4},{4,0},{8,12},{12,8},{1,5},{5,1},{9,13},{13,9},{2,6},{6,2},{1... | collective-permute-start | bytes 393224 | tf_op jit(solution)/shard_map/ppermute | solution.py:301
  15.7 2.9 %collective-permute-start.12 = (f32[16,8,256]{2,1,0:T(8,128)S(1)}, f32[16,8,256]{2,1,0:T(8,128)S(1)}, u32[]{:S(2)}, u32[]{:S(2)}) collective-permute-start(f32[16,8,256]{2,1,0:T(8,128)S(1)} %collective-permute-done.6.u_far), channel_id=1, source_target_pairs={{0,4},{4,0},{8,12},{12,8},{1,5},{5,1},{9,13},{13,9},{2,6},{6,2},{1... | collective-permute-start | bytes 393224 | tf_op jit(solution)/shard_map/ppermute | solution.py:301
  15.7 1.7 %collective-permute-start.2 = (f32[8,8,256]{2,1,0:T(8,128)S(1)}, f32[8,8,256]{2,1,0:T(8,128)S(1)}, u32[]{:S(2)}, u32[]{:S(2)}) collective-permute-start(f32[8,8,256]{2,1,0:T(8,128)S(1)} %collective-permute-done.1.v_far), channel_id=1, source_target_pairs={{0,4},{4,0},{8,12},{12,8},{1,5},{5,1},{9,13},{13,9},{2,6},{6,2},{1... | collective-permute-start | bytes 196616 | tf_op jit(solution)/shard_map/ppermute | solution.py:301
  16.2 1.2 %collective-permute-start.9 = (f32[2,16,128]{2,1,0:T(8,128)S(1)}, f32[2,16,128]{2,1,0:T(8,128)S(1)}, u32[]{:S(2)}, u32[]{:S(2)}) collective-permute-start(f32[2,16,128]{2,1,0:T(8,128)S(1)} %pad_maximum_fusion.halos), channel_id=1, source_target_pairs={{0,4},{4,0},{8,12},{12,8},{1,5},{5,1},{9,13},{13,9},{2,6},{6,2},{1... | collective-permute-start | bytes 49160 | tf_op jit(solution)/shard_map/ppermute | solution.py:301
  20.5 4.6 %collective-permute-start.13 = (f32[2,40,256]{2,1,0:T(8,128)S(1)}, f32[2,40,256]{2,1,0:T(8,128)S(1)}, u32[]{:S(2)}, u32[]{:S(2)}) collective-permute-start(f32[2,40,256]{2,1,0:T(8,128)S(1)} %shard_map.42), channel_id=1, source_target_pairs={{0,1},{1,0},{2,3},{3,2},{4,5},{5,4},{6,7},{7,6},{8,9},{9,8},{10,11... | collective-permute-start | bytes 245768 | tf_op jit(solution)/shard_map/ppermute | solution.py:321
  25.1 5.2 %collective-permute-start.14 = (f32[40,256]{1,0:T(8,128)S(1)}, f32[40,256]{1,0:T(8,128)S(1)}, u32[]{:S(2)}, u32[]{:S(2)}) collective-permute-start(f32[40,256]{1,0:T(8,128)S(1)} %fusion), channel_id=1, source_target_pairs={{0,2},{1,3},{2,0},{3,1},{4,6},{5,7},{6,4},{7,5},{8,10},{9,11},{10,... | collective-permute-start | bytes 122888 | tf_op jit(solution)/shard_map/ppermute | solution.py:323

commit v4 on v3

--- a/solution.py
+++ b/solution.py
@@ -42,7 +42,7 @@
     out[...] = velocity[...]
     lane = lax.broadcasted_iota(jnp.int32, ends_near.shape, 1) // MAXLAG
     for ends, first in ((ends_near, row_y * half), (ends_away, (1 - row_y) * half)):
-        acc = jnp.zeros(ends.shape, F32)
+        acc = jnp.zeros(ends_near.shape, F32)
         for j in range(half):
             def tile(lo):
                 return in_core_order(core, velocity[first + j, :, lo : lo + LANES], v_sib[first + j, :, lo : lo + LANES])
@@ -66,42 +66,33 @@
     return jnp.where(lane < LANES // 2, after, before)
 
 
-def lag_kernel(flip, v_own, v_sib, v_far, v_far_sib, halos, halos_sib, out):
+def lag_kernel(flips, away, v_a, v_b, h_a, h_b, out):
     az, core, row_y, place = position()
-    rows, times = v_own.shape[1:]
-    mine = v_own.shape[0] // lax.axis_size("az")
+    rows, times = v_a.shape[1:]
+    mine = lax.axis_size("ta")
     width = times + LANES
     for i in range(out.shape[0]):
-        station = place ^ (flip + 2 * i)
+        station = i if flips is None else place ^ flips[i]
         in_chip = mine * core + station
-        near = (v_own, v_sib, mine * az + station, row_y)
-        away = (v_far, v_far_sib, in_chip, 1 - row_y)
-        for which, (v_a, v_b, at_v, at) in enumerate((near, away)):
-            series = in_core_order(core, v_a[at_v], v_b[at_v])
-            edges = halo_tile(in_chip, halos[which], halos_sib[which])
-            series = jnp.concatenate([series, edges], axis=1)
-            for b in range(2 * rows):
-                line = jnp.broadcast_to(series[b : b + 1, :], (8, width))
-                for half in range(MAIN // 16):
-                    parts = [
-                        pltpu.roll(line, (8 * g - MAXLAG) % width, 1, stride=1, stride_axis=0)[:, :times]
-                        for g in (2 * half, 2 * half + 1)
-                    ]
-                    high, low = split(jnp.concatenate(parts, axis=0))
-                    row = b * MAIN + 16 * half
-                    out[i, 0, at, row : row + 16, :] = high
-                    out[i, 1, at, row : row + 16, :] = low
-            high, low = split(pltpu.roll(series, MAXLAG, 1)[:, :times])
-            row = 2 * rows * MAIN
-            out[i, 0, at, row : row + 2 * rows, :] = high
-            out[i, 1, at, row : row + 2 * rows, :] = low
-
-
-def turn(x, by, azim):
-    lane = lax.broadcasted_iota(jnp.int32, x.shape, 1) % azim
-    left = pltpu.roll(x, LANES - by, 1)
-    right = pltpu.roll(x, azim - by, 1)
-    return jnp.where(lane < azim - by, left, right)
+        at_v = in_chip if away else mine * az + station
+        series = in_core_order(core, v_a[at_v], v_b[at_v])
+        edges = halo_tile(in_chip, h_a[...], h_b[...])
+        series = jnp.concatenate([series, edges], axis=1)
+        for b in range(2 * rows):
+            line = jnp.broadcast_to(series[b : b + 1, :], (8, width))
+            for half in range(MAIN // 16):
+                parts = [
+                    pltpu.roll(line, (8 * g - MAXLAG) % width, 1, stride=1, stride_axis=0)[:, :times]
+                    for g in (2 * half, 2 * half + 1)
+                ]
+                high, low = split(jnp.concatenate(parts, axis=0))
+                row = b * MAIN + 16 * half
+                out[i, 0, row : row + 16, :] = high
+                out[i, 1, row : row + 16, :] = low
+        high, low = split(pltpu.roll(series, MAXLAG, 1)[:, :times])
+        row = 2 * rows * MAIN
+        out[i, 0, row : row + 2 * rows, :] = high
+        out[i, 1, row : row + 2 * rows, :] = low
 
 
 def window_kernel(o_own, u_own, o_far, u_far, o_sib, u_sib, o_far_sib, u_far_sib, high_p, low_p):
@@ -132,16 +123,16 @@
     lax.fori_loop(0, half, one, 0)
 
 
-def product_kernel(flip, offsets, lags, high_p, low_p, out, prod):
-    _, core, _, place = position()
+def product_kernel(flips, offsets, lags_near, lags_away, high_p, low_p, out, prod):
+    _, core, row_y, place = position()
     half = high_p.shape[0] // 3
     rows, azim = high_p.shape[2] // 2, 2 * high_p.shape[2]
     count = offsets.shape[1]
-    for i in range(out.shape[0]):
-        station = place ^ (flip + 2 * i)
+    for i, flip in enumerate(flips):
+        station = place ^ flip
         first = (half // 2) * core + station
         right = []
-        for turned in (0, 1):
+        for turned in (row_y, 1 - row_y):
             tiles = {0: [], 1: []}
             for k in range(count):
                 w = first + offsets[0, k]
@@ -152,29 +143,36 @@
             right += [high, low, high]
         right = jnp.concatenate(right, axis=1)
         left = []
-        for y in (0, 1):
-            left += [lags[i, 0, y], lags[i, 0, y], lags[i, 1, y]]
+        for lags, at in ((lags_near, station), (lags_away, i)):
+            left += [lags[at, 0], lags[at, 0], lags[at, 1]]
         left = jnp.concatenate(left, axis=1)
         prod[i] = lax.dot_general(left, right, (((1,), (1,)), ((), ())), preferred_element_type=F32)
         out[i] = diagonals(prod.at[i], rows, azim, count)
 
 
 def diagonals(prod, rows, azim, count):
+    lane = lax.broadcasted_iota(jnp.int32, (1, LANES), 1) % azim
     pieces = []
     for c in range(0, count * azim, LANES):
-        level = [prod[b * MAIN : (b + 1) * MAIN, c : c + LANES] for b in range(2 * rows)]
-        by = 1
-        while len(level) > 1:
-            level = [level[i] + turn(level[i + 1], by, azim) for i in range(0, len(level), 2)]
-            by *= 2
+        inside = prod[:MAIN, c : c + LANES]
+        beyond = jnp.zeros_like(inside)
+        for b in range(1, 2 * rows):
+            moved = pltpu.roll(prod[b * MAIN : (b + 1) * MAIN, c : c + LANES], LANES - b, 1)
+            inside += jnp.where(lane < azim - b, moved, 0.0)
+            beyond += jnp.where(lane < azim - b, 0.0, moved)
         extra = prod[2 * rows * MAIN : 2 * rows * (MAIN + 1), c : c + LANES]
         row = lax.broadcasted_iota(jnp.int32, extra.shape, 0)
-        by = 1
+        moved, by = extra, 1
         while by < 2 * rows:
-            extra = jnp.where((row & by) != 0, turn(extra, by, azim), extra)
+            moved = jnp.where((row & by) != 0, pltpu.roll(moved, LANES - by, 1), moved)
             by *= 2
-        tail = jnp.broadcast_to(jnp.sum(extra, axis=0, keepdims=True), (8, LANES))
-        pieces.append(jnp.concatenate([level[0], tail], axis=0))
+        ends = [
+            jnp.broadcast_to(jnp.sum(jnp.where(keep, moved, 0.0), axis=0, keepdims=True), (8, LANES))
+            for keep in (lane < azim - row, lane >= azim - row)
+        ]
+        inside = jnp.concatenate([inside, ends[0]], axis=0)
+        beyond = jnp.concatenate([beyond, ends[1]], axis=0)
+        pieces.append(inside + pltpu.roll(beyond, azim, 1))
     return jnp.concatenate(pieces, axis=1)
 
 
@@ -223,11 +221,12 @@
     )(velocity, v_sib)
 
 
-def lag_rows(flip, stations, *arrays):
+def lag_rows(flips, away, *arrays):
     rows, times = arrays[0].shape[1:]
-    shape = (stations, 2, 2, 2 * rows * (MAIN + 1), times)
-    return pl.pallas_call(
-        functools.partial(lag_kernel, flip),
+    stations = lax.axis_size("ta") if flips is None else len(flips)
+    shape = (stations, 2, 2 * rows * (MAIN + 1), times)
+    return pl.pallas_call(
+        functools.partial(lag_kernel, flips, away),
         in_specs=[VMEM] * len(arrays),
         out_specs=VMEM,
         out_shape=jax.ShapeDtypeStruct(shape, BF16),
@@ -249,12 +248,12 @@
     )(*pieces)
 
 
-def products(flip, offsets, lags, high_p, low_p):
-    stations, _, _, height, times = lags.shape
+def products(flips, offsets, near, away, high_p, low_p):
+    stations, _, height, times = away.shape
     columns = offsets.shape[1] * 2 * high_p.shape[2]
     return pl.pallas_call(
-        functools.partial(product_kernel, flip),
-        in_specs=[VMEM] * 4,
+        functools.partial(product_kernel, flips),
+        in_specs=[VMEM] * 5,
         out_specs=VMEM,
         out_shape=jax.ShapeDtypeStruct((stations, MAIN + 8, columns), F32),
         scratch_shapes=[pltpu.VMEM((stations, height, columns), F32)],
@@ -263,7 +262,7 @@
             flops=2 * 3 * stations * 2 * height * times * columns,
             bytes_accessed=4 << 20, transcendentals=0,
         ),
-    )(offsets, lags, high_p, low_p)
+    )(offsets, near, away, high_p, low_p)
 
 
 def close(parts, factor, count, azim):
@@ -309,17 +308,21 @@
     v_far = lax.ppermute(v_for, "az", across)
     h_near = lax.ppermute(ends_near, ("az", "ta"), in_time)
     h_away = lax.ppermute(ends_away, ("az", "ta"), in_time_across)
-
     h_away, h_near, diag, up, far = lax.optimization_barrier((h_away, h_near, diag, up, far))
-    halos = jnp.stack([h_near, h_away])
-    halos_sib = to_sibling(halos)
-    up_sib, diag_sib, far_sib = (to_sibling(x) for x in (up, diag, far))
-    series = (vel, v_sib, v_far, to_sibling(v_far), halos, halos_sib)
+    both = jnp.stack([h_near, h_away])
+    both_sib = to_sibling(both)
+    h_near_sib, h_away_sib = both_sib[0], both_sib[1]
+    up_sib, diag_sib, far_sib, v_far_sib = (to_sibling(x) for x in (up, diag, far, v_far))
+    near = lag_rows(None, False, vel, v_sib, h_near, h_near_sib)
     high_p, low_p = window([pressure, up, far, diag, p_sib, up_sib, far_sib, diag_sib])
+    series = (v_far, v_far_sib, h_away, h_away_sib)
+
     offsets = offsets.reshape(1, -1)
-    give = products(1, offsets, lag_rows(1, ta_n // 2, *series), high_p, low_p)
+    flips = (1, 3)
+    give = products(flips, offsets, near, lag_rows(flips, True, *series), high_p, low_p)
     first = lax.ppermute(give, "ta", [(i, i ^ 1) for i in range(ta_n)])
-    keep = products(0, offsets, lag_rows(0, ta_n // 2, *series), high_p, low_p)
+    flips = (0, 2)
+    keep = products(flips, offsets, near, lag_rows(flips, True, *series), high_p, low_p)
     second = lax.ppermute(keep[1] + first[1], "ta", [(i, i ^ 2) for i in range(ta_n)])
     return close([keep, first, second], factor, offsets.shape[1], azim)
 

time: 31.2 us -> 30.7 us (0.984)
  waiting for transfers between devices: 8.83 us -> 6.83 us
  starting transfers between devices: 14.4 us -> 15.8 us
    ppermute x1, starting transfers between devices: 1.49 us -> 3.89 us  [shards(): diag = lax.ppermute(pressure, ('gx', 'az'), diagonal)]
    ppermute x1, starting transfers between devices: 2.94 us -> 0.54 us  [shards(): up = lax.ppermute(pressure, 'gx', upstream)]
    ppermute x1, waiting for transfers between devices: 2.01 us -> 0.06 us  [shards(): far = lax.ppermute(pressure, 'az', across)]
    ppermute x1, starting transfers between devices: 2.06 us -> 0.2 us  [shards(): v_far = lax.ppermute(v_for, 'az', across)]
    ppermute x1, starting transfers between devices: 1.52 us -> 3.07 us  [shards(): h_away = lax.ppermute(ends_away, ('az', 'ta'), in_time_across)]
    ppermute x1, starting transfers between devices: 0.17 us -> 1.63 us  [shards(): first = lax.ppermute(give, 'ta', [(i, i ^ 1) for i in range(ta_n)])]
    ppermute x1, waiting for transfers between devices: 1.5 us -> 2.89 us  [shards(): h_near = lax.ppermute(ends_near, ('az', 'ta'), in_time)]
    ppermute x7, waiting for transfers between devices: 1.13 us -> 0.1 us  [shards(): to_sibling = lambda x: lax.ppermute(x, 'az', sibling)]
  transfers between devices with their start and end apart: 15 -> 15, of which waited for: 5 -> 6; matrix products, arithmetic and copies ran while one was open for 0% -> 0% of each run, Pallas kernels for 13% -> 13%
where the time goes in v4:
time: 30.7 us; the launch traced here: 30.5 us
  starting transfers between devices  15.8 us (51%)
  waiting for transfers between devices  6.83 us (22%)
  Pallas kernels  6.58 us (21%)
  local copies, waits for them, and re-layouts  1.12 us (4%)
    ppermute x1, starting transfers between devices, shards(): diag = lax.ppermute(pressure, ('gx', 'az'), diagonal)  3.89 us
    pallas_call x2, Pallas kernels, products(): pl.pallas_call(functools.partial(product_kernel, flips), in_specs=[VMEM]...  3.09 us
    ppermute x1, starting transfers between devices, shards(): h_away = lax.ppermute(ends_away, ('az', 'ta'), in_time_across)  3.07 us
    ppermute x1, waiting for transfers between devices, shards(): h_near = lax.ppermute(ends_near, ('az', 'ta'), in_time)  2.89 us
    ppermute x1, starting transfers between devices, shards(): lax.ppermute(keep[1] + first[1], 'ta', [(i, i ^ 2) for i in range(ta_n)])  2.59 us
    ppermute x1, waiting for transfers between devices, shards(): lax.ppermute(keep[1] + first[1], 'ta', [(i, i ^ 2) for i in range(ta_n)])  2.51 us
    ppermute x1, starting transfers between devices, shards(): h_near = lax.ppermute(ends_near, ('az', 'ta'), in_time)  2.35 us
    pallas_call x3, Pallas kernels, lag_rows(): pl.pallas_call(functools.partial(lag_kernel, flips, away), in_specs=[VMEM...  2.33 us
  transfers between devices with their start and end apart: 15, of which 6 were waited for; matrix products, arithmetic and copies ran while one was open for 0% of the time, Pallas kernels for 13%

profile of v4, /device:TPU:0, one launch (start us, length us, event | category | flops | bytes accessed | tf_op | source)
XLA Modules:
  0.0 30.5 jit_solution(15080844226885497914)
XLA Ops:
  0.0 0.5 %collective-permute-start = (f32[16,8,256]{2,1,0:T(8,128)}, f32[16,8,256]{2,1,0:T(8,128)S(1)}, u32[]{:S(2)}, u32[]{:S(2)}) collective-permute-start(f32[16,8,256]{2,1,0:T(8,128)} %velocity.1), channel_id=1, source_target_pairs={{0,4},{4,0},{8,12},{12,8},{1,5},{5,1},{9,13},{13,9},{2,6},{6,2},{1... | collective-permute-start | bytes 393224 | tf_op jit(solution)/shard_map/ppermute | solution.py:300
  0.5 0.1 collective-permute-start.1
  0.5 3.9 %collective-permute-start.4 = (f32[16,8,256]{2,1,0:T(8,128)}, f32[16,8,256]{2,1,0:T(8,128)S(1)}, u32[]{:S(2)}, u32[]{:S(2)}) collective-permute-start(f32[16,8,256]{2,1,0:T(8,128)} %o_own.1), channel_id=1, source_target_pairs={{0,24},{4,28},{8,16},{12,20},{16,8},{20,12},{24,0},{28,4},{1,25},{... | collective-permute-start | bytes 393224 | tf_op jit(solution)/shard_map/ppermute | solution.py:304
  4.4 0.5 %collective-permute-start.5 = (f32[16,8,256]{2,1,0:T(8,128)}, f32[16,8,256]{2,1,0:T(8,128)S(1)}, u32[]{:S(2)}, u32[]{:S(2)}) collective-permute-start(f32[16,8,256]{2,1,0:T(8,128)} %o_own.1), channel_id=1, source_target_pairs={{0,16},{16,0},{1,17},{17,1},{2,18},{18,2},{3,19},{19,3},{4,20},{20... | collective-permute-start | bytes 393224 | tf_op jit(solution)/shard_map/ppermute | solution.py:303
  4.9 0.0 collective-permute-start.6
  5.0 0.0 collective-permute-done.v_sib.v_b
  5.0 0.0 copy-start
  5.0 0.9 %copy-done = f32[16,8,256]{2,1,0:T(8,128)S(1)} copy-done((f32[16,8,256]{2,1,0:T(8,128)S(1)}, f32[16,8,256]{2,1,0:T(8,128)}, u32[]{:S(2)}) %copy-start) | copy-done | bytes 131096
  5.9 0.2 shard_map.37
  6.1 0.0 collective-permute-done.1.o_sib
  6.1 3.1 %collective-permute-start.2 = (f32[16,128]{1,0:T(8,128)S(1)}, f32[16,128]{1,0:T(8,128)S(1)}, u32[]{:S(2)}, u32[]{:S(2)}) collective-permute-start(f32[16,128]{1,0:T(8,128)S(1)} %get-tuple-element.22), channel_id=1, source_target_pairs={{0,9},{1,8},{2,11},{3,10},{4,12},{5,14},{6,13},{7,15},{8,1},{9,0},... | collective-permute-start | bytes 24584 | tf_op jit(solution)/shard_map/ppermute | solution.py:310
  9.1 2.3 %collective-permute-start.3 = (f32[16,128]{1,0:T(8,128)S(1)}, f32[16,128]{1,0:T(8,128)S(1)}, u32[]{:S(2)}, u32[]{:S(2)}) collective-permute-start(f32[16,128]{1,0:T(8,128)S(1)} %get-tuple-element.23), channel_id=1, source_target_pairs={{0,1},{1,0},{2,3},{3,2},{4,4},{5,6},{6,5},{7,7},{8,9},{9,8},{10,11... | collective-permute-start | bytes 24584 | tf_op jit(solution)/shard_map/ppermute | solution.py:309
  11.5 0.0 collective-permute-done.4.u_far
  11.5 0.2 collective-permute-start.8
  11.7 0.0 collective-permute-done.5.u_own
  11.7 0.1 collective-permute-done.6.o_far
  11.8 0.0 collective-permute-done.2.h_a
  11.8 2.9 %collective-permute-done.3.h_a = f32[16,128]{1,0:T(8,128)S(1)} collective-permute-done((f32[16,128]{1,0:T(8,128)S(1)}, f32[16,128]{1,0:T(8,128)S(1)}, u32[]{:S(2)}, u32[]{:S(2)}) %collective-permute-start.3) | collective-permute-done | bytes 8224 | tf_op jit(solution)/shard_map/ppermute | solution.py:309
  14.7 0.0 collective-permute-start.7
  14.7 0.5 %collective-permute-start.10 = (f32[16,8,256]{2,1,0:T(8,128)S(1)}, f32[16,8,256]{2,1,0:T(8,128)S(1)}, u32[]{:S(2)}, u32[]{:S(2)}) collective-permute-start(f32[16,8,256]{2,1,0:T(8,128)S(1)} %collective-permute-done.5.u_own), channel_id=1, source_target_pairs={{0,4},{4,0},{8,12},{12,8},{1,5},{5,1},{9,13},{13,9},{2,6},{6,2},{1... | collective-permute-start | bytes 393224 | tf_op jit(solution)/shard_map/ppermute | solution.py:300
  15.2 0.0 collective-permute-start.11
  15.2 0.5 %collective-permute-start.12 = (f32[16,8,256]{2,1,0:T(8,128)S(1)}, f32[16,8,256]{2,1,0:T(8,128)S(1)}, u32[]{:S(2)}, u32[]{:S(2)}) collective-permute-start(f32[16,8,256]{2,1,0:T(8,128)S(1)} %collective-permute-done.4.u_far), channel_id=1, source_target_pairs={{0,4},{4,0},{8,12},{12,8},{1,5},{5,1},{9,13},{13,9},{2,6},{6,2},{1... | collective-permute-start | bytes 393224 | tf_op jit(solution)/shard_map/ppermute | solution.py:300
  15.7 0.1 collective-permute-done.8.v_a
  15.8 0.0 collective-permute-start.9
  15.8 0.0 collective-permute-done.7
  15.9 1.1 %shard_map.38.lags_near = bf16[4,2,528,256]{3,2,1,0:T(8,128)(2,1)S(1)} custom-call(f32[16,8,256]{2,1,0:T(8,128)S(1)} %get-tuple-element.19.v_a, f32[16,8,256]{2,1,0:T(8,128)S(1)} %collective-permute-done.v_sib.v_b, f32[16,128]{1,0:T(8,128)S(1)} %collective-permute-done.3.h_a, f32[16,128]{1,0:T(8,128)S(1)} %get-tuple-element.34.h_b), custom_call_target="tpu_custom_call" | custom-call | flops 10000000 | bytes 3145728 | tf_op jit(solution)/shard_map/pallas_call | solution.py:228
  17.0 0.0 copy-start.1
  17.0 0.1 collective-permute-done.9.v_b
  17.1 0.0 copy-start.2
  17.1 0.6 %shard_map.42.lags_away = bf16[2,2,528,256]{3,2,1,0:T(8,128)(2,1)S(1)} custom-call(f32[8,8,256]{2,1,0:T(8,128)S(1)} %collective-permute-done.8.v_a, f32[8,8,256]{2,1,0:T(8,128)S(1)} %collective-permute-done.9.v_b, f32[16,128]{1,0:T(8,128)S(1)} %collective-permute-done.2.h_a, f32[16,128]{1,0:T(8,128)S(1)} %get-tuple-element.33.h_b), custom_call_target="tpu_custom_call" | custom-call | flops 10000000 | bytes 3145728 | tf_op jit(solution)/shard_map/pallas_call | solution.py:228
  17.7 0.0 collective-permute-done.10.u_sib
  17.7 0.0 collective-permute-done.11.o_far_sib
  17.7 0.0 collective-permute-done.12.u_far_sib
  17.7 0.2 copy-done.1
  17.9 0.2 shard_map.40
  18.1 0.0 copy-done.2
  18.1 1.5 %shard_map.43 = f32[2,40,256]{2,1,0:T(8,128)S(1)} custom-call(s32[1,8]{1,0:T(1,128)S(1)} %bitcast.11, bf16[4,2,528,256]{3,2,1,0:T(8,128)(2,1)S(1)} %shard_map.38.lags_near, bf16[2,2,528,256]{3,2,1,0:T(8,128)(2,1)S(1)} %shard_map.42.lags_away, bf16[24,2,16,256]{3,2,1,0:T(8,128)(2,1)S(1)} %get-tuple-element.31.high_p, ...), custom_call_target="tpu_custom_call" | custom-call | flops 830472192 | bytes 4194304 | tf_op jit(solution)/shard_map/pallas_call | solution.py:254
  19.7 1.6 %collective-permute-start.13 = (f32[2,40,256]{2,1,0:T(8,128)S(1)}, f32[2,40,256]{2,1,0:T(8,128)S(1)}, u32[]{:S(2)}, u32[]{:S(2)}) collective-permute-start(f32[2,40,256]{2,1,0:T(8,128)S(1)} %shard_map.43), channel_id=1, source_target_pairs={{0,1},{1,0},{2,3},{3,2},{4,5},{5,4},{6,7},{7,6},{8,9},{9,8},{10,11... | collective-permute-start | bytes 245768 | tf_op jit(solution)/shard_map/ppermute | solution.py:323
  21.3 0.6 %shard_map.39.lags_away = bf16[2,2,528,256]{3,2,1,0:T(8,128)(2,1)S(1)} custom-call(f32[8,8,256]{2,1,0:T(8,128)S(1)} %collective-permute-done.8.v_a, f32[8,8,256]{2,1,0:T(8,128)S(1)} %collective-permute-done.9.v_b, f32[16,128]{1,0:T(8,128)S(1)} %collective-permute-done.2.h_a, f32[16,128]{1,0:T(8,128)S(1)} %get-tuple-element.33.h_b), custom_call_target="tpu_custom_call" | custom-call | flops 10000000 | bytes 3145728 | tf_op jit(solution)/shard_map/pallas_call | solution.py:228
  21.9 1.5 %shard_map.41.refs_0_ = f32[2,40,256]{2,1,0:T(8,128)S(1)} custom-call(s32[1,8]{1,0:T(1,128)S(1)} %bitcast.12, bf16[4,2,528,256]{3,2,1,0:T(8,128)(2,1)S(1)} %shard_map.38.lags_near, bf16[2,2,528,256]{3,2,1,0:T(8,128)(2,1)S(1)} %shard_map.39.lags_away, bf16[24,2,16,256]{3,2,1,0:T(8,128)(2,1)S(1)} %get-tuple-element.31.high_p, ...), custom_call_target="tpu_custom_call" | custom-call | flops 830472192 | bytes 4194304 | tf_op jit(solution)/shard_map/pallas_call | solution.py:254
  23.5 1.1 %collective-permute-done.13.refs_1_ = f32[2,40,256]{2,1,0:T(8,128)S(1)} collective-permute-done((f32[2,40,256]{2,1,0:T(8,128)S(1)}, f32[2,40,256]{2,1,0:T(8,128)S(1)}, u32[]{:S(2)}, u32[]{:S(2)}) %collective-permute-start.13) | collective-permute-done | bytes 81952 | tf_op jit(solution)/shard_map/ppermute | solution.py:323
  24.6 2.6 %collective-permute-start.14 = (f32[40,256]{1,0:T(8,128)S(1)}, f32[40,256]{1,0:T(8,128)S(1)}, u32[]{:S(2)}, u32[]{:S(2)}) collective-permute-start(f32[40,256]{1,0:T(8,128)S(1)} %fusion), channel_id=1, source_target_pairs={{0,2},{1,3},{2,0},{3,1},{4,6},{5,7},{6,4},{7,5},{8,10},{9,11},{10,... | collective-permute-start | bytes 122888 | tf_op jit(solution)/shard_map/ppermute | solution.py:326
  27.2 2.5 %collective-permute-done.14.refs_2_ = f32[40,256]{1,0:T(8,128)S(1)} collective-permute-done((f32[40,256]{1,0:T(8,128)S(1)}, f32[40,256]{1,0:T(8,128)S(1)}, u32[]{:S(2)}, u32[]{:S(2)}) %collective-permute-start.14) | collective-permute-done | bytes 40992 | tf_op jit(solution)/shard_map/ppermute | solution.py:326
  29.7 0.8 %shard_map.44 = f32[1,8,1056]{2,1,0:T(8,128)} custom-call(f32[2,40,256]{2,1,0:T(8,128)S(1)} %shard_map.41.refs_0_, f32[2,40,256]{2,1,0:T(8,128)S(1)} %collective-permute-done.13.refs_1_, f32[40,256]{1,0:T(8,128)S(1)} %collective-permute-done.14.refs_2_), custom_call_target="tpu_custom_call" | custom-call | flops 1000000 | bytes 262144 | tf_op jit(solution)/shard_map/pallas_call | solution.py:269
  (3 shorter events, 0.0 us)
Async XLA Ops:
  0.0 5.0 %collective-permute-start = (f32[16,8,256]{2,1,0:T(8,128)}, f32[16,8,256]{2,1,0:T(8,128)S(1)}, u32[]{:S(2)}, u32[]{:S(2)}) collective-permute-start(f32[16,8,256]{2,1,0:T(8,128)} %velocity.1), channel_id=1, source_target_pairs={{0,4},{4,0},{8,12},{12,8},{1,5},{5,1},{9,13},{13,9},{2,6},{6,2},{1... | collective-permute-start | bytes 393224 | tf_op jit(solution)/shard_map/ppermute | solution.py:300
  0.5 5.6 %collective-permute-start.1 = (f32[16,8,256]{2,1,0:T(8,128)}, f32[16,8,256]{2,1,0:T(8,128)S(1)}, u32[]{:S(2)}, u32[]{:S(2)}) collective-permute-start(f32[16,8,256]{2,1,0:T(8,128)} %o_own.1), channel_id=1, source_target_pairs={{0,4},{4,0},{8,12},{12,8},{1,5},{5,1},{9,13},{13,9},{2,6},{6,2},{1... | collective-permute-start | bytes 393224 | tf_op jit(solution)/shard_map/ppermute | solution.py:300
  0.5 11.0 %collective-permute-start.4 = (f32[16,8,256]{2,1,0:T(8,128)}, f32[16,8,256]{2,1,0:T(8,128)S(1)}, u32[]{:S(2)}, u32[]{:S(2)}) collective-permute-start(f32[16,8,256]{2,1,0:T(8,128)} %o_own.1), channel_id=1, source_target_pairs={{0,24},{4,28},{8,16},{12,20},{16,8},{20,12},{24,0},{28,4},{1,25},{... | collective-permute-start | bytes 393224 | tf_op jit(solution)/shard_map/ppermute | solution.py:304
  4.4 7.3 %collective-permute-start.5 = (f32[16,8,256]{2,1,0:T(8,128)}, f32[16,8,256]{2,1,0:T(8,128)S(1)}, u32[]{:S(2)}, u32[]{:S(2)}) collective-permute-start(f32[16,8,256]{2,1,0:T(8,128)} %o_own.1), channel_id=1, source_target_pairs={{0,16},{16,0},{1,17},{17,1},{2,18},{18,2},{3,19},{19,3},{4,20},{20... | collective-permute-start | bytes 393224 | tf_op jit(solution)/shard_map/ppermute | solution.py:303
  4.9 6.8 %collective-permute-start.6 = (f32[16,8,256]{2,1,0:T(8,128)}, f32[16,8,256]{2,1,0:T(8,128)S(1)}, u32[]{:S(2)}, u32[]{:S(2)}) collective-permute-start(f32[16,8,256]{2,1,0:T(8,128)} %o_own.1), channel_id=1, source_target_pairs={{0,8},{4,12},{8,0},{12,4},{1,9},{5,13},{9,1},{13,5},{2,10},{6,14},... | collective-permute-start | bytes 393224 | tf_op jit(solution)/shard_map/ppermute | solution.py:302
  5.0 0.9 %copy-start = (f32[16,8,256]{2,1,0:T(8,128)S(1)}, f32[16,8,256]{2,1,0:T(8,128)}, u32[]{:S(2)}) copy-start(f32[16,8,256]{2,1,0:T(8,128)} %velocity.1) | copy-start | bytes 393220
  6.1 5.7 %collective-permute-start.2 = (f32[16,128]{1,0:T(8,128)S(1)}, f32[16,128]{1,0:T(8,128)S(1)}, u32[]{:S(2)}, u32[]{:S(2)}) collective-permute-start(f32[16,128]{1,0:T(8,128)S(1)} %get-tuple-element.22), channel_id=1, source_target_pairs={{0,9},{1,8},{2,11},{3,10},{4,12},{5,14},{6,13},{7,15},{8,1},{9,0},... | collective-permute-start | bytes 24584 | tf_op jit(solution)/shard_map/ppermute | solution.py:310
  9.1 5.5 %collective-permute-start.3 = (f32[16,128]{1,0:T(8,128)S(1)}, f32[16,128]{1,0:T(8,128)S(1)}, u32[]{:S(2)}, u32[]{:S(2)}) collective-permute-start(f32[16,128]{1,0:T(8,128)S(1)} %get-tuple-element.23), channel_id=1, source_target_pairs={{0,1},{1,0},{2,3},{3,2},{4,4},{5,6},{6,5},{7,7},{8,9},{9,8},{10,11... | collective-permute-start | bytes 24584 | tf_op jit(solution)/shard_map/ppermute | solution.py:309
  11.5 4.3 %collective-permute-start.8 = (f32[8,8,256]{2,1,0:T(8,128)S(1)}, f32[8,8,256]{2,1,0:T(8,128)S(1)}, u32[]{:S(2)}, u32[]{:S(2)}) collective-permute-start(f32[8,8,256]{2,1,0:T(8,128)S(1)} %get-tuple-element.26), channel_id=1, source_target_pairs={{0,8},{4,12},{8,0},{12,4},{1,9},{5,13},{9,1},{13,5},{2,10},{6,14},... | collective-permute-start | bytes 196616 | tf_op jit(solution)/shard_map/ppermute | solution.py:308
  14.7 1.2 %collective-permute-start.7 = (f32[2,16,128]{2,1,0:T(8,128)S(1)}, f32[2,16,128]{2,1,0:T(8,128)S(1)}, u32[]{:S(2)}, u32[]{:S(2)}) collective-permute-start(f32[2,16,128]{2,1,0:T(8,128)S(1)} %pad_maximum_fusion), channel_id=1, source_target_pairs={{0,4},{4,0},{8,12},{12,8},{1,5},{5,1},{9,13},{13,9},{2,6},{6,2},{1... | collective-permute-start | bytes 49160 | tf_op jit(solution)/shard_map/ppermute | solution.py:300
  14.7 3.0 %collective-permute-start.10 = (f32[16,8,256]{2,1,0:T(8,128)S(1)}, f32[16,8,256]{2,1,0:T(8,128)S(1)}, u32[]{:S(2)}, u32[]{:S(2)}) collective-permute-start(f32[16,8,256]{2,1,0:T(8,128)S(1)} %collective-permute-done.5.u_own), channel_id=1, source_target_pairs={{0,4},{4,0},{8,12},{12,8},{1,5},{5,1},{9,13},{13,9},{2,6},{6,2},{1... | collective-permute-start | bytes 393224 | tf_op jit(solution)/shard_map/ppermute | solution.py:300
  15.2 2.5 %collective-permute-start.11 = (f32[16,8,256]{2,1,0:T(8,128)S(1)}, f32[16,8,256]{2,1,0:T(8,128)S(1)}, u32[]{:S(2)}, u32[]{:S(2)}) collective-permute-start(f32[16,8,256]{2,1,0:T(8,128)S(1)} %collective-permute-done.6.o_far), channel_id=1, source_target_pairs={{0,4},{4,0},{8,12},{12,8},{1,5},{5,1},{9,13},{13,9},{2,6},{6,2},{1... | collective-permute-start | bytes 393224 | tf_op jit(solution)/shard_map/ppermute | solution.py:300
  15.2 2.5 %collective-permute-start.12 = (f32[16,8,256]{2,1,0:T(8,128)S(1)}, f32[16,8,256]{2,1,0:T(8,128)S(1)}, u32[]{:S(2)}, u32[]{:S(2)}) collective-permute-start(f32[16,8,256]{2,1,0:T(8,128)S(1)} %collective-permute-done.4.u_far), channel_id=1, source_target_pairs={{0,4},{4,0},{8,12},{12,8},{1,5},{5,1},{9,13},{13,9},{2,6},{6,2},{1... | collective-permute-start | bytes 393224 | tf_op jit(solution)/shard_map/ppermute | solution.py:300
  15.8 1.3 %collective-permute-start.9 = (f32[8,8,256]{2,1,0:T(8,128)S(1)}, f32[8,8,256]{2,1,0:T(8,128)S(1)}, u32[]{:S(2)}, u32[]{:S(2)}) collective-permute-start(f32[8,8,256]{2,1,0:T(8,128)S(1)} %collective-permute-done.8.v_a), channel_id=1, source_target_pairs={{0,4},{4,0},{8,12},{12,8},{1,5},{5,1},{9,13},{13,9},{2,6},{6,2},{1... | collective-permute-start | bytes 196616 | tf_op jit(solution)/shard_map/ppermute | solution.py:300
  17.0 0.9 %copy-start.1 = (f32[16,8,256]{2,1,0:T(8,128)S(1)}, f32[16,8,256]{2,1,0:T(8,128)}, u32[]{:S(2)}) copy-start(f32[16,8,256]{2,1,0:T(8,128)} %o_own.1) | copy-start | bytes 393220
  17.1 1.0 %copy-start.2 = (s32[8]{0:T(128)S(1)}, s32[8]{0:T(128)}, u32[]{:S(2)}) copy-start(s32[8]{0:T(128)} %param.5) | copy-start | bytes 100
  19.7 4.9 %collective-permute-start.13 = (f32[2,40,256]{2,1,0:T(8,128)S(1)}, f32[2,40,256]{2,1,0:T(8,128)S(1)}, u32[]{:S(2)}, u32[]{:S(2)}) collective-permute-start(f32[2,40,256]{2,1,0:T(8,128)S(1)} %shard_map.43), channel_id=1, source_target_pairs={{0,1},{1,0},{2,3},{3,2},{4,5},{5,4},{6,7},{7,6},{8,9},{9,8},{10,11... | collective-permute-start | bytes 245768 | tf_op jit(solution)/shard_map/ppermute | solution.py:323
  24.6 5.1 %collective-permute-start.14 = (f32[40,256]{1,0:T(8,128)S(1)}, f32[40,256]{1,0:T(8,128)S(1)}, u32[]{:S(2)}, u32[]{:S(2)}) collective-permute-start(f32[40,256]{1,0:T(8,128)S(1)} %fusion), channel_id=1, source_target_pairs={{0,2},{1,3},{2,0},{3,1},{4,6},{5,7},{6,4},{7,5},{8,10},{9,11},{10,... | collective-permute-start | bytes 122888 | tf_op jit(solution)/shard_map/ppermute | solution.py:326

commit v5 on v4

--- a/solution.py
+++ b/solution.py
@@ -143,7 +143,7 @@
             right += [high, low, high]
         right = jnp.concatenate(right, axis=1)
         left = []
-        for lags, at in ((lags_near, station), (lags_away, i)):
+        for lags, at in ((lags_near, i), (lags_away, i)):
             left += [lags[at, 0], lags[at, 0], lags[at, 1]]
         left = jnp.concatenate(left, axis=1)
         prod[i] = lax.dot_general(left, right, (((1,), (1,)), ((), ())), preferred_element_type=F32)
@@ -313,16 +313,16 @@
     both_sib = to_sibling(both)
     h_near_sib, h_away_sib = both_sib[0], both_sib[1]
     up_sib, diag_sib, far_sib, v_far_sib = (to_sibling(x) for x in (up, diag, far, v_far))
-    near = lag_rows(None, False, vel, v_sib, h_near, h_near_sib)
+    own = (vel, v_sib, h_near, h_near_sib)
     high_p, low_p = window([pressure, up, far, diag, p_sib, up_sib, far_sib, diag_sib])
     series = (v_far, v_far_sib, h_away, h_away_sib)
 
     offsets = offsets.reshape(1, -1)
     flips = (1, 3)
-    give = products(flips, offsets, near, lag_rows(flips, True, *series), high_p, low_p)
+    give = products(flips, offsets, lag_rows(flips, False, *own), lag_rows(flips, True, *series), high_p, low_p)
     first = lax.ppermute(give, "ta", [(i, i ^ 1) for i in range(ta_n)])
     flips = (0, 2)
-    keep = products(flips, offsets, near, lag_rows(flips, True, *series), high_p, low_p)
+    keep = products(flips, offsets, lag_rows(flips, False, *own), lag_rows(flips, True, *series), high_p, low_p)
     second = lax.ppermute(keep[1] + first[1], "ta", [(i, i ^ 2) for i in range(ta_n)])
     return close([keep, first, second], factor, offsets.shape[1], azim)
 

time: 30.7 us -> 30 us (0.977)
  waiting for transfers between devices: 6.83 us -> 6.23 us
    ppermute x1, waiting for transfers between devices: 1.12 us -> 0.17 us  [shards(): first = lax.ppermute(give, 'ta', [(i, i ^ 1) for i in range(ta_n)])]
    ppermute x7, waiting for transfers between devices: 0.1 us -> 0.66 us  [shards(): to_sibling = lambda x: lax.ppermute(x, 'az', sibling)]
    pallas_call x3 -> x4, Pallas kernels: 2.33 us -> 2.38 us  [lag_rows(): pl.pallas_call(functools.partial(lag_kernel, flips, away), in_specs=[VMEM...]
  transfers between devices with their start and end apart: 15 -> 15, of which waited for: 6 -> 6; matrix products, arithmetic and copies ran while one was open for 0% -> 0% of each run, Pallas kernels for 13% -> 14%
where the time goes in v5:
time: 30 us; the launch traced here: 29.8 us
  starting transfers between devices  15.9 us (53%)
  Pallas kernels  6.67 us (22%)
  waiting for transfers between devices  6.23 us (21%)
  local copies, waits for them, and re-layouts  0.91 us (3%)
    ppermute x1, starting transfers between devices, shards(): diag = lax.ppermute(pressure, ('gx', 'az'), diagonal)  3.89 us
    pallas_call x2, Pallas kernels, products(): pl.pallas_call(functools.partial(product_kernel, flips), in_specs=[VMEM]...  3.1 us
    ppermute x1, starting transfers between devices, shards(): h_away = lax.ppermute(ends_away, ('az', 'ta'), in_time_across)  3.07 us
    ppermute x1, waiting for transfers between devices, shards(): h_near = lax.ppermute(ends_near, ('az', 'ta'), in_time)  2.89 us
    ppermute x1, starting transfers between devices, shards(): lax.ppermute(keep[1] + first[1], 'ta', [(i, i ^ 2) for i in range(ta_n)])  2.61 us
    pallas_call x4, Pallas kernels, lag_rows(): pl.pallas_call(functools.partial(lag_kernel, flips, away), in_specs=[VMEM...  2.38 us
    ppermute x1, starting transfers between devices, shards(): h_near = lax.ppermute(ends_near, ('az', 'ta'), in_time)  2.35 us
    ppermute x1, waiting for transfers between devices, shards(): lax.ppermute(keep[1] + first[1], 'ta', [(i, i ^ 2) for i in range(ta_n)])  2.31 us
  transfers between devices with their start and end apart: 15, of which 6 were waited for; matrix products, arithmetic and copies ran while one was open for 0% of the time, Pallas kernels for 14%

profile of v5, /device:TPU:0, one launch (start us, length us, event | category | flops | bytes accessed | tf_op | source)
XLA Modules:
  0.0 29.8 jit_solution(3783245764419402656)
XLA Ops:
  0.0 0.5 %collective-permute-start = (f32[16,8,256]{2,1,0:T(8,128)}, f32[16,8,256]{2,1,0:T(8,128)S(1)}, u32[]{:S(2)}, u32[]{:S(2)}) collective-permute-start(f32[16,8,256]{2,1,0:T(8,128)} %velocity.1), channel_id=1, source_target_pairs={{0,4},{4,0},{8,12},{12,8},{1,5},{5,1},{9,13},{13,9},{2,6},{6,2},{1... | collective-permute-start | bytes 393224 | tf_op jit(solution)/shard_map/ppermute | solution.py:300
  0.5 0.1 collective-permute-start.1
  0.5 3.9 %collective-permute-start.4 = (f32[16,8,256]{2,1,0:T(8,128)}, f32[16,8,256]{2,1,0:T(8,128)S(1)}, u32[]{:S(2)}, u32[]{:S(2)}) collective-permute-start(f32[16,8,256]{2,1,0:T(8,128)} %o_own.1), channel_id=1, source_target_pairs={{0,24},{4,28},{8,16},{12,20},{16,8},{20,12},{24,0},{28,4},{1,25},{... | collective-permute-start | bytes 393224 | tf_op jit(solution)/shard_map/ppermute | solution.py:304
  4.4 0.5 %collective-permute-start.5 = (f32[16,8,256]{2,1,0:T(8,128)}, f32[16,8,256]{2,1,0:T(8,128)S(1)}, u32[]{:S(2)}, u32[]{:S(2)}) collective-permute-start(f32[16,8,256]{2,1,0:T(8,128)} %o_own.1), channel_id=1, source_target_pairs={{0,16},{16,0},{1,17},{17,1},{2,18},{18,2},{3,19},{19,3},{4,20},{20... | collective-permute-start | bytes 393224 | tf_op jit(solution)/shard_map/ppermute | solution.py:303
  4.9 0.0 collective-permute-start.6
  5.0 0.0 collective-permute-done.v_sib.v_b
  5.0 0.0 copy-start
  5.0 0.9 %copy-done = f32[16,8,256]{2,1,0:T(8,128)S(1)} copy-done((f32[16,8,256]{2,1,0:T(8,128)S(1)}, f32[16,8,256]{2,1,0:T(8,128)}, u32[]{:S(2)}) %copy-start) | copy-done | bytes 131096
  5.9 0.2 shard_map.37
  6.1 0.0 collective-permute-done.1.o_sib
  6.1 3.1 %collective-permute-start.2 = (f32[16,128]{1,0:T(8,128)S(1)}, f32[16,128]{1,0:T(8,128)S(1)}, u32[]{:S(2)}, u32[]{:S(2)}) collective-permute-start(f32[16,128]{1,0:T(8,128)S(1)} %get-tuple-element.22), channel_id=1, source_target_pairs={{0,9},{1,8},{2,11},{3,10},{4,12},{5,14},{6,13},{7,15},{8,1},{9,0},... | collective-permute-start | bytes 24584 | tf_op jit(solution)/shard_map/ppermute | solution.py:310
  9.1 2.3 %collective-permute-start.3 = (f32[16,128]{1,0:T(8,128)S(1)}, f32[16,128]{1,0:T(8,128)S(1)}, u32[]{:S(2)}, u32[]{:S(2)}) collective-permute-start(f32[16,128]{1,0:T(8,128)S(1)} %get-tuple-element.23), channel_id=1, source_target_pairs={{0,1},{1,0},{2,3},{3,2},{4,4},{5,6},{6,5},{7,7},{8,9},{9,8},{10,11... | collective-permute-start | bytes 24584 | tf_op jit(solution)/shard_map/ppermute | solution.py:309
  11.5 0.0 collective-permute-done.4.u_far
  11.5 0.2 collective-permute-start.8
  11.7 0.0 collective-permute-done.5.u_own
  11.7 0.1 collective-permute-done.6.o_far
  11.8 0.0 collective-permute-done.2.h_a
  11.8 2.9 %collective-permute-done.3.h_a = f32[16,128]{1,0:T(8,128)S(1)} collective-permute-done((f32[16,128]{1,0:T(8,128)S(1)}, f32[16,128]{1,0:T(8,128)S(1)}, u32[]{:S(2)}, u32[]{:S(2)}) %collective-permute-start.3) | collective-permute-done | bytes 8224 | tf_op jit(solution)/shard_map/ppermute | solution.py:309
  14.7 0.0 collective-permute-start.7
  14.7 0.5 %collective-permute-start.10 = (f32[16,8,256]{2,1,0:T(8,128)S(1)}, f32[16,8,256]{2,1,0:T(8,128)S(1)}, u32[]{:S(2)}, u32[]{:S(2)}) collective-permute-start(f32[16,8,256]{2,1,0:T(8,128)S(1)} %collective-permute-done.5.u_own), channel_id=1, source_target_pairs={{0,4},{4,0},{8,12},{12,8},{1,5},{5,1},{9,13},{13,9},{2,6},{6,2},{1... | collective-permute-start | bytes 393224 | tf_op jit(solution)/shard_map/ppermute | solution.py:300
  15.2 0.0 collective-permute-start.11
  15.2 0.5 %collective-permute-start.12 = (f32[16,8,256]{2,1,0:T(8,128)S(1)}, f32[16,8,256]{2,1,0:T(8,128)S(1)}, u32[]{:S(2)}, u32[]{:S(2)}) collective-permute-start(f32[16,8,256]{2,1,0:T(8,128)S(1)} %collective-permute-done.4.u_far), channel_id=1, source_target_pairs={{0,4},{4,0},{8,12},{12,8},{1,5},{5,1},{9,13},{13,9},{2,6},{6,2},{1... | collective-permute-start | bytes 393224 | tf_op jit(solution)/shard_map/ppermute | solution.py:300
  15.7 0.1 collective-permute-done.8.v_a
  15.8 0.0 collective-permute-start.9
  15.8 0.0 collective-permute-done.7
  15.9 0.0 copy-start.1
  15.9 0.6 %shard_map.42.lags_near = bf16[2,2,528,256]{3,2,1,0:T(8,128)(2,1)S(1)} custom-call(f32[16,8,256]{2,1,0:T(8,128)S(1)} %get-tuple-element.19.v_a, f32[16,8,256]{2,1,0:T(8,128)S(1)} %collective-permute-done.v_sib.v_b, f32[16,128]{1,0:T(8,128)S(1)} %collective-permute-done.3.h_a, f32[16,128]{1,0:T(8,128)S(1)} %get-tuple-element.34.h_b), custom_call_target="tpu_custom_call" | custom-call | flops 10000000 | bytes 3145728 | tf_op jit(solution)/shard_map/pallas_call | solution.py:228
  16.5 0.6 %collective-permute-done.9.v_b = f32[8,8,256]{2,1,0:T(8,128)S(1)} collective-permute-done((f32[8,8,256]{2,1,0:T(8,128)S(1)}, f32[8,8,256]{2,1,0:T(8,128)S(1)}, u32[]{:S(2)}, u32[]{:S(2)}) %collective-permute-start.9) | collective-permute-done | bytes 65568 | tf_op jit(solution)/shard_map/ppermute | solution.py:300
  17.1 0.0 copy-start.2
  17.1 0.6 %shard_map.43.lags_away = bf16[2,2,528,256]{3,2,1,0:T(8,128)(2,1)S(1)} custom-call(f32[8,8,256]{2,1,0:T(8,128)S(1)} %collective-permute-done.8.v_a, f32[8,8,256]{2,1,0:T(8,128)S(1)} %collective-permute-done.9.v_b, f32[16,128]{1,0:T(8,128)S(1)} %collective-permute-done.2.h_a, f32[16,128]{1,0:T(8,128)S(1)} %get-tuple-element.33.h_b), custom_call_target="tpu_custom_call" | custom-call | flops 10000000 | bytes 3145728 | tf_op jit(solution)/shard_map/pallas_call | solution.py:228
  17.7 0.0 collective-permute-done.10.u_sib
  17.7 0.0 collective-permute-done.11.o_far_sib
  17.7 0.0 collective-permute-done.12.u_far_sib
  17.7 0.0 copy-done.1
  17.7 0.2 shard_map.40
  18.0 0.0 copy-done.2
  18.0 1.5 %shard_map.44 = f32[2,40,256]{2,1,0:T(8,128)S(1)} custom-call(s32[1,8]{1,0:T(1,128)S(1)} %bitcast.11, bf16[2,2,528,256]{3,2,1,0:T(8,128)(2,1)S(1)} %shard_map.42.lags_near, bf16[2,2,528,256]{3,2,1,0:T(8,128)(2,1)S(1)} %shard_map.43.lags_away, bf16[24,2,16,256]{3,2,1,0:T(8,128)(2,1)S(1)} %get-tuple-element.31.high_p, ...), custom_call_target="tpu_custom_call" | custom-call | flops 830472192 | bytes 4194304 | tf_op jit(solution)/shard_map/pallas_call | solution.py:254
  19.5 1.6 %collective-permute-start.13 = (f32[2,40,256]{2,1,0:T(8,128)S(1)}, f32[2,40,256]{2,1,0:T(8,128)S(1)}, u32[]{:S(2)}, u32[]{:S(2)}) collective-permute-start(f32[2,40,256]{2,1,0:T(8,128)S(1)} %shard_map.44), channel_id=1, source_target_pairs={{0,1},{1,0},{2,3},{3,2},{4,5},{5,4},{6,7},{7,6},{8,9},{9,8},{10,11... | collective-permute-start | bytes 245768 | tf_op jit(solution)/shard_map/ppermute | solution.py:323
  21.2 0.6 %shard_map.38.lags_near = bf16[2,2,528,256]{3,2,1,0:T(8,128)(2,1)S(1)} custom-call(f32[16,8,256]{2,1,0:T(8,128)S(1)} %get-tuple-element.19.v_a, f32[16,8,256]{2,1,0:T(8,128)S(1)} %collective-permute-done.v_sib.v_b, f32[16,128]{1,0:T(8,128)S(1)} %collective-permute-done.3.h_a, f32[16,128]{1,0:T(8,128)S(1)} %get-tuple-element.34.h_b), custom_call_target="tpu_custom_call" | custom-call | flops 10000000 | bytes 3145728 | tf_op jit(solution)/shard_map/pallas_call | solution.py:228
  21.8 0.6 %shard_map.39.lags_away = bf16[2,2,528,256]{3,2,1,0:T(8,128)(2,1)S(1)} custom-call(f32[8,8,256]{2,1,0:T(8,128)S(1)} %collective-permute-done.8.v_a, f32[8,8,256]{2,1,0:T(8,128)S(1)} %collective-permute-done.9.v_b, f32[16,128]{1,0:T(8,128)S(1)} %collective-permute-done.2.h_a, f32[16,128]{1,0:T(8,128)S(1)} %get-tuple-element.33.h_b), custom_call_target="tpu_custom_call" | custom-call | flops 10000000 | bytes 3145728 | tf_op jit(solution)/shard_map/pallas_call | solution.py:228
  22.4 1.6 %shard_map.41.refs_0_ = f32[2,40,256]{2,1,0:T(8,128)S(1)} custom-call(s32[1,8]{1,0:T(1,128)S(1)} %bitcast.12, bf16[2,2,528,256]{3,2,1,0:T(8,128)(2,1)S(1)} %shard_map.38.lags_near, bf16[2,2,528,256]{3,2,1,0:T(8,128)(2,1)S(1)} %shard_map.39.lags_away, bf16[24,2,16,256]{3,2,1,0:T(8,128)(2,1)S(1)} %get-tuple-element.31.high_p, ...), custom_call_target="tpu_custom_call" | custom-call | flops 830472192 | bytes 4194304 | tf_op jit(solution)/shard_map/pallas_call | solution.py:254
  23.9 0.2 collective-permute-done.13.refs_1_
  24.1 2.6 %collective-permute-start.14 = (f32[40,256]{1,0:T(8,128)S(1)}, f32[40,256]{1,0:T(8,128)S(1)}, u32[]{:S(2)}, u32[]{:S(2)}) collective-permute-start(f32[40,256]{1,0:T(8,128)S(1)} %fusion), channel_id=1, source_target_pairs={{0,2},{1,3},{2,0},{3,1},{4,6},{5,7},{6,4},{7,5},{8,10},{9,11},{10,... | collective-permute-start | bytes 122888 | tf_op jit(solution)/shard_map/ppermute | solution.py:326
  26.7 2.3 %collective-permute-done.14.refs_2_ = f32[40,256]{1,0:T(8,128)S(1)} collective-permute-done((f32[40,256]{1,0:T(8,128)S(1)}, f32[40,256]{1,0:T(8,128)S(1)}, u32[]{:S(2)}, u32[]{:S(2)}) %collective-permute-start.14) | collective-permute-done | bytes 40992 | tf_op jit(solution)/shard_map/ppermute | solution.py:326
  29.0 0.8 %shard_map.45 = f32[1,8,1056]{2,1,0:T(8,128)} custom-call(f32[2,40,256]{2,1,0:T(8,128)S(1)} %shard_map.41.refs_0_, f32[2,40,256]{2,1,0:T(8,128)S(1)} %collective-permute-done.13.refs_1_, f32[40,256]{1,0:T(8,128)S(1)} %collective-permute-done.14.refs_2_), custom_call_target="tpu_custom_call" | custom-call | flops 1000000 | bytes 262144 | tf_op jit(solution)/shard_map/pallas_call | solution.py:269
  (3 shorter events, 0.0 us)
Async XLA Ops:
  0.0 5.0 %collective-permute-start = (f32[16,8,256]{2,1,0:T(8,128)}, f32[16,8,256]{2,1,0:T(8,128)S(1)}, u32[]{:S(2)}, u32[]{:S(2)}) collective-permute-start(f32[16,8,256]{2,1,0:T(8,128)} %velocity.1), channel_id=1, source_target_pairs={{0,4},{4,0},{8,12},{12,8},{1,5},{5,1},{9,13},{13,9},{2,6},{6,2},{1... | collective-permute-start | bytes 393224 | tf_op jit(solution)/shard_map/ppermute | solution.py:300
  0.5 5.6 %collective-permute-start.1 = (f32[16,8,256]{2,1,0:T(8,128)}, f32[16,8,256]{2,1,0:T(8,128)S(1)}, u32[]{:S(2)}, u32[]{:S(2)}) collective-permute-start(f32[16,8,256]{2,1,0:T(8,128)} %o_own.1), channel_id=1, source_target_pairs={{0,4},{4,0},{8,12},{12,8},{1,5},{5,1},{9,13},{13,9},{2,6},{6,2},{1... | collective-permute-start | bytes 393224 | tf_op jit(solution)/shard_map/ppermute | solution.py:300
  0.5 11.0 %collective-permute-start.4 = (f32[16,8,256]{2,1,0:T(8,128)}, f32[16,8,256]{2,1,0:T(8,128)S(1)}, u32[]{:S(2)}, u32[]{:S(2)}) collective-permute-start(f32[16,8,256]{2,1,0:T(8,128)} %o_own.1), channel_id=1, source_target_pairs={{0,24},{4,28},{8,16},{12,20},{16,8},{20,12},{24,0},{28,4},{1,25},{... | collective-permute-start | bytes 393224 | tf_op jit(solution)/shard_map/ppermute | solution.py:304
  4.4 7.3 %collective-permute-start.5 = (f32[16,8,256]{2,1,0:T(8,128)}, f32[16,8,256]{2,1,0:T(8,128)S(1)}, u32[]{:S(2)}, u32[]{:S(2)}) collective-permute-start(f32[16,8,256]{2,1,0:T(8,128)} %o_own.1), channel_id=1, source_target_pairs={{0,16},{16,0},{1,17},{17,1},{2,18},{18,2},{3,19},{19,3},{4,20},{20... | collective-permute-start | bytes 393224 | tf_op jit(solution)/shard_map/ppermute | solution.py:303
  4.9 6.8 %collective-permute-start.6 = (f32[16,8,256]{2,1,0:T(8,128)}, f32[16,8,256]{2,1,0:T(8,128)S(1)}, u32[]{:S(2)}, u32[]{:S(2)}) collective-permute-start(f32[16,8,256]{2,1,0:T(8,128)} %o_own.1), channel_id=1, source_target_pairs={{0,8},{4,12},{8,0},{12,4},{1,9},{5,13},{9,1},{13,5},{2,10},{6,14},... | collective-permute-start | bytes 393224 | tf_op jit(solution)/shard_map/ppermute | solution.py:302
  5.0 0.9 %copy-start = (f32[16,8,256]{2,1,0:T(8,128)S(1)}, f32[16,8,256]{2,1,0:T(8,128)}, u32[]{:S(2)}) copy-start(f32[16,8,256]{2,1,0:T(8,128)} %velocity.1) | copy-start | bytes 393220
  6.1 5.7 %collective-permute-start.2 = (f32[16,128]{1,0:T(8,128)S(1)}, f32[16,128]{1,0:T(8,128)S(1)}, u32[]{:S(2)}, u32[]{:S(2)}) collective-permute-start(f32[16,128]{1,0:T(8,128)S(1)} %get-tuple-element.22), channel_id=1, source_target_pairs={{0,9},{1,8},{2,11},{3,10},{4,12},{5,14},{6,13},{7,15},{8,1},{9,0},... | collective-permute-start | bytes 24584 | tf_op jit(solution)/shard_map/ppermute | solution.py:310
  9.1 5.5 %collective-permute-start.3 = (f32[16,128]{1,0:T(8,128)S(1)}, f32[16,128]{1,0:T(8,128)S(1)}, u32[]{:S(2)}, u32[]{:S(2)}) collective-permute-start(f32[16,128]{1,0:T(8,128)S(1)} %get-tuple-element.23), channel_id=1, source_target_pairs={{0,1},{1,0},{2,3},{3,2},{4,4},{5,6},{6,5},{7,7},{8,9},{9,8},{10,11... | collective-permute-start | bytes 24584 | tf_op jit(solution)/shard_map/ppermute | solution.py:309
  11.5 4.3 %collective-permute-start.8 = (f32[8,8,256]{2,1,0:T(8,128)S(1)}, f32[8,8,256]{2,1,0:T(8,128)S(1)}, u32[]{:S(2)}, u32[]{:S(2)}) collective-permute-start(f32[8,8,256]{2,1,0:T(8,128)S(1)} %get-tuple-element.26), channel_id=1, source_target_pairs={{0,8},{4,12},{8,0},{12,4},{1,9},{5,13},{9,1},{13,5},{2,10},{6,14},... | collective-permute-start | bytes 196616 | tf_op jit(solution)/shard_map/ppermute | solution.py:308
  14.7 1.2 %collective-permute-start.7 = (f32[2,16,128]{2,1,0:T(8,128)S(1)}, f32[2,16,128]{2,1,0:T(8,128)S(1)}, u32[]{:S(2)}, u32[]{:S(2)}) collective-permute-start(f32[2,16,128]{2,1,0:T(8,128)S(1)} %pad_maximum_fusion), channel_id=1, source_target_pairs={{0,4},{4,0},{8,12},{12,8},{1,5},{5,1},{9,13},{13,9},{2,6},{6,2},{1... | collective-permute-start | bytes 49160 | tf_op jit(solution)/shard_map/ppermute | solution.py:300
  14.7 3.0 %collective-permute-start.10 = (f32[16,8,256]{2,1,0:T(8,128)S(1)}, f32[16,8,256]{2,1,0:T(8,128)S(1)}, u32[]{:S(2)}, u32[]{:S(2)}) collective-permute-start(f32[16,8,256]{2,1,0:T(8,128)S(1)} %collective-permute-done.5.u_own), channel_id=1, source_target_pairs={{0,4},{4,0},{8,12},{12,8},{1,5},{5,1},{9,13},{13,9},{2,6},{6,2},{1... | collective-permute-start | bytes 393224 | tf_op jit(solution)/shard_map/ppermute | solution.py:300
  15.2 2.5 %collective-permute-start.11 = (f32[16,8,256]{2,1,0:T(8,128)S(1)}, f32[16,8,256]{2,1,0:T(8,128)S(1)}, u32[]{:S(2)}, u32[]{:S(2)}) collective-permute-start(f32[16,8,256]{2,1,0:T(8,128)S(1)} %collective-permute-done.6.o_far), channel_id=1, source_target_pairs={{0,4},{4,0},{8,12},{12,8},{1,5},{5,1},{9,13},{13,9},{2,6},{6,2},{1... | collective-permute-start | bytes 393224 | tf_op jit(solution)/shard_map/ppermute | solution.py:300
  15.2 2.5 %collective-permute-start.12 = (f32[16,8,256]{2,1,0:T(8,128)S(1)}, f32[16,8,256]{2,1,0:T(8,128)S(1)}, u32[]{:S(2)}, u32[]{:S(2)}) collective-permute-start(f32[16,8,256]{2,1,0:T(8,128)S(1)} %collective-permute-done.4.u_far), channel_id=1, source_target_pairs={{0,4},{4,0},{8,12},{12,8},{1,5},{5,1},{9,13},{13,9},{2,6},{6,2},{1... | collective-permute-start | bytes 393224 | tf_op jit(solution)/shard_map/ppermute | solution.py:300
  15.8 1.3 %collective-permute-start.9 = (f32[8,8,256]{2,1,0:T(8,128)S(1)}, f32[8,8,256]{2,1,0:T(8,128)S(1)}, u32[]{:S(2)}, u32[]{:S(2)}) collective-permute-start(f32[8,8,256]{2,1,0:T(8,128)S(1)} %collective-permute-done.8.v_a), channel_id=1, source_target_pairs={{0,4},{4,0},{8,12},{12,8},{1,5},{5,1},{9,13},{13,9},{2,6},{6,2},{1... | collective-permute-start | bytes 196616 | tf_op jit(solution)/shard_map/ppermute | solution.py:300
  15.9 1.9 %copy-start.1 = (f32[16,8,256]{2,1,0:T(8,128)S(1)}, f32[16,8,256]{2,1,0:T(8,128)}, u32[]{:S(2)}) copy-start(f32[16,8,256]{2,1,0:T(8,128)} %o_own.1) | copy-start | bytes 393220
  17.1 0.9 %copy-start.2 = (s32[8]{0:T(128)S(1)}, s32[8]{0:T(128)}, u32[]{:S(2)}) copy-start(s32[8]{0:T(128)} %param.5) | copy-start | bytes 100
  19.5 4.6 %collective-permute-start.13 = (f32[2,40,256]{2,1,0:T(8,128)S(1)}, f32[2,40,256]{2,1,0:T(8,128)S(1)}, u32[]{:S(2)}, u32[]{:S(2)}) collective-permute-start(f32[2,40,256]{2,1,0:T(8,128)S(1)} %shard_map.44), channel_id=1, source_target_pairs={{0,1},{1,0},{2,3},{3,2},{4,5},{5,4},{6,7},{7,6},{8,9},{9,8},{10,11... | collective-permute-start | bytes 245768 | tf_op jit(solution)/shard_map/ppermute | solution.py:323
  24.1 4.9 %collective-permute-start.14 = (f32[40,256]{1,0:T(8,128)S(1)}, f32[40,256]{1,0:T(8,128)S(1)}, u32[]{:S(2)}, u32[]{:S(2)}) collective-permute-start(f32[40,256]{1,0:T(8,128)S(1)} %fusion), channel_id=1, source_target_pairs={{0,2},{1,3},{2,0},{3,1},{4,6},{5,7},{6,4},{7,5},{8,10},{9,11},{10,... | collective-permute-start | bytes 122888 | tf_op jit(solution)/shard_map/ppermute | solution.py:326

commit v6 on v5

--- a/solution.py
+++ b/solution.py
@@ -299,20 +299,25 @@
 
     to_sibling = lambda x: lax.ppermute(x, "az", sibling)
 
+    diag = lax.ppermute(pressure, ("gx", "az"), diagonal)
     far = lax.ppermute(pressure, "az", across)
+    p_sib = to_sibling(pressure)
+    v_sib = to_sibling(velocity)
     up = lax.ppermute(pressure, "gx", upstream)
-    diag = lax.ppermute(pressure, ("gx", "az"), diagonal)
-    v_sib, p_sib = to_sibling(velocity), to_sibling(pressure)
     vel, v_for, ends_near, ends_away = fetch(velocity, v_sib)
-    ends_near, ends_away, p_sib = lax.optimization_barrier((ends_near, ends_away, p_sib))
+    ends_near, ends_away = lax.optimization_barrier((ends_near, ends_away))
+    h_near = lax.ppermute(ends_near, ("az", "ta"), in_time)
     v_far = lax.ppermute(v_for, "az", across)
-    h_near = lax.ppermute(ends_near, ("az", "ta"), in_time)
     h_away = lax.ppermute(ends_away, ("az", "ta"), in_time_across)
-    h_away, h_near, diag, up, far = lax.optimization_barrier((h_away, h_near, diag, up, far))
+    diag, h_away, h_near, up, far = lax.optimization_barrier((diag, h_away, h_near, up, far))
     both = jnp.stack([h_near, h_away])
+    v_far, far = lax.optimization_barrier((v_far, far))
+    up_sib = to_sibling(up)
+    v_far_sib = to_sibling(v_far)
+    diag_sib = to_sibling(diag)
+    far_sib = to_sibling(far)
     both_sib = to_sibling(both)
     h_near_sib, h_away_sib = both_sib[0], both_sib[1]
-    up_sib, diag_sib, far_sib, v_far_sib = (to_sibling(x) for x in (up, diag, far, v_far))
     own = (vel, v_sib, h_near, h_near_sib)
     high_p, low_p = window([pressure, up, far, diag, p_sib, up_sib, far_sib, diag_sib])
     series = (v_far, v_far_sib, h_away, h_away_sib)
@@ -322,9 +327,12 @@
     give = products(flips, offsets, lag_rows(flips, False, *own), lag_rows(flips, True, *series), high_p, low_p)
     first = lax.ppermute(give, "ta", [(i, i ^ 1) for i in range(ta_n)])
     flips = (0, 2)
-    keep = products(flips, offsets, lag_rows(flips, False, *own), lag_rows(flips, True, *series), high_p, low_p)
-    second = lax.ppermute(keep[1] + first[1], "ta", [(i, i ^ 2) for i in range(ta_n)])
-    return close([keep, first, second], factor, offsets.shape[1], azim)
+    keep = [
+        products((flip,), offsets, lag_rows((flip,), False, *own), lag_rows((flip,), True, *series), high_p, low_p)
+        for flip in (2, 0)
+    ]
+    second = lax.ppermute(keep[0][0] + first[1], "ta", [(i, i ^ 2) for i in range(ta_n)])
+    return close([keep[1], first, second], factor, offsets.shape[1], azim)
 
 
 def solution(mesh):

time: 30 us -> 29.5 us (0.983)
  waiting for transfers between devices: 6.23 us -> 5.08 us
  Pallas kernels: 6.67 us -> 7.33 us
    ppermute x1, starting transfers between devices: 3.89 us -> 0.04 us  [shards(): diag = lax.ppermute(pressure, ('gx', 'az'), diagonal)]
    ppermute x1, starting transfers between devices: 0.03 us -> 2.52 us  [shards(): far = lax.ppermute(pressure, 'az', across)]
    ppermute x1, waiting for transfers between devices: 2.31 us -> 0.59 us  [shards(): lax.ppermute(keep[0][0] + first[1], 'ta', [(i, i ^ 2) for i in range(ta_n)])]
    ppermute x1, waiting for transfers between devices: 0.17 us -> 1.21 us  [shards(): first = lax.ppermute(give, 'ta', [(i, i ^ 1) for i in range(ta_n)])]
    ppermute x1, starting transfers between devices: 0.54 us -> 1.49 us  [shards(): up = lax.ppermute(pressure, 'gx', upstream)]
    pallas_call x2 -> x3, Pallas kernels: 3.1 us -> 3.67 us  [products(): pl.pallas_call(functools.partial(product_kernel, flips), in_specs=[VMEM]...]
    ppermute x7, waiting for transfers between devices: 0.66 us -> 0.17 us  [shards(): to_sibling = lambda x: lax.ppermute(x, 'az', sibling)]
    ppermute x7, starting transfers between devices: 1.53 us -> 1.96 us  [shards(): to_sibling = lambda x: lax.ppermute(x, 'az', sibling)]
  transfers between devices with their start and end apart: 15 -> 15, of which waited for: 6 -> 6; matrix products, arithmetic and copies ran while one was open for 0% -> 0% of each run, Pallas kernels for 14% -> 16%
where the time goes in v6:
time: 29.5 us; the launch traced here: 29.3 us
  starting transfers between devices  15.8 us (54%)
  Pallas kernels  7.33 us (25%)
  waiting for transfers between devices  5.08 us (17%)
  local copies, waits for them, and re-layouts  0.91 us (3%)
    pallas_call x3, Pallas kernels, products(): pl.pallas_call(functools.partial(product_kernel, flips), in_specs=[VMEM]...  3.67 us
    ppermute x1, starting transfers between devices, shards(): h_away = lax.ppermute(ends_away, ('az', 'ta'), in_time_across)  3.03 us
    ppermute x1, waiting for transfers between devices, shards(): h_near = lax.ppermute(ends_near, ('az', 'ta'), in_time)  2.62 us
    ppermute x1, starting transfers between devices, shards(): lax.ppermute(keep[0][0] + first[1], 'ta', [(i, i ^ 2) for i in range(ta_n)])  2.59 us
    ppermute x1, starting transfers between devices, shards(): far = lax.ppermute(pressure, 'az', across)  2.52 us
    pallas_call x6, Pallas kernels, lag_rows(): pl.pallas_call(functools.partial(lag_kernel, flips, away), in_specs=[VMEM...  2.47 us
    ppermute x1, starting transfers between devices, shards(): h_near = lax.ppermute(ends_near, ('az', 'ta'), in_time)  2.35 us
    ppermute x7, starting transfers between devices, shards(): to_sibling = lambda x: lax.ppermute(x, 'az', sibling)  1.96 us
  transfers between devices with their start and end apart: 15, of which 6 were waited for; matrix products, arithmetic and copies ran while one was open for 0% of the time, Pallas kernels for 16%

profile of v6, /device:TPU:0, one launch (start us, length us, event | category | flops | bytes accessed | tf_op | source)
XLA Modules:
  0.0 29.3 jit_solution(3807360074933265882)
XLA Ops:
  0.0 0.5 %collective-permute-start = (f32[16,8,256]{2,1,0:T(8,128)}, f32[16,8,256]{2,1,0:T(8,128)S(1)}, u32[]{:S(2)}, u32[]{:S(2)}) collective-permute-start(f32[16,8,256]{2,1,0:T(8,128)} %velocity.1), channel_id=1, source_target_pairs={{0,4},{4,0},{8,12},{12,8},{1,5},{5,1},{9,13},{13,9},{2,6},{6,2},{1... | collective-permute-start | bytes 393224 | tf_op jit(solution)/shard_map/ppermute | solution.py:300
  0.5 2.5 %collective-permute-start.5 = (f32[16,8,256]{2,1,0:T(8,128)}, f32[16,8,256]{2,1,0:T(8,128)S(1)}, u32[]{:S(2)}, u32[]{:S(2)}) collective-permute-start(f32[16,8,256]{2,1,0:T(8,128)} %o_own.1), channel_id=1, source_target_pairs={{0,8},{4,12},{8,0},{12,4},{1,9},{5,13},{9,1},{13,5},{2,10},{6,14},... | collective-permute-start | bytes 393224 | tf_op jit(solution)/shard_map/ppermute | solution.py:303
  3.0 1.5 %collective-permute-start.4 = (f32[16,8,256]{2,1,0:T(8,128)}, f32[16,8,256]{2,1,0:T(8,128)S(1)}, u32[]{:S(2)}, u32[]{:S(2)}) collective-permute-start(f32[16,8,256]{2,1,0:T(8,128)} %o_own.1), channel_id=1, source_target_pairs={{0,16},{16,0},{1,17},{17,1},{2,18},{18,2},{3,19},{19,3},{4,20},{20... | collective-permute-start | bytes 393224 | tf_op jit(solution)/shard_map/ppermute | solution.py:306
  4.5 0.0 collective-permute-start.1
  4.5 0.0 collective-permute-done.v_sib.v_b
  4.5 0.0 copy-start
  4.5 0.9 %copy-done = f32[16,8,256]{2,1,0:T(8,128)S(1)} copy-done((f32[16,8,256]{2,1,0:T(8,128)S(1)}, f32[16,8,256]{2,1,0:T(8,128)}, u32[]{:S(2)}) %copy-start) | copy-done | bytes 131096
  5.4 0.2 shard_map.37
  5.6 3.0 %collective-permute-start.2 = (f32[16,128]{1,0:T(8,128)S(1)}, f32[16,128]{1,0:T(8,128)S(1)}, u32[]{:S(2)}, u32[]{:S(2)}) collective-permute-start(f32[16,128]{1,0:T(8,128)S(1)} %get-tuple-element.23), channel_id=1, source_target_pairs={{0,9},{1,8},{2,11},{3,10},{4,12},{5,14},{6,13},{7,15},{8,1},{9,0},... | collective-permute-start | bytes 24584 | tf_op jit(solution)/shard_map/ppermute | solution.py:311
  8.6 2.3 %collective-permute-start.3 = (f32[16,128]{1,0:T(8,128)S(1)}, f32[16,128]{1,0:T(8,128)S(1)}, u32[]{:S(2)}, u32[]{:S(2)}) collective-permute-start(f32[16,128]{1,0:T(8,128)S(1)} %get-tuple-element.24), channel_id=1, source_target_pairs={{0,1},{1,0},{2,3},{3,2},{4,4},{5,6},{6,5},{7,7},{8,9},{9,8},{10,11... | collective-permute-start | bytes 24584 | tf_op jit(solution)/shard_map/ppermute | solution.py:309
  11.0 0.0 collective-permute-done.5.o_far
  11.0 0.2 collective-permute-start.7
  11.2 0.0 collective-permute-done.4.u_own
  11.2 0.3 %collective-permute-done.1.u_far = f32[16,8,256]{2,1,0:T(8,128)S(1)} collective-permute-done((f32[16,8,256]{2,1,0:T(8,128)}, f32[16,8,256]{2,1,0:T(8,128)S(1)}, u32[]{:S(2)}, u32[]{:S(2)}) %collective-permute-start.1) | collective-permute-done | bytes 131104 | tf_op jit(solution)/shard_map/ppermute | solution.py:302
  11.5 0.0 collective-permute-done.2.h_a
  11.5 2.6 %collective-permute-done.3.h_a = f32[16,128]{1,0:T(8,128)S(1)} collective-permute-done((f32[16,128]{1,0:T(8,128)S(1)}, f32[16,128]{1,0:T(8,128)S(1)}, u32[]{:S(2)}, u32[]{:S(2)}) %collective-permute-start.3) | collective-permute-done | bytes 8224 | tf_op jit(solution)/shard_map/ppermute | solution.py:309
  14.2 0.0 collective-permute-start.6
  14.2 0.5 %collective-permute-start.9 = (f32[16,8,256]{2,1,0:T(8,128)}, f32[16,8,256]{2,1,0:T(8,128)S(1)}, u32[]{:S(2)}, u32[]{:S(2)}) collective-permute-start(f32[16,8,256]{2,1,0:T(8,128)} %o_own.1), channel_id=1, source_target_pairs={{0,4},{4,0},{8,12},{12,8},{1,5},{5,1},{9,13},{13,9},{2,6},{6,2},{1... | collective-permute-start | bytes 393224 | tf_op jit(solution)/shard_map/ppermute | solution.py:300
  14.7 0.0 collective-permute-start.10
  14.7 0.5 %collective-permute-start.12 = (f32[16,8,256]{2,1,0:T(8,128)S(1)}, f32[16,8,256]{2,1,0:T(8,128)S(1)}, u32[]{:S(2)}, u32[]{:S(2)}) collective-permute-start(f32[16,8,256]{2,1,0:T(8,128)S(1)} %collective-permute-done.1.u_far), channel_id=1, source_target_pairs={{0,4},{4,0},{8,12},{12,8},{1,5},{5,1},{9,13},{13,9},{2,6},{6,2},{1... | collective-permute-start | bytes 393224 | tf_op jit(solution)/shard_map/ppermute | solution.py:300
  15.2 0.1 collective-permute-done.7.v_a
  15.3 0.0 collective-permute-start.8
  15.3 0.0 collective-permute-done.6
  15.3 0.5 %collective-permute-start.11 = (f32[16,8,256]{2,1,0:T(8,128)S(1)}, f32[16,8,256]{2,1,0:T(8,128)S(1)}, u32[]{:S(2)}, u32[]{:S(2)}) collective-permute-start(f32[16,8,256]{2,1,0:T(8,128)S(1)} %collective-permute-done.5.o_far), channel_id=1, source_target_pairs={{0,4},{4,0},{8,12},{12,8},{1,5},{5,1},{9,13},{13,9},{2,6},{6,2},{1... | collective-permute-start | bytes 393224 | tf_op jit(solution)/shard_map/ppermute | solution.py:300
  15.8 0.0 copy-start.1
  15.8 0.6 %shard_map.42.lags_near = bf16[2,2,528,256]{3,2,1,0:T(8,128)(2,1)S(1)} custom-call(f32[16,8,256]{2,1,0:T(8,128)S(1)} %get-tuple-element.20.v_a, f32[16,8,256]{2,1,0:T(8,128)S(1)} %collective-permute-done.v_sib.v_b, f32[16,128]{1,0:T(8,128)S(1)} %collective-permute-done.3.h_a, f32[16,128]{1,0:T(8,128)S(1)} %get-tuple-element.36.h_b), custom_call_target="tpu_custom_call" | custom-call | flops 10000000 | bytes 3145728 | tf_op jit(solution)/shard_map/pallas_call | solution.py:228
  16.4 0.1 collective-permute-done.8.v_b
  16.6 0.0 copy-start.2
  16.6 0.6 %shard_map.43.lags_away = bf16[2,2,528,256]{3,2,1,0:T(8,128)(2,1)S(1)} custom-call(f32[8,8,256]{2,1,0:T(8,128)S(1)} %collective-permute-done.7.v_a, f32[8,8,256]{2,1,0:T(8,128)S(1)} %collective-permute-done.8.v_b, f32[16,128]{1,0:T(8,128)S(1)} %collective-permute-done.2.h_a, f32[16,128]{1,0:T(8,128)S(1)} %get-tuple-element.35.h_b), custom_call_target="tpu_custom_call" | custom-call | flops 10000000 | bytes 3145728 | tf_op jit(solution)/shard_map/pallas_call | solution.py:228
  17.2 0.0 collective-permute-done.9.o_sib
  17.2 0.0 collective-permute-done.10.u_sib
  17.2 0.0 collective-permute-done.12.u_far_sib
  17.2 0.0 collective-permute-done.11.o_far_sib
  17.2 0.0 copy-done.1
  17.2 0.2 shard_map.40
  17.4 0.0 copy-done.2
  17.5 1.5 %shard_map.44 = f32[2,40,256]{2,1,0:T(8,128)S(1)} custom-call(s32[1,8]{1,0:T(1,128)S(1)} %bitcast.11, bf16[2,2,528,256]{3,2,1,0:T(8,128)(2,1)S(1)} %shard_map.42.lags_near, bf16[2,2,528,256]{3,2,1,0:T(8,128)(2,1)S(1)} %shard_map.43.lags_away, bf16[24,2,16,256]{3,2,1,0:T(8,128)(2,1)S(1)} %get-tuple-element.33.high_p, ...), custom_call_target="tpu_custom_call" | custom-call | flops 830472192 | bytes 4194304 | tf_op jit(solution)/shard_map/pallas_call | solution.py:254
  19.0 1.6 %collective-permute-start.13 = (f32[2,40,256]{2,1,0:T(8,128)S(1)}, f32[2,40,256]{2,1,0:T(8,128)S(1)}, u32[]{:S(2)}, u32[]{:S(2)}) collective-permute-start(f32[2,40,256]{2,1,0:T(8,128)S(1)} %shard_map.44), channel_id=1, source_target_pairs={{0,1},{1,0},{2,3},{3,2},{4,5},{5,4},{6,7},{7,6},{8,9},{9,8},{10,11... | collective-permute-start | bytes 245768 | tf_op jit(solution)/shard_map/ppermute | solution.py:328
  20.7 0.3 %shard_map.45.lags_near = bf16[1,2,528,256]{3,2,1,0:T(8,128)(2,1)S(1)} custom-call(f32[16,8,256]{2,1,0:T(8,128)S(1)} %get-tuple-element.20.v_a, f32[16,8,256]{2,1,0:T(8,128)S(1)} %collective-permute-done.v_sib.v_b, f32[16,128]{1,0:T(8,128)S(1)} %collective-permute-done.3.h_a, f32[16,128]{1,0:T(8,128)S(1)} %get-tuple-element.36.h_b), custom_call_target="tpu_custom_call" | custom-call | flops 10000000 | bytes 3145728 | tf_op jit(solution)/shard_map/pallas_call | solution.py:228
  21.0 0.3 %shard_map.46.lags_away = bf16[1,2,528,256]{3,2,1,0:T(8,128)(2,1)S(1)} custom-call(f32[8,8,256]{2,1,0:T(8,128)S(1)} %collective-permute-done.7.v_a, f32[8,8,256]{2,1,0:T(8,128)S(1)} %collective-permute-done.8.v_b, f32[16,128]{1,0:T(8,128)S(1)} %collective-permute-done.2.h_a, f32[16,128]{1,0:T(8,128)S(1)} %get-tuple-element.35.h_b), custom_call_target="tpu_custom_call" | custom-call | flops 10000000 | bytes 3145728 | tf_op jit(solution)/shard_map/pallas_call | solution.py:228
  21.3 1.1 %shard_map.47 = f32[1,40,256]{2,1,0:T(8,128)S(1)} custom-call(s32[1,8]{1,0:T(1,128)S(1)} %bitcast.12, bf16[1,2,528,256]{3,2,1,0:T(8,128)(2,1)S(1)} %shard_map.45.lags_near, bf16[1,2,528,256]{3,2,1,0:T(8,128)(2,1)S(1)} %shard_map.46.lags_away, bf16[24,2,16,256]{3,2,1,0:T(8,128)(2,1)S(1)} %get-tuple-element.33.high_p, ...), custom_call_target="tpu_custom_call" | custom-call | flops 415236096 | bytes 4194304 | tf_op jit(solution)/shard_map/pallas_call | solution.py:254
  22.4 1.2 %collective-permute-done.13.refs_1_ = f32[2,40,256]{2,1,0:T(8,128)S(1)} collective-permute-done((f32[2,40,256]{2,1,0:T(8,128)S(1)}, f32[2,40,256]{2,1,0:T(8,128)S(1)}, u32[]{:S(2)}, u32[]{:S(2)}) %collective-permute-start.13) | collective-permute-done | bytes 81952 | tf_op jit(solution)/shard_map/ppermute | solution.py:328
  23.6 2.6 %collective-permute-start.14 = (f32[40,256]{1,0:T(8,128)S(1)}, f32[40,256]{1,0:T(8,128)S(1)}, u32[]{:S(2)}, u32[]{:S(2)}) collective-permute-start(f32[40,256]{1,0:T(8,128)S(1)} %fusion), channel_id=1, source_target_pairs={{0,2},{1,3},{2,0},{3,1},{4,6},{5,7},{6,4},{7,5},{8,10},{9,11},{10,... | collective-permute-start | bytes 122888 | tf_op jit(solution)/shard_map/ppermute | solution.py:334
  26.2 0.3 %shard_map.38.lags_near = bf16[1,2,528,256]{3,2,1,0:T(8,128)(2,1)S(1)} custom-call(f32[16,8,256]{2,1,0:T(8,128)S(1)} %get-tuple-element.20.v_a, f32[16,8,256]{2,1,0:T(8,128)S(1)} %collective-permute-done.v_sib.v_b, f32[16,128]{1,0:T(8,128)S(1)} %collective-permute-done.3.h_a, f32[16,128]{1,0:T(8,128)S(1)} %get-tuple-element.36.h_b), custom_call_target="tpu_custom_call" | custom-call | flops 10000000 | bytes 3145728 | tf_op jit(solution)/shard_map/pallas_call | solution.py:228
  26.5 0.3 %shard_map.39.lags_away = bf16[1,2,528,256]{3,2,1,0:T(8,128)(2,1)S(1)} custom-call(f32[8,8,256]{2,1,0:T(8,128)S(1)} %collective-permute-done.7.v_a, f32[8,8,256]{2,1,0:T(8,128)S(1)} %collective-permute-done.8.v_b, f32[16,128]{1,0:T(8,128)S(1)} %collective-permute-done.2.h_a, f32[16,128]{1,0:T(8,128)S(1)} %get-tuple-element.35.h_b), custom_call_target="tpu_custom_call" | custom-call | flops 10000000 | bytes 3145728 | tf_op jit(solution)/shard_map/pallas_call | solution.py:228
  26.8 1.1 %shard_map.41.refs_0_ = f32[1,40,256]{2,1,0:T(8,128)S(1)} custom-call(s32[1,8]{1,0:T(1,128)S(1)} %bitcast.13, bf16[1,2,528,256]{3,2,1,0:T(8,128)(2,1)S(1)} %shard_map.38.lags_near, bf16[1,2,528,256]{3,2,1,0:T(8,128)(2,1)S(1)} %shard_map.39.lags_away, bf16[24,2,16,256]{3,2,1,0:T(8,128)(2,1)S(1)} %get-tuple-element.33.high_p, ...), custom_call_target="tpu_custom_call" | custom-call | flops 415236096 | bytes 4194304 | tf_op jit(solution)/shard_map/pallas_call | solution.py:254
  27.9 0.6 %collective-permute-done.14.refs_2_ = f32[40,256]{1,0:T(8,128)S(1)} collective-permute-done((f32[40,256]{1,0:T(8,128)S(1)}, f32[40,256]{1,0:T(8,128)S(1)}, u32[]{:S(2)}, u32[]{:S(2)}) %collective-permute-start.14) | collective-permute-done | bytes 40992 | tf_op jit(solution)/shard_map/ppermute | solution.py:334
  28.5 0.8 %shard_map.48 = f32[1,8,1056]{2,1,0:T(8,128)} custom-call(f32[1,40,256]{2,1,0:T(8,128)S(1)} %shard_map.41.refs_0_, f32[2,40,256]{2,1,0:T(8,128)S(1)} %collective-permute-done.13.refs_1_, f32[40,256]{1,0:T(8,128)S(1)} %collective-permute-done.14.refs_2_), custom_call_target="tpu_custom_call" | custom-call | flops 1000000 | bytes 262144 | tf_op jit(solution)/shard_map/pallas_call | solution.py:269
  (3 shorter events, 0.0 us)
Async XLA Ops:
  0.0 4.5 %collective-permute-start = (f32[16,8,256]{2,1,0:T(8,128)}, f32[16,8,256]{2,1,0:T(8,128)S(1)}, u32[]{:S(2)}, u32[]{:S(2)}) collective-permute-start(f32[16,8,256]{2,1,0:T(8,128)} %velocity.1), channel_id=1, source_target_pairs={{0,4},{4,0},{8,12},{12,8},{1,5},{5,1},{9,13},{13,9},{2,6},{6,2},{1... | collective-permute-start | bytes 393224 | tf_op jit(solution)/shard_map/ppermute | solution.py:300
  0.5 10.5 %collective-permute-start.5 = (f32[16,8,256]{2,1,0:T(8,128)}, f32[16,8,256]{2,1,0:T(8,128)S(1)}, u32[]{:S(2)}, u32[]{:S(2)}) collective-permute-start(f32[16,8,256]{2,1,0:T(8,128)} %o_own.1), channel_id=1, source_target_pairs={{0,8},{4,12},{8,0},{12,4},{1,9},{5,13},{9,1},{13,5},{2,10},{6,14},... | collective-permute-start | bytes 393224 | tf_op jit(solution)/shard_map/ppermute | solution.py:303
  3.0 8.2 %collective-permute-start.4 = (f32[16,8,256]{2,1,0:T(8,128)}, f32[16,8,256]{2,1,0:T(8,128)S(1)}, u32[]{:S(2)}, u32[]{:S(2)}) collective-permute-start(f32[16,8,256]{2,1,0:T(8,128)} %o_own.1), channel_id=1, source_target_pairs={{0,16},{16,0},{1,17},{17,1},{2,18},{18,2},{3,19},{19,3},{4,20},{20... | collective-permute-start | bytes 393224 | tf_op jit(solution)/shard_map/ppermute | solution.py:306
  4.5 7.1 %collective-permute-start.1 = (f32[16,8,256]{2,1,0:T(8,128)}, f32[16,8,256]{2,1,0:T(8,128)S(1)}, u32[]{:S(2)}, u32[]{:S(2)}) collective-permute-start(f32[16,8,256]{2,1,0:T(8,128)} %o_own.1), channel_id=1, source_target_pairs={{0,24},{4,28},{8,16},{12,20},{16,8},{20,12},{24,0},{28,4},{1,25},{... | collective-permute-start | bytes 393224 | tf_op jit(solution)/shard_map/ppermute | solution.py:302
  4.5 0.9 %copy-start = (f32[16,8,256]{2,1,0:T(8,128)S(1)}, f32[16,8,256]{2,1,0:T(8,128)}, u32[]{:S(2)}) copy-start(f32[16,8,256]{2,1,0:T(8,128)} %velocity.1) | copy-start | bytes 393220
  5.6 5.9 %collective-permute-start.2 = (f32[16,128]{1,0:T(8,128)S(1)}, f32[16,128]{1,0:T(8,128)S(1)}, u32[]{:S(2)}, u32[]{:S(2)}) collective-permute-start(f32[16,128]{1,0:T(8,128)S(1)} %get-tuple-element.23), channel_id=1, source_target_pairs={{0,9},{1,8},{2,11},{3,10},{4,12},{5,14},{6,13},{7,15},{8,1},{9,0},... | collective-permute-start | bytes 24584 | tf_op jit(solution)/shard_map/ppermute | solution.py:311
  8.6 5.5 %collective-permute-start.3 = (f32[16,128]{1,0:T(8,128)S(1)}, f32[16,128]{1,0:T(8,128)S(1)}, u32[]{:S(2)}, u32[]{:S(2)}) collective-permute-start(f32[16,128]{1,0:T(8,128)S(1)} %get-tuple-element.24), channel_id=1, source_target_pairs={{0,1},{1,0},{2,3},{3,2},{4,4},{5,6},{6,5},{7,7},{8,9},{9,8},{10,11... | collective-permute-start | bytes 24584 | tf_op jit(solution)/shard_map/ppermute | solution.py:309
  11.0 4.3 %collective-permute-start.7 = (f32[8,8,256]{2,1,0:T(8,128)S(1)}, f32[8,8,256]{2,1,0:T(8,128)S(1)}, u32[]{:S(2)}, u32[]{:S(2)}) collective-permute-start(f32[8,8,256]{2,1,0:T(8,128)S(1)} %get-tuple-element.27), channel_id=1, source_target_pairs={{0,8},{4,12},{8,0},{12,4},{1,9},{5,13},{9,1},{13,5},{2,10},{6,14},... | collective-permute-start | bytes 196616 | tf_op jit(solution)/shard_map/ppermute | solution.py:310
  14.2 1.2 %collective-permute-start.6 = (f32[2,16,128]{2,1,0:T(8,128)S(1)}, f32[2,16,128]{2,1,0:T(8,128)S(1)}, u32[]{:S(2)}, u32[]{:S(2)}) collective-permute-start(f32[2,16,128]{2,1,0:T(8,128)S(1)} %pad_maximum_fusion), channel_id=1, source_target_pairs={{0,4},{4,0},{8,12},{12,8},{1,5},{5,1},{9,13},{13,9},{2,6},{6,2},{1... | collective-permute-start | bytes 49160 | tf_op jit(solution)/shard_map/ppermute | solution.py:300
  14.2 3.0 %collective-permute-start.9 = (f32[16,8,256]{2,1,0:T(8,128)}, f32[16,8,256]{2,1,0:T(8,128)S(1)}, u32[]{:S(2)}, u32[]{:S(2)}) collective-permute-start(f32[16,8,256]{2,1,0:T(8,128)} %o_own.1), channel_id=1, source_target_pairs={{0,4},{4,0},{8,12},{12,8},{1,5},{5,1},{9,13},{13,9},{2,6},{6,2},{1... | collective-permute-start | bytes 393224 | tf_op jit(solution)/shard_map/ppermute | solution.py:300
  14.7 2.5 %collective-permute-start.10 = (f32[16,8,256]{2,1,0:T(8,128)S(1)}, f32[16,8,256]{2,1,0:T(8,128)S(1)}, u32[]{:S(2)}, u32[]{:S(2)}) collective-permute-start(f32[16,8,256]{2,1,0:T(8,128)S(1)} %collective-permute-done.4.u_own), channel_id=1, source_target_pairs={{0,4},{4,0},{8,12},{12,8},{1,5},{5,1},{9,13},{13,9},{2,6},{6,2},{1... | collective-permute-start | bytes 393224 | tf_op jit(solution)/shard_map/ppermute | solution.py:300
  14.7 2.5 %collective-permute-start.12 = (f32[16,8,256]{2,1,0:T(8,128)S(1)}, f32[16,8,256]{2,1,0:T(8,128)S(1)}, u32[]{:S(2)}, u32[]{:S(2)}) collective-permute-start(f32[16,8,256]{2,1,0:T(8,128)S(1)} %collective-permute-done.1.u_far), channel_id=1, source_target_pairs={{0,4},{4,0},{8,12},{12,8},{1,5},{5,1},{9,13},{13,9},{2,6},{6,2},{1... | collective-permute-start | bytes 393224 | tf_op jit(solution)/shard_map/ppermute | solution.py:300
  15.3 1.3 %collective-permute-start.8 = (f32[8,8,256]{2,1,0:T(8,128)S(1)}, f32[8,8,256]{2,1,0:T(8,128)S(1)}, u32[]{:S(2)}, u32[]{:S(2)}) collective-permute-start(f32[8,8,256]{2,1,0:T(8,128)S(1)} %collective-permute-done.7.v_a), channel_id=1, source_target_pairs={{0,4},{4,0},{8,12},{12,8},{1,5},{5,1},{9,13},{13,9},{2,6},{6,2},{1... | collective-permute-start | bytes 196616 | tf_op jit(solution)/shard_map/ppermute | solution.py:300
  15.3 1.9 %collective-permute-start.11 = (f32[16,8,256]{2,1,0:T(8,128)S(1)}, f32[16,8,256]{2,1,0:T(8,128)S(1)}, u32[]{:S(2)}, u32[]{:S(2)}) collective-permute-start(f32[16,8,256]{2,1,0:T(8,128)S(1)} %collective-permute-done.5.o_far), channel_id=1, source_target_pairs={{0,4},{4,0},{8,12},{12,8},{1,5},{5,1},{9,13},{13,9},{2,6},{6,2},{1... | collective-permute-start | bytes 393224 | tf_op jit(solution)/shard_map/ppermute | solution.py:300
  15.8 1.4 %copy-start.1 = (f32[16,8,256]{2,1,0:T(8,128)S(1)}, f32[16,8,256]{2,1,0:T(8,128)}, u32[]{:S(2)}) copy-start(f32[16,8,256]{2,1,0:T(8,128)} %o_own.1) | copy-start | bytes 393220
  16.6 0.9 %copy-start.2 = (s32[8]{0:T(128)S(1)}, s32[8]{0:T(128)}, u32[]{:S(2)}) copy-start(s32[8]{0:T(128)} %param.5) | copy-start | bytes 100
  19.0 4.6 %collective-permute-start.13 = (f32[2,40,256]{2,1,0:T(8,128)S(1)}, f32[2,40,256]{2,1,0:T(8,128)S(1)}, u32[]{:S(2)}, u32[]{:S(2)}) collective-permute-start(f32[2,40,256]{2,1,0:T(8,128)S(1)} %shard_map.44), channel_id=1, source_target_pairs={{0,1},{1,0},{2,3},{3,2},{4,5},{5,4},{6,7},{7,6},{8,9},{9,8},{10,11... | collective-permute-start | bytes 245768 | tf_op jit(solution)/shard_map/ppermute | solution.py:328
  23.6 4.9 %collective-permute-start.14 = (f32[40,256]{1,0:T(8,128)S(1)}, f32[40,256]{1,0:T(8,128)S(1)}, u32[]{:S(2)}, u32[]{:S(2)}) collective-permute-start(f32[40,256]{1,0:T(8,128)S(1)} %fusion), channel_id=1, source_target_pairs={{0,2},{1,3},{2,0},{3,1},{4,6},{5,7},{6,4},{7,5},{8,10},{9,11},{10,... | collective-permute-start | bytes 122888 | tf_op jit(solution)/shard_map/ppermute | solution.py:334

commit v7 on v6

--- a/solution.py
+++ b/solution.py
@@ -147,7 +147,11 @@
             left += [lags[at, 0], lags[at, 0], lags[at, 1]]
         left = jnp.concatenate(left, axis=1)
         prod[i] = lax.dot_general(left, right, (((1,), (1,)), ((), ())), preferred_element_type=F32)
-        out[i] = diagonals(prod.at[i], rows, azim, count)
+        sums = diagonals(prod.at[i], rows, azim, count)
+        out[i * MAIN : (i + 1) * MAIN] = sums[:MAIN]
+        end = sums[MAIN:]
+        tail = end if i == 0 else jnp.where(lax.broadcasted_iota(jnp.int32, end.shape, 0) < i, tail, end)
+    out[len(flips) * MAIN :] = tail
 
 
 def diagonals(prod, rows, azim, count):
@@ -178,7 +182,9 @@
 
 def close_kernel(factor, count, azim, *refs):
     mine, first, second, out = refs
-    total = (mine[0] + first[0] + second[...]) * factor
+    total = (mine[:MAIN] + first[:MAIN] + second[:MAIN]) * factor
+    last = 2 * MAIN
+    tail = (mine[MAIN : MAIN + 1] + first[last : last + 1] + second[MAIN + 1 : MAIN + 2]) * factor
     groups = LANES // azim
     lane = lax.broadcasted_iota(jnp.int32, (count, LANES), 1) // azim
     sub = lax.broadcasted_iota(jnp.int32, (count, LANES), 0)
@@ -190,7 +196,8 @@
                 continue
             x = jnp.zeros((count, LANES), F32)
             for part in range(count // groups):
-                line = total[tau : tau + 1, part * LANES : (part + 1) * LANES]
+                source = total[tau : tau + 1] if tau < MAIN else tail
+                line = source[:, part * LANES : (part + 1) * LANES]
                 x = jnp.where(sub // groups == part, jnp.broadcast_to(line, (count, LANES)), x)
             moved = x
             for s in range(groups):
@@ -255,7 +262,7 @@
         functools.partial(product_kernel, flips),
         in_specs=[VMEM] * 5,
         out_specs=VMEM,
-        out_shape=jax.ShapeDtypeStruct((stations, MAIN + 8, columns), F32),
+        out_shape=jax.ShapeDtypeStruct((stations * MAIN + 8, columns), F32),
         scratch_shapes=[pltpu.VMEM((stations, height, columns), F32)],
         compiler_params=pltpu.CompilerParams(vmem_limit_bytes=24 << 20),
         cost_estimate=pl.CostEstimate(
@@ -331,7 +338,7 @@
         products((flip,), offsets, lag_rows((flip,), False, *own), lag_rows((flip,), True, *series), high_p, low_p)
         for flip in (2, 0)
     ]
-    second = lax.ppermute(keep[0][0] + first[1], "ta", [(i, i ^ 2) for i in range(ta_n)])
+    second = lax.ppermute(keep[0] + first[MAIN:], "ta", [(i, i ^ 2) for i in range(ta_n)])
     return close([keep[1], first, second], factor, offsets.shape[1], azim)
 
 

time: 29.5 us -> 29.3 us (level)
  no operation moved by 1% of the time
where the time goes in v7:
time: 29.3 us; the launch traced here: 29.1 us
  starting transfers between devices  15.8 us (54%)
  Pallas kernels  7.34 us (25%)
  waiting for transfers between devices  4.92 us (17%)
  local copies, waits for them, and re-layouts  0.91 us (3%)
    pallas_call x3, Pallas kernels, products(): pl.pallas_call(functools.partial(product_kernel, flips), in_specs=[VMEM]...  3.68 us
    ppermute x1, starting transfers between devices, shards(): h_away = lax.ppermute(ends_away, ('az', 'ta'), in_time_across)  3.03 us
    ppermute x1, waiting for transfers between devices, shards(): h_near = lax.ppermute(ends_near, ('az', 'ta'), in_time)  2.62 us
    ppermute x1, starting transfers between devices, shards(): lax.ppermute(keep[0] + first[MAIN:], 'ta', [(i, i ^ 2) for i in range(ta_...  2.59 us
    ppermute x1, starting transfers between devices, shards(): far = lax.ppermute(pressure, 'az', across)  2.52 us
    pallas_call x6, Pallas kernels, lag_rows(): pl.pallas_call(functools.partial(lag_kernel, flips, away), in_specs=[VMEM...  2.47 us
    ppermute x1, starting transfers between devices, shards(): h_near = lax.ppermute(ends_near, ('az', 'ta'), in_time)  2.35 us
    ppermute x7, starting transfers between devices, shards(): to_sibling = lambda x: lax.ppermute(x, 'az', sibling)  1.96 us
  transfers between devices with their start and end apart: 15, of which 6 were waited for; matrix products, arithmetic and copies ran while one was open for 0% of the time, Pallas kernels for 16%

profile of v7, /device:TPU:0, one launch (start us, length us, event | category | flops | bytes accessed | tf_op | source)
XLA Modules:
  0.0 29.1 jit_solution(16287285186968161546)
XLA Ops:
  0.0 0.5 %collective-permute-start = (f32[16,8,256]{2,1,0:T(8,128)}, f32[16,8,256]{2,1,0:T(8,128)S(1)}, u32[]{:S(2)}, u32[]{:S(2)}) collective-permute-start(f32[16,8,256]{2,1,0:T(8,128)} %velocity.1), channel_id=1, source_target_pairs={{0,4},{4,0},{8,12},{12,8},{1,5},{5,1},{9,13},{13,9},{2,6},{6,2},{1... | collective-permute-start | bytes 393224 | tf_op jit(solution)/shard_map/ppermute | solution.py:307
  0.5 2.5 %collective-permute-start.5 = (f32[16,8,256]{2,1,0:T(8,128)}, f32[16,8,256]{2,1,0:T(8,128)S(1)}, u32[]{:S(2)}, u32[]{:S(2)}) collective-permute-start(f32[16,8,256]{2,1,0:T(8,128)} %o_own.1), channel_id=1, source_target_pairs={{0,8},{4,12},{8,0},{12,4},{1,9},{5,13},{9,1},{13,5},{2,10},{6,14},... | collective-permute-start | bytes 393224 | tf_op jit(solution)/shard_map/ppermute | solution.py:310
  3.0 1.5 %collective-permute-start.4 = (f32[16,8,256]{2,1,0:T(8,128)}, f32[16,8,256]{2,1,0:T(8,128)S(1)}, u32[]{:S(2)}, u32[]{:S(2)}) collective-permute-start(f32[16,8,256]{2,1,0:T(8,128)} %o_own.1), channel_id=1, source_target_pairs={{0,16},{16,0},{1,17},{17,1},{2,18},{18,2},{3,19},{19,3},{4,20},{20... | collective-permute-start | bytes 393224 | tf_op jit(solution)/shard_map/ppermute | solution.py:313
  4.5 0.0 collective-permute-start.1
  4.5 0.0 collective-permute-done.v_sib.v_b
  4.5 0.0 copy-start
  4.5 0.9 %copy-done = f32[16,8,256]{2,1,0:T(8,128)S(1)} copy-done((f32[16,8,256]{2,1,0:T(8,128)S(1)}, f32[16,8,256]{2,1,0:T(8,128)}, u32[]{:S(2)}) %copy-start) | copy-done | bytes 131096
  5.4 0.2 shard_map.37
  5.6 3.0 %collective-permute-start.2 = (f32[16,128]{1,0:T(8,128)S(1)}, f32[16,128]{1,0:T(8,128)S(1)}, u32[]{:S(2)}, u32[]{:S(2)}) collective-permute-start(f32[16,128]{1,0:T(8,128)S(1)} %get-tuple-element.23), channel_id=1, source_target_pairs={{0,9},{1,8},{2,11},{3,10},{4,12},{5,14},{6,13},{7,15},{8,1},{9,0},... | collective-permute-start | bytes 24584 | tf_op jit(solution)/shard_map/ppermute | solution.py:318
  8.6 2.3 %collective-permute-start.3 = (f32[16,128]{1,0:T(8,128)S(1)}, f32[16,128]{1,0:T(8,128)S(1)}, u32[]{:S(2)}, u32[]{:S(2)}) collective-permute-start(f32[16,128]{1,0:T(8,128)S(1)} %get-tuple-element.24), channel_id=1, source_target_pairs={{0,1},{1,0},{2,3},{3,2},{4,4},{5,6},{6,5},{7,7},{8,9},{9,8},{10,11... | collective-permute-start | bytes 24584 | tf_op jit(solution)/shard_map/ppermute | solution.py:316
  11.0 0.0 collective-permute-done.5.o_far
  11.0 0.2 collective-permute-start.7
  11.2 0.0 collective-permute-done.4.u_own
  11.2 0.3 %collective-permute-done.1.u_far = f32[16,8,256]{2,1,0:T(8,128)S(1)} collective-permute-done((f32[16,8,256]{2,1,0:T(8,128)}, f32[16,8,256]{2,1,0:T(8,128)S(1)}, u32[]{:S(2)}, u32[]{:S(2)}) %collective-permute-start.1) | collective-permute-done | bytes 131104 | tf_op jit(solution)/shard_map/ppermute | solution.py:309
  11.5 0.0 collective-permute-done.2.h_a
  11.5 2.6 %collective-permute-done.3.h_a = f32[16,128]{1,0:T(8,128)S(1)} collective-permute-done((f32[16,128]{1,0:T(8,128)S(1)}, f32[16,128]{1,0:T(8,128)S(1)}, u32[]{:S(2)}, u32[]{:S(2)}) %collective-permute-start.3) | collective-permute-done | bytes 8224 | tf_op jit(solution)/shard_map/ppermute | solution.py:316
  14.2 0.0 collective-permute-start.6
  14.2 0.5 %collective-permute-start.9 = (f32[16,8,256]{2,1,0:T(8,128)}, f32[16,8,256]{2,1,0:T(8,128)S(1)}, u32[]{:S(2)}, u32[]{:S(2)}) collective-permute-start(f32[16,8,256]{2,1,0:T(8,128)} %o_own.1), channel_id=1, source_target_pairs={{0,4},{4,0},{8,12},{12,8},{1,5},{5,1},{9,13},{13,9},{2,6},{6,2},{1... | collective-permute-start | bytes 393224 | tf_op jit(solution)/shard_map/ppermute | solution.py:307
  14.7 0.0 collective-permute-start.10
  14.7 0.5 %collective-permute-start.12 = (f32[16,8,256]{2,1,0:T(8,128)S(1)}, f32[16,8,256]{2,1,0:T(8,128)S(1)}, u32[]{:S(2)}, u32[]{:S(2)}) collective-permute-start(f32[16,8,256]{2,1,0:T(8,128)S(1)} %collective-permute-done.1.u_far), channel_id=1, source_target_pairs={{0,4},{4,0},{8,12},{12,8},{1,5},{5,1},{9,13},{13,9},{2,6},{6,2},{1... | collective-permute-start | bytes 393224 | tf_op jit(solution)/shard_map/ppermute | solution.py:307
  15.2 0.1 collective-permute-done.7.v_a
  15.3 0.0 collective-permute-start.8
  15.3 0.0 collective-permute-done.6
  15.3 0.5 %collective-permute-start.11 = (f32[16,8,256]{2,1,0:T(8,128)S(1)}, f32[16,8,256]{2,1,0:T(8,128)S(1)}, u32[]{:S(2)}, u32[]{:S(2)}) collective-permute-start(f32[16,8,256]{2,1,0:T(8,128)S(1)} %collective-permute-done.5.o_far), channel_id=1, source_target_pairs={{0,4},{4,0},{8,12},{12,8},{1,5},{5,1},{9,13},{13,9},{2,6},{6,2},{1... | collective-permute-start | bytes 393224 | tf_op jit(solution)/shard_map/ppermute | solution.py:307
  15.8 0.0 copy-start.1
  15.8 0.6 %shard_map.42.lags_near = bf16[2,2,528,256]{3,2,1,0:T(8,128)(2,1)S(1)} custom-call(f32[16,8,256]{2,1,0:T(8,128)S(1)} %get-tuple-element.20.v_a, f32[16,8,256]{2,1,0:T(8,128)S(1)} %collective-permute-done.v_sib.v_b, f32[16,128]{1,0:T(8,128)S(1)} %collective-permute-done.3.h_a, f32[16,128]{1,0:T(8,128)S(1)} %get-tuple-element.36.h_b), custom_call_target="tpu_custom_call" | custom-call | flops 10000000 | bytes 3145728 | tf_op jit(solution)/shard_map/pallas_call | solution.py:235
  16.4 0.1 collective-permute-done.8.v_b
  16.6 0.0 copy-start.2
  16.6 0.6 %shard_map.43.lags_away = bf16[2,2,528,256]{3,2,1,0:T(8,128)(2,1)S(1)} custom-call(f32[8,8,256]{2,1,0:T(8,128)S(1)} %collective-permute-done.7.v_a, f32[8,8,256]{2,1,0:T(8,128)S(1)} %collective-permute-done.8.v_b, f32[16,128]{1,0:T(8,128)S(1)} %collective-permute-done.2.h_a, f32[16,128]{1,0:T(8,128)S(1)} %get-tuple-element.35.h_b), custom_call_target="tpu_custom_call" | custom-call | flops 10000000 | bytes 3145728 | tf_op jit(solution)/shard_map/pallas_call | solution.py:235
  17.2 0.0 collective-permute-done.9.o_sib
  17.2 0.0 collective-permute-done.10.u_sib
  17.2 0.0 collective-permute-done.12.u_far_sib
  17.2 0.0 collective-permute-done.11.o_far_sib
  17.2 0.0 copy-done.1
  17.2 0.2 shard_map.40
  17.5 0.0 copy-done.2
  17.5 1.6 %shard_map.44 = f32[72,256]{1,0:T(8,128)S(1)} custom-call(s32[1,8]{1,0:T(1,128)S(1)} %bitcast.9, bf16[2,2,528,256]{3,2,1,0:T(8,128)(2,1)S(1)} %shard_map.42.lags_near, bf16[2,2,528,256]{3,2,1,0:T(8,128)(2,1)S(1)} %shard_map.43.lags_away, bf16[24,2,16,256]{3,2,1,0:T(8,128)(2,1)S(1)} %get-tuple-element.33.high_p, ...), custom_call_target="tpu_custom_call" | custom-call | flops 830472192 | bytes 4194304 | tf_op jit(solution)/shard_map/pallas_call | solution.py:261
  19.0 1.6 %collective-permute-start.13 = (f32[72,256]{1,0:T(8,128)S(1)}, f32[72,256]{1,0:T(8,128)S(1)}, u32[]{:S(2)}, u32[]{:S(2)}) collective-permute-start(f32[72,256]{1,0:T(8,128)S(1)} %shard_map.44), channel_id=1, source_target_pairs={{0,1},{1,0},{2,3},{3,2},{4,5},{5,4},{6,7},{7,6},{8,9},{9,8},{10,11... | collective-permute-start | bytes 221192 | tf_op jit(solution)/shard_map/ppermute | solution.py:335
  20.7 0.3 %shard_map.45.lags_near = bf16[1,2,528,256]{3,2,1,0:T(8,128)(2,1)S(1)} custom-call(f32[16,8,256]{2,1,0:T(8,128)S(1)} %get-tuple-element.20.v_a, f32[16,8,256]{2,1,0:T(8,128)S(1)} %collective-permute-done.v_sib.v_b, f32[16,128]{1,0:T(8,128)S(1)} %collective-permute-done.3.h_a, f32[16,128]{1,0:T(8,128)S(1)} %get-tuple-element.36.h_b), custom_call_target="tpu_custom_call" | custom-call | flops 10000000 | bytes 3145728 | tf_op jit(solution)/shard_map/pallas_call | solution.py:235
  21.0 0.3 %shard_map.46.lags_away = bf16[1,2,528,256]{3,2,1,0:T(8,128)(2,1)S(1)} custom-call(f32[8,8,256]{2,1,0:T(8,128)S(1)} %collective-permute-done.7.v_a, f32[8,8,256]{2,1,0:T(8,128)S(1)} %collective-permute-done.8.v_b, f32[16,128]{1,0:T(8,128)S(1)} %collective-permute-done.2.h_a, f32[16,128]{1,0:T(8,128)S(1)} %get-tuple-element.35.h_b), custom_call_target="tpu_custom_call" | custom-call | flops 10000000 | bytes 3145728 | tf_op jit(solution)/shard_map/pallas_call | solution.py:235
  21.3 1.1 %shard_map.47 = f32[40,256]{1,0:T(8,128)S(1)} custom-call(s32[1,8]{1,0:T(1,128)S(1)} %bitcast.10, bf16[1,2,528,256]{3,2,1,0:T(8,128)(2,1)S(1)} %shard_map.45.lags_near, bf16[1,2,528,256]{3,2,1,0:T(8,128)(2,1)S(1)} %shard_map.46.lags_away, bf16[24,2,16,256]{3,2,1,0:T(8,128)(2,1)S(1)} %get-tuple-element.33.high_p, ...), custom_call_target="tpu_custom_call" | custom-call | flops 415236096 | bytes 4194304 | tf_op jit(solution)/shard_map/pallas_call | solution.py:261
  22.4 1.1 %collective-permute-done.13.refs_1_ = f32[72,256]{1,0:T(8,128)S(1)} collective-permute-done((f32[72,256]{1,0:T(8,128)S(1)}, f32[72,256]{1,0:T(8,128)S(1)}, u32[]{:S(2)}, u32[]{:S(2)}) %collective-permute-start.13) | collective-permute-done | bytes 73760 | tf_op jit(solution)/shard_map/ppermute | solution.py:335
  23.4 2.6 %collective-permute-start.14 = (f32[40,256]{1,0:T(8,128)S(1)}, f32[40,256]{1,0:T(8,128)S(1)}, u32[]{:S(2)}, u32[]{:S(2)}) collective-permute-start(f32[40,256]{1,0:T(8,128)S(1)} %slice_add_fusion), channel_id=1, source_target_pairs={{0,2},{1,3},{2,0},{3,1},{4,6},{5,7},{6,4},{7,5},{8,10},{9,11},{10,... | collective-permute-start | bytes 122888 | tf_op jit(solution)/shard_map/ppermute | solution.py:341
  26.0 0.3 %shard_map.38.lags_near = bf16[1,2,528,256]{3,2,1,0:T(8,128)(2,1)S(1)} custom-call(f32[16,8,256]{2,1,0:T(8,128)S(1)} %get-tuple-element.20.v_a, f32[16,8,256]{2,1,0:T(8,128)S(1)} %collective-permute-done.v_sib.v_b, f32[16,128]{1,0:T(8,128)S(1)} %collective-permute-done.3.h_a, f32[16,128]{1,0:T(8,128)S(1)} %get-tuple-element.36.h_b), custom_call_target="tpu_custom_call" | custom-call | flops 10000000 | bytes 3145728 | tf_op jit(solution)/shard_map/pallas_call | solution.py:235
  26.4 0.3 %shard_map.39.lags_away = bf16[1,2,528,256]{3,2,1,0:T(8,128)(2,1)S(1)} custom-call(f32[8,8,256]{2,1,0:T(8,128)S(1)} %collective-permute-done.7.v_a, f32[8,8,256]{2,1,0:T(8,128)S(1)} %collective-permute-done.8.v_b, f32[16,128]{1,0:T(8,128)S(1)} %collective-permute-done.2.h_a, f32[16,128]{1,0:T(8,128)S(1)} %get-tuple-element.35.h_b), custom_call_target="tpu_custom_call" | custom-call | flops 10000000 | bytes 3145728 | tf_op jit(solution)/shard_map/pallas_call | solution.py:235
  26.7 1.1 %shard_map.41.refs_0_ = f32[40,256]{1,0:T(8,128)S(1)} custom-call(s32[1,8]{1,0:T(1,128)S(1)} %bitcast.11, bf16[1,2,528,256]{3,2,1,0:T(8,128)(2,1)S(1)} %shard_map.38.lags_near, bf16[1,2,528,256]{3,2,1,0:T(8,128)(2,1)S(1)} %shard_map.39.lags_away, bf16[24,2,16,256]{3,2,1,0:T(8,128)(2,1)S(1)} %get-tuple-element.33.high_p, ...), custom_call_target="tpu_custom_call" | custom-call | flops 415236096 | bytes 4194304 | tf_op jit(solution)/shard_map/pallas_call | solution.py:261
  27.8 0.6 %collective-permute-done.14.refs_2_ = f32[40,256]{1,0:T(8,128)S(1)} collective-permute-done((f32[40,256]{1,0:T(8,128)S(1)}, f32[40,256]{1,0:T(8,128)S(1)}, u32[]{:S(2)}, u32[]{:S(2)}) %collective-permute-start.14) | collective-permute-done | bytes 40992 | tf_op jit(solution)/shard_map/ppermute | solution.py:341
  28.4 0.8 %shard_map.48 = f32[1,8,1056]{2,1,0:T(8,128)} custom-call(f32[40,256]{1,0:T(8,128)S(1)} %shard_map.41.refs_0_, f32[72,256]{1,0:T(8,128)S(1)} %collective-permute-done.13.refs_1_, f32[40,256]{1,0:T(8,128)S(1)} %collective-permute-done.14.refs_2_), custom_call_target="tpu_custom_call" | custom-call | flops 1000000 | bytes 262144 | tf_op jit(solution)/shard_map/pallas_call | solution.py:276
  (3 shorter events, 0.0 us)
Async XLA Ops:
  0.0 4.5 %collective-permute-start = (f32[16,8,256]{2,1,0:T(8,128)}, f32[16,8,256]{2,1,0:T(8,128)S(1)}, u32[]{:S(2)}, u32[]{:S(2)}) collective-permute-start(f32[16,8,256]{2,1,0:T(8,128)} %velocity.1), channel_id=1, source_target_pairs={{0,4},{4,0},{8,12},{12,8},{1,5},{5,1},{9,13},{13,9},{2,6},{6,2},{1... | collective-permute-start | bytes 393224 | tf_op jit(solution)/shard_map/ppermute | solution.py:307
  0.5 10.5 %collective-permute-start.5 = (f32[16,8,256]{2,1,0:T(8,128)}, f32[16,8,256]{2,1,0:T(8,128)S(1)}, u32[]{:S(2)}, u32[]{:S(2)}) collective-permute-start(f32[16,8,256]{2,1,0:T(8,128)} %o_own.1), channel_id=1, source_target_pairs={{0,8},{4,12},{8,0},{12,4},{1,9},{5,13},{9,1},{13,5},{2,10},{6,14},... | collective-permute-start | bytes 393224 | tf_op jit(solution)/shard_map/ppermute | solution.py:310
  3.0 8.2 %collective-permute-start.4 = (f32[16,8,256]{2,1,0:T(8,128)}, f32[16,8,256]{2,1,0:T(8,128)S(1)}, u32[]{:S(2)}, u32[]{:S(2)}) collective-permute-start(f32[16,8,256]{2,1,0:T(8,128)} %o_own.1), channel_id=1, source_target_pairs={{0,16},{16,0},{1,17},{17,1},{2,18},{18,2},{3,19},{19,3},{4,20},{20... | collective-permute-start | bytes 393224 | tf_op jit(solution)/shard_map/ppermute | solution.py:313
  4.5 7.1 %collective-permute-start.1 = (f32[16,8,256]{2,1,0:T(8,128)}, f32[16,8,256]{2,1,0:T(8,128)S(1)}, u32[]{:S(2)}, u32[]{:S(2)}) collective-permute-start(f32[16,8,256]{2,1,0:T(8,128)} %o_own.1), channel_id=1, source_target_pairs={{0,24},{4,28},{8,16},{12,20},{16,8},{20,12},{24,0},{28,4},{1,25},{... | collective-permute-start | bytes 393224 | tf_op jit(solution)/shard_map/ppermute | solution.py:309
  4.5 0.9 %copy-start = (f32[16,8,256]{2,1,0:T(8,128)S(1)}, f32[16,8,256]{2,1,0:T(8,128)}, u32[]{:S(2)}) copy-start(f32[16,8,256]{2,1,0:T(8,128)} %velocity.1) | copy-start | bytes 393220
  5.6 5.9 %collective-permute-start.2 = (f32[16,128]{1,0:T(8,128)S(1)}, f32[16,128]{1,0:T(8,128)S(1)}, u32[]{:S(2)}, u32[]{:S(2)}) collective-permute-start(f32[16,128]{1,0:T(8,128)S(1)} %get-tuple-element.23), channel_id=1, source_target_pairs={{0,9},{1,8},{2,11},{3,10},{4,12},{5,14},{6,13},{7,15},{8,1},{9,0},... | collective-permute-start | bytes 24584 | tf_op jit(solution)/shard_map/ppermute | solution.py:318
  8.6 5.5 %collective-permute-start.3 = (f32[16,128]{1,0:T(8,128)S(1)}, f32[16,128]{1,0:T(8,128)S(1)}, u32[]{:S(2)}, u32[]{:S(2)}) collective-permute-start(f32[16,128]{1,0:T(8,128)S(1)} %get-tuple-element.24), channel_id=1, source_target_pairs={{0,1},{1,0},{2,3},{3,2},{4,4},{5,6},{6,5},{7,7},{8,9},{9,8},{10,11... | collective-permute-start | bytes 24584 | tf_op jit(solution)/shard_map/ppermute | solution.py:316
  11.0 4.3 %collective-permute-start.7 = (f32[8,8,256]{2,1,0:T(8,128)S(1)}, f32[8,8,256]{2,1,0:T(8,128)S(1)}, u32[]{:S(2)}, u32[]{:S(2)}) collective-permute-start(f32[8,8,256]{2,1,0:T(8,128)S(1)} %get-tuple-element.27), channel_id=1, source_target_pairs={{0,8},{4,12},{8,0},{12,4},{1,9},{5,13},{9,1},{13,5},{2,10},{6,14},... | collective-permute-start | bytes 196616 | tf_op jit(solution)/shard_map/ppermute | solution.py:317
  14.2 1.2 %collective-permute-start.6 = (f32[2,16,128]{2,1,0:T(8,128)S(1)}, f32[2,16,128]{2,1,0:T(8,128)S(1)}, u32[]{:S(2)}, u32[]{:S(2)}) collective-permute-start(f32[2,16,128]{2,1,0:T(8,128)S(1)} %pad_maximum_fusion), channel_id=1, source_target_pairs={{0,4},{4,0},{8,12},{12,8},{1,5},{5,1},{9,13},{13,9},{2,6},{6,2},{1... | collective-permute-start | bytes 49160 | tf_op jit(solution)/shard_map/ppermute | solution.py:307
  14.2 3.0 %collective-permute-start.9 = (f32[16,8,256]{2,1,0:T(8,128)}, f32[16,8,256]{2,1,0:T(8,128)S(1)}, u32[]{:S(2)}, u32[]{:S(2)}) collective-permute-start(f32[16,8,256]{2,1,0:T(8,128)} %o_own.1), channel_id=1, source_target_pairs={{0,4},{4,0},{8,12},{12,8},{1,5},{5,1},{9,13},{13,9},{2,6},{6,2},{1... | collective-permute-start | bytes 393224 | tf_op jit(solution)/shard_map/ppermute | solution.py:307
  14.7 2.5 %collective-permute-start.10 = (f32[16,8,256]{2,1,0:T(8,128)S(1)}, f32[16,8,256]{2,1,0:T(8,128)S(1)}, u32[]{:S(2)}, u32[]{:S(2)}) collective-permute-start(f32[16,8,256]{2,1,0:T(8,128)S(1)} %collective-permute-done.4.u_own), channel_id=1, source_target_pairs={{0,4},{4,0},{8,12},{12,8},{1,5},{5,1},{9,13},{13,9},{2,6},{6,2},{1... | collective-permute-start | bytes 393224 | tf_op jit(solution)/shard_map/ppermute | solution.py:307
  14.7 2.5 %collective-permute-start.12 = (f32[16,8,256]{2,1,0:T(8,128)S(1)}, f32[16,8,256]{2,1,0:T(8,128)S(1)}, u32[]{:S(2)}, u32[]{:S(2)}) collective-permute-start(f32[16,8,256]{2,1,0:T(8,128)S(1)} %collective-permute-done.1.u_far), channel_id=1, source_target_pairs={{0,4},{4,0},{8,12},{12,8},{1,5},{5,1},{9,13},{13,9},{2,6},{6,2},{1... | collective-permute-start | bytes 393224 | tf_op jit(solution)/shard_map/ppermute | solution.py:307
  15.3 1.3 %collective-permute-start.8 = (f32[8,8,256]{2,1,0:T(8,128)S(1)}, f32[8,8,256]{2,1,0:T(8,128)S(1)}, u32[]{:S(2)}, u32[]{:S(2)}) collective-permute-start(f32[8,8,256]{2,1,0:T(8,128)S(1)} %collective-permute-done.7.v_a), channel_id=1, source_target_pairs={{0,4},{4,0},{8,12},{12,8},{1,5},{5,1},{9,13},{13,9},{2,6},{6,2},{1... | collective-permute-start | bytes 196616 | tf_op jit(solution)/shard_map/ppermute | solution.py:307
  15.3 1.9 %collective-permute-start.11 = (f32[16,8,256]{2,1,0:T(8,128)S(1)}, f32[16,8,256]{2,1,0:T(8,128)S(1)}, u32[]{:S(2)}, u32[]{:S(2)}) collective-permute-start(f32[16,8,256]{2,1,0:T(8,128)S(1)} %collective-permute-done.5.o_far), channel_id=1, source_target_pairs={{0,4},{4,0},{8,12},{12,8},{1,5},{5,1},{9,13},{13,9},{2,6},{6,2},{1... | collective-permute-start | bytes 393224 | tf_op jit(solution)/shard_map/ppermute | solution.py:307
  15.8 1.4 %copy-start.1 = (f32[16,8,256]{2,1,0:T(8,128)S(1)}, f32[16,8,256]{2,1,0:T(8,128)}, u32[]{:S(2)}) copy-start(f32[16,8,256]{2,1,0:T(8,128)} %o_own.1) | copy-start | bytes 393220
  16.6 0.9 %copy-start.2 = (s32[8]{0:T(128)S(1)}, s32[8]{0:T(128)}, u32[]{:S(2)}) copy-start(s32[8]{0:T(128)} %param.5) | copy-start | bytes 100
  19.0 4.4 %collective-permute-start.13 = (f32[72,256]{1,0:T(8,128)S(1)}, f32[72,256]{1,0:T(8,128)S(1)}, u32[]{:S(2)}, u32[]{:S(2)}) collective-permute-start(f32[72,256]{1,0:T(8,128)S(1)} %shard_map.44), channel_id=1, source_target_pairs={{0,1},{1,0},{2,3},{3,2},{4,5},{5,4},{6,7},{7,6},{8,9},{9,8},{10,11... | collective-permute-start | bytes 221192 | tf_op jit(solution)/shard_map/ppermute | solution.py:335
  23.4 4.9 %collective-permute-start.14 = (f32[40,256]{1,0:T(8,128)S(1)}, f32[40,256]{1,0:T(8,128)S(1)}, u32[]{:S(2)}, u32[]{:S(2)}) collective-permute-start(f32[40,256]{1,0:T(8,128)S(1)} %slice_add_fusion), channel_id=1, source_target_pairs={{0,2},{1,3},{2,0},{3,1},{4,6},{5,7},{6,4},{7,5},{8,10},{9,11},{10,... | collective-permute-start | bytes 122888 | tf_op jit(solution)/shard_map/ppermute | solution.py:341

commit v8 on v7

--- a/solution.py
+++ b/solution.py
@@ -146,7 +146,11 @@
         for lags, at in ((lags_near, i), (lags_away, i)):
             left += [lags[at, 0], lags[at, 0], lags[at, 1]]
         left = jnp.concatenate(left, axis=1)
-        prod[i] = lax.dot_general(left, right, (((1,), (1,)), ((), ())), preferred_element_type=F32)
+        middle = rows * MAIN
+        for part in (slice(0, middle), slice(middle, left.shape[0])):
+            prod[i, part] = lax.dot_general(
+                left[part], right, (((1,), (1,)), ((), ())), preferred_element_type=F32
+            )
         sums = diagonals(prod.at[i], rows, azim, count)
         out[i * MAIN : (i + 1) * MAIN] = sums[:MAIN]
         end = sums[MAIN:]

time: 29.3 us -> 29.2 us (level)
  no operation moved by 1% of the time
where the time goes in v8:
time: 29.2 us; the launch traced here: 29.1 us
  starting transfers between devices  15.8 us (54%)
  Pallas kernels  7.31 us (25%)
  waiting for transfers between devices  4.92 us (17%)
  local copies, waits for them, and re-layouts  0.91 us (3%)
    pallas_call x3, Pallas kernels, products(): pl.pallas_call(functools.partial(product_kernel, flips), in_specs=[VMEM]...  3.65 us
    ppermute x1, starting transfers between devices, shards(): h_away = lax.ppermute(ends_away, ('az', 'ta'), in_time_across)  3.03 us
    ppermute x1, waiting for transfers between devices, shards(): h_near = lax.ppermute(ends_near, ('az', 'ta'), in_time)  2.62 us
    ppermute x1, starting transfers between devices, shards(): lax.ppermute(keep[0] + first[MAIN:], 'ta', [(i, i ^ 2) for i in range(ta_...  2.59 us
    ppermute x1, starting transfers between devices, shards(): far = lax.ppermute(pressure, 'az', across)  2.52 us
    pallas_call x6, Pallas kernels, lag_rows(): pl.pallas_call(functools.partial(lag_kernel, flips, away), in_specs=[VMEM...  2.47 us
    ppermute x1, starting transfers between devices, shards(): h_near = lax.ppermute(ends_near, ('az', 'ta'), in_time)  2.35 us
    ppermute x7, starting transfers between devices, shards(): to_sibling = lambda x: lax.ppermute(x, 'az', sibling)  1.96 us
  transfers between devices with their start and end apart: 15, of which 6 were waited for; matrix products, arithmetic and copies ran while one was open for 0% of the time, Pallas kernels for 16%

profile of v8, /device:TPU:0, one launch (start us, length us, event | category | flops | bytes accessed | tf_op | source)
XLA Modules:
  0.0 29.1 jit_solution(8733005341118864714)
XLA Ops:
  0.0 0.5 %collective-permute-start = (f32[16,8,256]{2,1,0:T(8,128)}, f32[16,8,256]{2,1,0:T(8,128)S(1)}, u32[]{:S(2)}, u32[]{:S(2)}) collective-permute-start(f32[16,8,256]{2,1,0:T(8,128)} %velocity.1), channel_id=1, source_target_pairs={{0,4},{4,0},{8,12},{12,8},{1,5},{5,1},{9,13},{13,9},{2,6},{6,2},{1... | collective-permute-start | bytes 393224 | tf_op jit(solution)/shard_map/ppermute | solution.py:311
  0.5 2.5 %collective-permute-start.5 = (f32[16,8,256]{2,1,0:T(8,128)}, f32[16,8,256]{2,1,0:T(8,128)S(1)}, u32[]{:S(2)}, u32[]{:S(2)}) collective-permute-start(f32[16,8,256]{2,1,0:T(8,128)} %o_own.1), channel_id=1, source_target_pairs={{0,8},{4,12},{8,0},{12,4},{1,9},{5,13},{9,1},{13,5},{2,10},{6,14},... | collective-permute-start | bytes 393224 | tf_op jit(solution)/shard_map/ppermute | solution.py:314
  3.0 1.5 %collective-permute-start.4 = (f32[16,8,256]{2,1,0:T(8,128)}, f32[16,8,256]{2,1,0:T(8,128)S(1)}, u32[]{:S(2)}, u32[]{:S(2)}) collective-permute-start(f32[16,8,256]{2,1,0:T(8,128)} %o_own.1), channel_id=1, source_target_pairs={{0,16},{16,0},{1,17},{17,1},{2,18},{18,2},{3,19},{19,3},{4,20},{20... | collective-permute-start | bytes 393224 | tf_op jit(solution)/shard_map/ppermute | solution.py:317
  4.5 0.0 collective-permute-start.1
  4.5 0.0 collective-permute-done.v_sib.v_b
  4.5 0.0 copy-start
  4.5 0.9 %copy-done = f32[16,8,256]{2,1,0:T(8,128)S(1)} copy-done((f32[16,8,256]{2,1,0:T(8,128)S(1)}, f32[16,8,256]{2,1,0:T(8,128)}, u32[]{:S(2)}) %copy-start) | copy-done | bytes 131096
  5.4 0.2 shard_map.37
  5.6 3.0 %collective-permute-start.2 = (f32[16,128]{1,0:T(8,128)S(1)}, f32[16,128]{1,0:T(8,128)S(1)}, u32[]{:S(2)}, u32[]{:S(2)}) collective-permute-start(f32[16,128]{1,0:T(8,128)S(1)} %get-tuple-element.23), channel_id=1, source_target_pairs={{0,9},{1,8},{2,11},{3,10},{4,12},{5,14},{6,13},{7,15},{8,1},{9,0},... | collective-permute-start | bytes 24584 | tf_op jit(solution)/shard_map/ppermute | solution.py:322
  8.6 2.3 %collective-permute-start.3 = (f32[16,128]{1,0:T(8,128)S(1)}, f32[16,128]{1,0:T(8,128)S(1)}, u32[]{:S(2)}, u32[]{:S(2)}) collective-permute-start(f32[16,128]{1,0:T(8,128)S(1)} %get-tuple-element.24), channel_id=1, source_target_pairs={{0,1},{1,0},{2,3},{3,2},{4,4},{5,6},{6,5},{7,7},{8,9},{9,8},{10,11... | collective-permute-start | bytes 24584 | tf_op jit(solution)/shard_map/ppermute | solution.py:320
  11.0 0.0 collective-permute-done.5.o_far
  11.0 0.2 collective-permute-start.7
  11.2 0.0 collective-permute-done.4.u_own
  11.2 0.3 %collective-permute-done.1.u_far = f32[16,8,256]{2,1,0:T(8,128)S(1)} collective-permute-done((f32[16,8,256]{2,1,0:T(8,128)}, f32[16,8,256]{2,1,0:T(8,128)S(1)}, u32[]{:S(2)}, u32[]{:S(2)}) %collective-permute-start.1) | collective-permute-done | bytes 131104 | tf_op jit(solution)/shard_map/ppermute | solution.py:313
  11.5 0.0 collective-permute-done.2.h_a
  11.5 2.6 %collective-permute-done.3.h_a = f32[16,128]{1,0:T(8,128)S(1)} collective-permute-done((f32[16,128]{1,0:T(8,128)S(1)}, f32[16,128]{1,0:T(8,128)S(1)}, u32[]{:S(2)}, u32[]{:S(2)}) %collective-permute-start.3) | collective-permute-done | bytes 8224 | tf_op jit(solution)/shard_map/ppermute | solution.py:320
  14.2 0.0 collective-permute-start.6
  14.2 0.5 %collective-permute-start.9 = (f32[16,8,256]{2,1,0:T(8,128)}, f32[16,8,256]{2,1,0:T(8,128)S(1)}, u32[]{:S(2)}, u32[]{:S(2)}) collective-permute-start(f32[16,8,256]{2,1,0:T(8,128)} %o_own.1), channel_id=1, source_target_pairs={{0,4},{4,0},{8,12},{12,8},{1,5},{5,1},{9,13},{13,9},{2,6},{6,2},{1... | collective-permute-start | bytes 393224 | tf_op jit(solution)/shard_map/ppermute | solution.py:311
  14.7 0.0 collective-permute-start.10
  14.7 0.5 %collective-permute-start.12 = (f32[16,8,256]{2,1,0:T(8,128)S(1)}, f32[16,8,256]{2,1,0:T(8,128)S(1)}, u32[]{:S(2)}, u32[]{:S(2)}) collective-permute-start(f32[16,8,256]{2,1,0:T(8,128)S(1)} %collective-permute-done.1.u_far), channel_id=1, source_target_pairs={{0,4},{4,0},{8,12},{12,8},{1,5},{5,1},{9,13},{13,9},{2,6},{6,2},{1... | collective-permute-start | bytes 393224 | tf_op jit(solution)/shard_map/ppermute | solution.py:311
  15.2 0.1 collective-permute-done.7.v_a
  15.3 0.0 collective-permute-start.8
  15.3 0.0 collective-permute-done.6
  15.3 0.5 %collective-permute-start.11 = (f32[16,8,256]{2,1,0:T(8,128)S(1)}, f32[16,8,256]{2,1,0:T(8,128)S(1)}, u32[]{:S(2)}, u32[]{:S(2)}) collective-permute-start(f32[16,8,256]{2,1,0:T(8,128)S(1)} %collective-permute-done.5.o_far), channel_id=1, source_target_pairs={{0,4},{4,0},{8,12},{12,8},{1,5},{5,1},{9,13},{13,9},{2,6},{6,2},{1... | collective-permute-start | bytes 393224 | tf_op jit(solution)/shard_map/ppermute | solution.py:311
  15.8 0.0 copy-start.1
  15.8 0.6 %shard_map.42.lags_near = bf16[2,2,528,256]{3,2,1,0:T(8,128)(2,1)S(1)} custom-call(f32[16,8,256]{2,1,0:T(8,128)S(1)} %get-tuple-element.20.v_a, f32[16,8,256]{2,1,0:T(8,128)S(1)} %collective-permute-done.v_sib.v_b, f32[16,128]{1,0:T(8,128)S(1)} %collective-permute-done.3.h_a, f32[16,128]{1,0:T(8,128)S(1)} %get-tuple-element.36.h_b), custom_call_target="tpu_custom_call" | custom-call | flops 10000000 | bytes 3145728 | tf_op jit(solution)/shard_map/pallas_call | solution.py:239
  16.4 0.1 collective-permute-done.8.v_b
  16.6 0.0 copy-start.2
  16.6 0.6 %shard_map.43.lags_away = bf16[2,2,528,256]{3,2,1,0:T(8,128)(2,1)S(1)} custom-call(f32[8,8,256]{2,1,0:T(8,128)S(1)} %collective-permute-done.7.v_a, f32[8,8,256]{2,1,0:T(8,128)S(1)} %collective-permute-done.8.v_b, f32[16,128]{1,0:T(8,128)S(1)} %collective-permute-done.2.h_a, f32[16,128]{1,0:T(8,128)S(1)} %get-tuple-element.35.h_b), custom_call_target="tpu_custom_call" | custom-call | flops 10000000 | bytes 3145728 | tf_op jit(solution)/shard_map/pallas_call | solution.py:239
  17.2 0.0 collective-permute-done.9.o_sib
  17.2 0.0 collective-permute-done.10.u_sib
  17.2 0.0 collective-permute-done.12.u_far_sib
  17.2 0.0 collective-permute-done.11.o_far_sib
  17.2 0.0 copy-done.1
  17.2 0.2 shard_map.40
  17.5 0.0 copy-done.2
  17.5 1.5 %shard_map.44 = f32[72,256]{1,0:T(8,128)S(1)} custom-call(s32[1,8]{1,0:T(1,128)S(1)} %bitcast.9, bf16[2,2,528,256]{3,2,1,0:T(8,128)(2,1)S(1)} %shard_map.42.lags_near, bf16[2,2,528,256]{3,2,1,0:T(8,128)(2,1)S(1)} %shard_map.43.lags_away, bf16[24,2,16,256]{3,2,1,0:T(8,128)(2,1)S(1)} %get-tuple-element.33.high_p, ...), custom_call_target="tpu_custom_call" | custom-call | flops 830472192 | bytes 4194304 | tf_op jit(solution)/shard_map/pallas_call | solution.py:265
  19.0 1.6 %collective-permute-start.13 = (f32[72,256]{1,0:T(8,128)S(1)}, f32[72,256]{1,0:T(8,128)S(1)}, u32[]{:S(2)}, u32[]{:S(2)}) collective-permute-start(f32[72,256]{1,0:T(8,128)S(1)} %shard_map.44), channel_id=1, source_target_pairs={{0,1},{1,0},{2,3},{3,2},{4,5},{5,4},{6,7},{7,6},{8,9},{9,8},{10,11... | collective-permute-start | bytes 221192 | tf_op jit(solution)/shard_map/ppermute | solution.py:339
  20.6 0.3 %shard_map.45.lags_near = bf16[1,2,528,256]{3,2,1,0:T(8,128)(2,1)S(1)} custom-call(f32[16,8,256]{2,1,0:T(8,128)S(1)} %get-tuple-element.20.v_a, f32[16,8,256]{2,1,0:T(8,128)S(1)} %collective-permute-done.v_sib.v_b, f32[16,128]{1,0:T(8,128)S(1)} %collective-permute-done.3.h_a, f32[16,128]{1,0:T(8,128)S(1)} %get-tuple-element.36.h_b), custom_call_target="tpu_custom_call" | custom-call | flops 10000000 | bytes 3145728 | tf_op jit(solution)/shard_map/pallas_call | solution.py:239
  20.9 0.3 %shard_map.46.lags_away = bf16[1,2,528,256]{3,2,1,0:T(8,128)(2,1)S(1)} custom-call(f32[8,8,256]{2,1,0:T(8,128)S(1)} %collective-permute-done.7.v_a, f32[8,8,256]{2,1,0:T(8,128)S(1)} %collective-permute-done.8.v_b, f32[16,128]{1,0:T(8,128)S(1)} %collective-permute-done.2.h_a, f32[16,128]{1,0:T(8,128)S(1)} %get-tuple-element.35.h_b), custom_call_target="tpu_custom_call" | custom-call | flops 10000000 | bytes 3145728 | tf_op jit(solution)/shard_map/pallas_call | solution.py:239
  21.3 1.1 %shard_map.47 = f32[40,256]{1,0:T(8,128)S(1)} custom-call(s32[1,8]{1,0:T(1,128)S(1)} %bitcast.10, bf16[1,2,528,256]{3,2,1,0:T(8,128)(2,1)S(1)} %shard_map.45.lags_near, bf16[1,2,528,256]{3,2,1,0:T(8,128)(2,1)S(1)} %shard_map.46.lags_away, bf16[24,2,16,256]{3,2,1,0:T(8,128)(2,1)S(1)} %get-tuple-element.33.high_p, ...), custom_call_target="tpu_custom_call" | custom-call | flops 415236096 | bytes 4194304 | tf_op jit(solution)/shard_map/pallas_call | solution.py:265
  22.3 1.1 %collective-permute-done.13.refs_1_ = f32[72,256]{1,0:T(8,128)S(1)} collective-permute-done((f32[72,256]{1,0:T(8,128)S(1)}, f32[72,256]{1,0:T(8,128)S(1)}, u32[]{:S(2)}, u32[]{:S(2)}) %collective-permute-start.13) | collective-permute-done | bytes 73760 | tf_op jit(solution)/shard_map/ppermute | solution.py:339
  23.4 2.6 %collective-permute-start.14 = (f32[40,256]{1,0:T(8,128)S(1)}, f32[40,256]{1,0:T(8,128)S(1)}, u32[]{:S(2)}, u32[]{:S(2)}) collective-permute-start(f32[40,256]{1,0:T(8,128)S(1)} %slice_add_fusion), channel_id=1, source_target_pairs={{0,2},{1,3},{2,0},{3,1},{4,6},{5,7},{6,4},{7,5},{8,10},{9,11},{10,... | collective-permute-start | bytes 122888 | tf_op jit(solution)/shard_map/ppermute | solution.py:345
  26.0 0.3 %shard_map.38.lags_near = bf16[1,2,528,256]{3,2,1,0:T(8,128)(2,1)S(1)} custom-call(f32[16,8,256]{2,1,0:T(8,128)S(1)} %get-tuple-element.20.v_a, f32[16,8,256]{2,1,0:T(8,128)S(1)} %collective-permute-done.v_sib.v_b, f32[16,128]{1,0:T(8,128)S(1)} %collective-permute-done.3.h_a, f32[16,128]{1,0:T(8,128)S(1)} %get-tuple-element.36.h_b), custom_call_target="tpu_custom_call" | custom-call | flops 10000000 | bytes 3145728 | tf_op jit(solution)/shard_map/pallas_call | solution.py:239
  26.3 0.3 %shard_map.39.lags_away = bf16[1,2,528,256]{3,2,1,0:T(8,128)(2,1)S(1)} custom-call(f32[8,8,256]{2,1,0:T(8,128)S(1)} %collective-permute-done.7.v_a, f32[8,8,256]{2,1,0:T(8,128)S(1)} %collective-permute-done.8.v_b, f32[16,128]{1,0:T(8,128)S(1)} %collective-permute-done.2.h_a, f32[16,128]{1,0:T(8,128)S(1)} %get-tuple-element.35.h_b), custom_call_target="tpu_custom_call" | custom-call | flops 10000000 | bytes 3145728 | tf_op jit(solution)/shard_map/pallas_call | solution.py:239
  26.6 1.1 %shard_map.41.refs_0_ = f32[40,256]{1,0:T(8,128)S(1)} custom-call(s32[1,8]{1,0:T(1,128)S(1)} %bitcast.11, bf16[1,2,528,256]{3,2,1,0:T(8,128)(2,1)S(1)} %shard_map.38.lags_near, bf16[1,2,528,256]{3,2,1,0:T(8,128)(2,1)S(1)} %shard_map.39.lags_away, bf16[24,2,16,256]{3,2,1,0:T(8,128)(2,1)S(1)} %get-tuple-element.33.high_p, ...), custom_call_target="tpu_custom_call" | custom-call | flops 415236096 | bytes 4194304 | tf_op jit(solution)/shard_map/pallas_call | solution.py:265
  27.7 0.6 %collective-permute-done.14.refs_2_ = f32[40,256]{1,0:T(8,128)S(1)} collective-permute-done((f32[40,256]{1,0:T(8,128)S(1)}, f32[40,256]{1,0:T(8,128)S(1)}, u32[]{:S(2)}, u32[]{:S(2)}) %collective-permute-start.14) | collective-permute-done | bytes 40992 | tf_op jit(solution)/shard_map/ppermute | solution.py:345
  28.3 0.8 %shard_map.48 = f32[1,8,1056]{2,1,0:T(8,128)} custom-call(f32[40,256]{1,0:T(8,128)S(1)} %shard_map.41.refs_0_, f32[72,256]{1,0:T(8,128)S(1)} %collective-permute-done.13.refs_1_, f32[40,256]{1,0:T(8,128)S(1)} %collective-permute-done.14.refs_2_), custom_call_target="tpu_custom_call" | custom-call | flops 1000000 | bytes 262144 | tf_op jit(solution)/shard_map/pallas_call | solution.py:280
  (3 shorter events, 0.0 us)
Async XLA Ops:
  0.0 4.5 %collective-permute-start = (f32[16,8,256]{2,1,0:T(8,128)}, f32[16,8,256]{2,1,0:T(8,128)S(1)}, u32[]{:S(2)}, u32[]{:S(2)}) collective-permute-start(f32[16,8,256]{2,1,0:T(8,128)} %velocity.1), channel_id=1, source_target_pairs={{0,4},{4,0},{8,12},{12,8},{1,5},{5,1},{9,13},{13,9},{2,6},{6,2},{1... | collective-permute-start | bytes 393224 | tf_op jit(solution)/shard_map/ppermute | solution.py:311
  0.5 10.5 %collective-permute-start.5 = (f32[16,8,256]{2,1,0:T(8,128)}, f32[16,8,256]{2,1,0:T(8,128)S(1)}, u32[]{:S(2)}, u32[]{:S(2)}) collective-permute-start(f32[16,8,256]{2,1,0:T(8,128)} %o_own.1), channel_id=1, source_target_pairs={{0,8},{4,12},{8,0},{12,4},{1,9},{5,13},{9,1},{13,5},{2,10},{6,14},... | collective-permute-start | bytes 393224 | tf_op jit(solution)/shard_map/ppermute | solution.py:314
  3.0 8.2 %collective-permute-start.4 = (f32[16,8,256]{2,1,0:T(8,128)}, f32[16,8,256]{2,1,0:T(8,128)S(1)}, u32[]{:S(2)}, u32[]{:S(2)}) collective-permute-start(f32[16,8,256]{2,1,0:T(8,128)} %o_own.1), channel_id=1, source_target_pairs={{0,16},{16,0},{1,17},{17,1},{2,18},{18,2},{3,19},{19,3},{4,20},{20... | collective-permute-start | bytes 393224 | tf_op jit(solution)/shard_map/ppermute | solution.py:317
  4.5 7.1 %collective-permute-start.1 = (f32[16,8,256]{2,1,0:T(8,128)}, f32[16,8,256]{2,1,0:T(8,128)S(1)}, u32[]{:S(2)}, u32[]{:S(2)}) collective-permute-start(f32[16,8,256]{2,1,0:T(8,128)} %o_own.1), channel_id=1, source_target_pairs={{0,24},{4,28},{8,16},{12,20},{16,8},{20,12},{24,0},{28,4},{1,25},{... | collective-permute-start | bytes 393224 | tf_op jit(solution)/shard_map/ppermute | solution.py:313
  4.5 0.9 %copy-start = (f32[16,8,256]{2,1,0:T(8,128)S(1)}, f32[16,8,256]{2,1,0:T(8,128)}, u32[]{:S(2)}) copy-start(f32[16,8,256]{2,1,0:T(8,128)} %velocity.1) | copy-start | bytes 393220
  5.6 5.9 %collective-permute-start.2 = (f32[16,128]{1,0:T(8,128)S(1)}, f32[16,128]{1,0:T(8,128)S(1)}, u32[]{:S(2)}, u32[]{:S(2)}) collective-permute-start(f32[16,128]{1,0:T(8,128)S(1)} %get-tuple-element.23), channel_id=1, source_target_pairs={{0,9},{1,8},{2,11},{3,10},{4,12},{5,14},{6,13},{7,15},{8,1},{9,0},... | collective-permute-start | bytes 24584 | tf_op jit(solution)/shard_map/ppermute | solution.py:322
  8.6 5.5 %collective-permute-start.3 = (f32[16,128]{1,0:T(8,128)S(1)}, f32[16,128]{1,0:T(8,128)S(1)}, u32[]{:S(2)}, u32[]{:S(2)}) collective-permute-start(f32[16,128]{1,0:T(8,128)S(1)} %get-tuple-element.24), channel_id=1, source_target_pairs={{0,1},{1,0},{2,3},{3,2},{4,4},{5,6},{6,5},{7,7},{8,9},{9,8},{10,11... | collective-permute-start | bytes 24584 | tf_op jit(solution)/shard_map/ppermute | solution.py:320
  11.0 4.3 %collective-permute-start.7 = (f32[8,8,256]{2,1,0:T(8,128)S(1)}, f32[8,8,256]{2,1,0:T(8,128)S(1)}, u32[]{:S(2)}, u32[]{:S(2)}) collective-permute-start(f32[8,8,256]{2,1,0:T(8,128)S(1)} %get-tuple-element.27), channel_id=1, source_target_pairs={{0,8},{4,12},{8,0},{12,4},{1,9},{5,13},{9,1},{13,5},{2,10},{6,14},... | collective-permute-start | bytes 196616 | tf_op jit(solution)/shard_map/ppermute | solution.py:321
  14.2 1.2 %collective-permute-start.6 = (f32[2,16,128]{2,1,0:T(8,128)S(1)}, f32[2,16,128]{2,1,0:T(8,128)S(1)}, u32[]{:S(2)}, u32[]{:S(2)}) collective-permute-start(f32[2,16,128]{2,1,0:T(8,128)S(1)} %pad_maximum_fusion), channel_id=1, source_target_pairs={{0,4},{4,0},{8,12},{12,8},{1,5},{5,1},{9,13},{13,9},{2,6},{6,2},{1... | collective-permute-start | bytes 49160 | tf_op jit(solution)/shard_map/ppermute | solution.py:311
  14.2 3.0 %collective-permute-start.9 = (f32[16,8,256]{2,1,0:T(8,128)}, f32[16,8,256]{2,1,0:T(8,128)S(1)}, u32[]{:S(2)}, u32[]{:S(2)}) collective-permute-start(f32[16,8,256]{2,1,0:T(8,128)} %o_own.1), channel_id=1, source_target_pairs={{0,4},{4,0},{8,12},{12,8},{1,5},{5,1},{9,13},{13,9},{2,6},{6,2},{1... | collective-permute-start | bytes 393224 | tf_op jit(solution)/shard_map/ppermute | solution.py:311
  14.7 2.5 %collective-permute-start.10 = (f32[16,8,256]{2,1,0:T(8,128)S(1)}, f32[16,8,256]{2,1,0:T(8,128)S(1)}, u32[]{:S(2)}, u32[]{:S(2)}) collective-permute-start(f32[16,8,256]{2,1,0:T(8,128)S(1)} %collective-permute-done.4.u_own), channel_id=1, source_target_pairs={{0,4},{4,0},{8,12},{12,8},{1,5},{5,1},{9,13},{13,9},{2,6},{6,2},{1... | collective-permute-start | bytes 393224 | tf_op jit(solution)/shard_map/ppermute | solution.py:311
  14.7 2.5 %collective-permute-start.12 = (f32[16,8,256]{2,1,0:T(8,128)S(1)}, f32[16,8,256]{2,1,0:T(8,128)S(1)}, u32[]{:S(2)}, u32[]{:S(2)}) collective-permute-start(f32[16,8,256]{2,1,0:T(8,128)S(1)} %collective-permute-done.1.u_far), channel_id=1, source_target_pairs={{0,4},{4,0},{8,12},{12,8},{1,5},{5,1},{9,13},{13,9},{2,6},{6,2},{1... | collective-permute-start | bytes 393224 | tf_op jit(solution)/shard_map/ppermute | solution.py:311
  15.3 1.3 %collective-permute-start.8 = (f32[8,8,256]{2,1,0:T(8,128)S(1)}, f32[8,8,256]{2,1,0:T(8,128)S(1)}, u32[]{:S(2)}, u32[]{:S(2)}) collective-permute-start(f32[8,8,256]{2,1,0:T(8,128)S(1)} %collective-permute-done.7.v_a), channel_id=1, source_target_pairs={{0,4},{4,0},{8,12},{12,8},{1,5},{5,1},{9,13},{13,9},{2,6},{6,2},{1... | collective-permute-start | bytes 196616 | tf_op jit(solution)/shard_map/ppermute | solution.py:311
  15.3 1.9 %collective-permute-start.11 = (f32[16,8,256]{2,1,0:T(8,128)S(1)}, f32[16,8,256]{2,1,0:T(8,128)S(1)}, u32[]{:S(2)}, u32[]{:S(2)}) collective-permute-start(f32[16,8,256]{2,1,0:T(8,128)S(1)} %collective-permute-done.5.o_far), channel_id=1, source_target_pairs={{0,4},{4,0},{8,12},{12,8},{1,5},{5,1},{9,13},{13,9},{2,6},{6,2},{1... | collective-permute-start | bytes 393224 | tf_op jit(solution)/shard_map/ppermute | solution.py:311
  15.8 1.4 %copy-start.1 = (f32[16,8,256]{2,1,0:T(8,128)S(1)}, f32[16,8,256]{2,1,0:T(8,128)}, u32[]{:S(2)}) copy-start(f32[16,8,256]{2,1,0:T(8,128)} %o_own.1) | copy-start | bytes 393220
  16.6 0.9 %copy-start.2 = (s32[8]{0:T(128)S(1)}, s32[8]{0:T(128)}, u32[]{:S(2)}) copy-start(s32[8]{0:T(128)} %param.5) | copy-start | bytes 100
  19.0 4.4 %collective-permute-start.13 = (f32[72,256]{1,0:T(8,128)S(1)}, f32[72,256]{1,0:T(8,128)S(1)}, u32[]{:S(2)}, u32[]{:S(2)}) collective-permute-start(f32[72,256]{1,0:T(8,128)S(1)} %shard_map.44), channel_id=1, source_target_pairs={{0,1},{1,0},{2,3},{3,2},{4,5},{5,4},{6,7},{7,6},{8,9},{9,8},{10,11... | collective-permute-start | bytes 221192 | tf_op jit(solution)/shard_map/ppermute | solution.py:339
  23.4 4.9 %collective-permute-start.14 = (f32[40,256]{1,0:T(8,128)S(1)}, f32[40,256]{1,0:T(8,128)S(1)}, u32[]{:S(2)}, u32[]{:S(2)}) collective-permute-start(f32[40,256]{1,0:T(8,128)S(1)} %slice_add_fusion), channel_id=1, source_target_pairs={{0,2},{1,3},{2,0},{3,1},{4,6},{5,7},{6,4},{7,5},{8,10},{9,11},{10,... | collective-permute-start | bytes 122888 | tf_op jit(solution)/shard_map/ppermute | solution.py:345
